TPU v7x, 256 devices: a whole 4x4x8 slice. The times are simulated.
256 devices in a mesh: ens: 4 (over y_hi, core), grid: 64 (over z, x, y_lo).
Axes of the slice: x: 4, y: 4 (y_hi: 2, y_lo: 2; y = y_hi * 2 + y_lo), z: 8, core: 2. Of those that a mesh axis runs over, the one named last changes fastest.
Arguments:
- grid_embed: bfloat16 [8, 8192, 1024], P('ens', 'grid'), may hold values from -6 to 6
- latent: bfloat16 [8, 2048, 1024], P('ens', 'grid'), may hold values from -6 to 6
- key_weight: bfloat16 [1024, 1024], replicated, may hold values from -0.1875 to 0.1875
- value_weight: bfloat16 [1024, 1024], replicated, may hold values from -0.1875 to 0.1875
- out_weight: bfloat16 [100, 1024], replicated, may hold values from -0.1875 to 0.1875
- target: float32 [100, 8192], P(None, 'grid'), may hold values from -6 to 6
- edges: int32 [2, 32768], P(None, 'grid'), may hold values from -1 to 8191, as said below
Outputs:
- grad_key_weight: float32 [1024, 1024], P('grid')
- grad_value_weight: float32 [1024, 1024], P('grid')
- grad_out_weight_t: float32 [1024, 100], P('grid')
- grad_latent: float32 [8, 2048, 1024], P('ens', 'grid')
Inputs may be any that keep to these rules, and one draw needn't show every extreme that they name: The 512 slots of band s start at position s * 512: its live edges come first, then padding. A live edge's destination is a grid point of band s (s * 128 to (s + 1) * 128 - 1) and its source a latent node of bands s and s + 1 (s * 32 to (s + 2) * 32 - 1; only band s's own on the last band). Padding has destination -1 and source s * 32. Every grid point is the destination of 1 to 4 edges; in some bands every slot is live.
All inputs are finite; a program needn't handle non-finite values.
Results may differ from a plain program's by a relative error of at most 0.017.
Values may be sent and summed in bfloat16 or wider, within the bound.
No kernel may reach another device: no remote copies, remote signals or barrier semaphores. Data moves between devices by JAX's collectives and lax.ppermute only.
A program may use at most 128 MiB of HBM per device.

v0:
```python
import jax
import jax.numpy as jnp
from jax import lax
from jax.sharding import PartitionSpec as P

HEADS = 16
HEAD_DIM = 64


CAP = 5.0
DELTA_SQ = 0.0625
EPS = 1e-06


def from_behind(value, axis, by):
    devices = lax.axis_size(axis)
    pairs = [(i, i + by) for i in range(devices) if 0 <= i + by < devices]
    return lax.ppermute(value, axis, pairs)


def shifted(value, axis, by):
    devices = lax.axis_size(axis)
    return lax.ppermute(value, axis, [(i, (i + by) % devices) for i in range(devices)])


def slope(offset):
    return offset / jnp.sqrt(offset * offset + DELTA_SQ)


def edge_rows(queries, key_rows, value_rows, targets, sources):
    valid = targets >= 0
    target_rows = jnp.where(valid, targets, 0)
    query_edge = (
        jnp.take(queries, target_rows, axis=0).astype(jnp.float32).reshape(-1, HEADS, HEAD_DIM)
    )
    key_edge = jnp.take(key_rows, sources, axis=0).astype(jnp.float32).reshape(-1, HEADS, HEAD_DIM)
    value_edge = (
        jnp.take(value_rows, sources, axis=0).astype(jnp.float32).reshape(-1, HEADS, HEAD_DIM)
    )
    return (valid, target_rows, query_edge, key_edge, value_edge)


def attend_forward(queries, key_rows, value_rows, targets, sources):
    valid, target_rows, query_edge, key_edge, value_edge = edge_rows(
        queries, key_rows, value_rows, targets, sources
    )
    grid_count = queries.shape[0]
    raw_scores = jnp.sum(query_edge * key_edge, axis=-1) * HEAD_DIM ** (-0.5)
    capped = CAP * jnp.tanh(raw_scores / CAP)
    exp_scores = jnp.where(valid[:, None], jnp.exp(capped), 0.0)
    totals = jax.ops.segment_sum(exp_scores, target_rows, num_segments=grid_count)
    weights = exp_scores / jnp.take(totals, target_rows, axis=0)
    attended = jax.ops.segment_sum(
        weights[:, :, None] * value_edge, target_rows, num_segments=grid_count
    )
    return (attended, weights, capped)


def attend_backward(
    attn_grad, attended, weights, capped, queries, key_rows, value_rows, targets, sources
):
    valid, target_rows, query_edge, key_edge, value_edge = edge_rows(
        queries, key_rows, value_rows, targets, sources
    )
    row_count = key_rows.shape[0]
    features = queries.shape[1]
    edge_grad = jnp.take(attn_grad, target_rows, axis=0)
    weight_grad = jnp.sum(edge_grad * value_edge, axis=-1)
    inner = jnp.sum(attn_grad * attended, axis=-1)
    capped_grad = weights * (weight_grad - jnp.take(inner, target_rows, axis=0))
    raw_grad = capped_grad * (1.0 - capped / CAP * (capped / CAP)) * HEAD_DIM ** (-0.5)
    key_edge_grad = (raw_grad[:, :, None] * query_edge).reshape(-1, features)
    value_edge_grad = (weights[:, :, None] * edge_grad).reshape(-1, features)
    key_part = jax.ops.segment_sum(key_edge_grad, sources, num_segments=row_count)
    value_part = jax.ops.segment_sum(value_edge_grad, sources, num_segments=row_count)
    return (key_part, value_part)


def project_rows(rows, weight):
    return jnp.einsum("mld,de->mle", rows, weight, preferred_element_type=jnp.float32).astype(
        jnp.bfloat16
    )


def on_device(grid_embed, latent, key_weight, value_weight, out_weight, target, edges):
    member_count = grid_embed.shape[0]
    grid_count = grid_embed.shape[1]
    latent_count = latent.shape[1]
    features = grid_embed.shape[2]
    total_members = member_count * lax.axis_size("ens")
    band = lax.axis_index("grid")
    targets = jnp.where(edges[0] >= 0, edges[0] - band * grid_count, -1)
    sources = edges[1] - band * latent_count
    key_rows = project_rows(latent, key_weight)
    value_rows = project_rows(latent, value_weight)
    upper_keys, upper_values = from_behind((key_rows, value_rows), "grid", -1)
    window_keys = jnp.concatenate([key_rows, upper_keys], axis=1)
    window_values = jnp.concatenate([value_rows, upper_values], axis=1)
    saved = []
    predictions = []
    for member in range(member_count):
        attended, weights, capped = attend_forward(
            grid_embed[member], window_keys[member], window_values[member], targets, sources
        )
        mixed = grid_embed[member].astype(jnp.float32) + attended.reshape(grid_count, features)
        inverse = lax.rsqrt(jnp.mean(mixed * mixed, axis=-1, keepdims=True) + EPS)
        normed = mixed * inverse
        normed_low = normed.astype(jnp.bfloat16)
        predictions.append(
            lax.dot_general(
                out_weight, normed_low, (((1,), (1,)), ((), ())), preferred_element_type=jnp.float32
            )
        )
        saved.append((attended, weights, capped, normed, normed_low, inverse))
    preds = jnp.stack(predictions)
    base_term = slope(preds - target[None]) / total_members
    pair_term = jnp.sum(slope(preds[:, None] - preds[None, :]), axis=1)
    for shift_by in range(1, lax.axis_size("ens")):
        others = shifted(preds.astype(jnp.bfloat16), "ens", shift_by).astype(preds.dtype)
        pair_term = pair_term + jnp.sum(slope(preds[:, None] - others[None, :]), axis=1)
    pred_grad = (base_term - pair_term / (total_members * (total_members - 1))).astype(jnp.bfloat16)
    out_grad = jnp.zeros((features, out_weight.shape[0]), jnp.float32)
    key_parts = []
    value_parts = []
    for member in range(member_count):
        attended, weights, capped, normed, normed_low, inverse = saved[member]
        out_grad = out_grad + lax.dot_general(
            normed_low,
            pred_grad[member],
            (((0,), (1,)), ((), ())),
            preferred_element_type=jnp.float32,
        )
        normed_grad = lax.dot_general(
            pred_grad[member],
            out_weight,
            (((0,), (0,)), ((), ())),
            preferred_element_type=jnp.float32,
        )
        mixed_grad = inverse * (
            normed_grad - normed * jnp.mean(normed_grad * normed, axis=-1, keepdims=True)
        )
        key_part, value_part = attend_backward(
            mixed_grad.reshape(grid_count, HEADS, HEAD_DIM),
            attended,
            weights,
            capped,
            grid_embed[member],
            window_keys[member],
            window_values[member],
            targets,
            sources,
        )
        key_parts.append(key_part)
        value_parts.append(value_part)
    key_part = jnp.stack(key_parts)
    value_part = jnp.stack(value_parts)
    from_lower = (
        from_behind(key_part[:, latent_count:].astype(jnp.bfloat16), "grid", 1).astype(jnp.float32),
        from_behind(value_part[:, latent_count:].astype(jnp.bfloat16), "grid", 1).astype(
            jnp.float32
        ),
    )
    key_grad = (key_part[:, :latent_count] + from_lower[0]).astype(jnp.bfloat16)
    value_grad = (value_part[:, :latent_count] + from_lower[1]).astype(jnp.bfloat16)
    key_weight_grad = jnp.einsum(
        "mld,mle->de", latent, key_grad, preferred_element_type=jnp.float32
    )
    value_weight_grad = jnp.einsum(
        "mld,mle->de", latent, value_grad, preferred_element_type=jnp.float32
    )
    grad_latent = jnp.einsum(
        "mle,de->mld", key_grad, key_weight, preferred_element_type=jnp.float32
    ) + jnp.einsum("mle,de->mld", value_grad, value_weight, preferred_element_type=jnp.float32)
    shares = (
        lax.psum_scatter(key_weight_grad, "grid", scatter_dimension=0, tiled=True),
        lax.psum_scatter(value_weight_grad, "grid", scatter_dimension=0, tiled=True),
        lax.psum_scatter(out_grad, "grid", scatter_dimension=0, tiled=True),
    )
    results = (
        lax.psum(shares[0].astype(jnp.bfloat16), "ens").astype(jnp.float32),
        lax.psum(shares[1].astype(jnp.bfloat16), "ens").astype(jnp.float32),
        lax.psum(shares[2].astype(jnp.bfloat16), "ens").astype(jnp.float32),
    )
    return (results[0], results[1], results[2], grad_latent)


def solution(mesh):
    in_specs = (
        P("ens", "grid", None),
        P("ens", "grid", None),
        P(),
        P(),
        P(),
        P(None, "grid"),
        P(None, "grid"),
    )
    out_specs = (P("grid", None), P("grid", None), P("grid", None), P("ens", "grid", None))
    return jax.shard_map(
        on_device, mesh=mesh, in_specs=in_specs, out_specs=out_specs, check_vma=False
    )
```

profile of v0, /device:TPU:1, one launch (start us, length us, event | category | flops | bytes accessed | tf_op | source)
XLA Modules:
  0.0 1244.3 jit_solution(2654549624220839262)
XLA Ops:
  39.9 4.6 convert_multiply_fusion.1
  54.0 4.8 copy.233
  61.8 4.9 copy.242
  72.6 3.9 scatter_custom_fusion.2
  83.5 4.2 broadcast_multiply_fusion.1
  87.8 41.2 %scatter_fusion = f32[128,16,64]{2,1,0:T(8,128)S(1)} fusion(f32[128,16,64]{2,1,0:T(8,128)S(1)} %broadcast.186.clone.1, s32[512]{0:T(512)S(1)} %bitcast.147, f32[512,16,64]{2,1,0:T(8,128)} %broadcast_multiply_fusion.1), kind=kCustom, calls=%fused_computation.13 | custom fusion | flops 524288 | bytes 6293504 | tf_op jit(solution)/shard_map/scatter-add | solution.py:53
  134.3 4.2 broadcast_multiply_fusion
  138.6 41.2 %scatter_fusion.1 = f32[128,16,64]{2,1,0:T(8,128)S(1)} fusion(f32[128,16,64]{2,1,0:T(8,128)S(1)} %broadcast.186.clone, s32[512]{0:T(512)S(1)} %bitcast.148, f32[512,16,64]{2,1,0:T(8,128)} %broadcast_multiply_fusion), kind=kCustom, calls=%fused_computation.15 | custom fusion | flops 524288 | bytes 6293504 | tf_op jit(solution)/shard_map/scatter-add | solution.py:53
  207.4 4.2 gather_fusion.10
  217.7 4.2 gather_fusion.8
  225.8 10.9 multiply_reduce_fusion
  246.0 6.4 scatter_custom_fusion.5
  252.4 6.7 scatter_custom_fusion.4
  260.0 4.2 collective-permute-start.5
  269.8 5.4 copy.271
  275.2 3.8 copy.267
  288.7 5.8 scatter_custom_fusion.7
  294.5 5.8 scatter_custom_fusion.6
  300.3 4.9 collective-permute-start.6
  309.6 5.4 copy.273
  315.8 174.4 %reduce-scatter.8.cloned.1.call-done = f32[16,100]{1,0:T(8,128)} async-done(((f32[1024,100]{1,0:T(8,128)}), f32[16,100]{1,0:T(8,128)}) %reduce-scatter.8.cloned.1.call-update) | async-done | bytes 6416 | tf_op jit(solution)/shard_map/reduce_scatter | solution.py:177
  491.5 323.5 %reduce-scatter.10.cloned.1.call-done = f32[16,1024]{1,0:T(8,128)} async-done(((f32[1024,1024]{1,0:T(8,128)}), f32[16,1024]{1,0:T(8,128)}) %reduce-scatter.10.cloned.1.call-update) | async-done | bytes 65552
  816.7 319.1 %reduce-scatter.12.cloned.1.call-done = f32[16,1024]{1,0:T(8,128)} async-done(((f32[1024,1024]{1,0:T(8,128)}), f32[16,1024]{1,0:T(8,128)}) %reduce-scatter.12.cloned.1.call-update) | async-done | bytes 65552
  1140.6 92.1 %all-reduce.3.cloned.1.call-done = (bf16[16,1024]{0,1:T(8,128)(2,1)}, bf16[16,1024]{0,1:T(8,128)(2,1)}, bf16[16,100]{1,0:T(8,128)(2,1)}) async-done(((bf16[16,1024]{0,1:T(8,128)(2,1)}, bf16[16,1024]{0,1:T(8,128)(2,1)}, bf16[16,100]{1,0:T(8,128)(2,1)}), (bf16[16,1024]{0,1:T(8,128)(2,1)}, bf16[16,1024]{0,1:T(8,128)(2,1)}, bf16[16,100]{1,0:T(8,128)(2,1)})) %all-reduce.3.cloned.1.call-update) | async-done | bytes 68752 | tf_op jit(solution)/shard_map/psum | solution.py:180
  (189 shorter events, 143.7 us)
Async XLA Ops:
  7.2 7.5 copy-start.32
  7.2 483.0 %reduce-scatter.8.cloned.1.call-start = ((), (), s32[]{:S(2)}) async-start(), calls=%async_computation.3 | async-start | bytes 532480 | tf_op jit(solution)/shard_map/reduce_scatter | solution.py:177
  8.8 7.6 copy-start.8
  10.9 19.6 %collective-permute-start.1 = (bf16[2,32,1024]{2,1,0:T(8,128)(2,1)}, bf16[2,32,1024]{2,1,0:T(8,128)(2,1)}, u32[]{:S(2)}, u32[]{:S(2)}) collective-permute-start(bf16[2,32,1024]{2,1,0:T(8,128)(2,1)} %fusion.16), channel_id=1, source_target_pairs={{1,0},{2,1},{3,2},{4,3},{5,4},{6,5},{7,6},{8,7},{9,8},{10,9},{11,1... | collective-permute-start | bytes 393224 | tf_op jit(solution)/shard_map/ppermute | solution.py:18
  13.4 13.1 %collective-permute-start = (bf16[2,32,1024]{2,1,0:T(8,128)(2,1)}, bf16[2,32,1024]{2,1,0:T(8,128)(2,1)}, u32[]{:S(2)}, u32[]{:S(2)}) collective-permute-start(bf16[2,32,1024]{2,1,0:T(8,128)(2,1)} %fusion.13), channel_id=1, source_target_pairs={{1,0},{2,1},{3,2},{4,3},{5,4},{6,5},{7,6},{8,7},{9,8},{10,9},{11,1... | collective-permute-start | bytes 393224 | tf_op jit(solution)/shard_map/ppermute | solution.py:18
  26.5 13.5 %copy-start.3 = (bf16[512,1024]{1,0:T(8,128)(2,1)}, bf16[512,1024]{1,0:T(8,128)(2,1)S(1)}, u32[]{:S(2)}) copy-start(bf16[512,1024]{1,0:T(8,128)(2,1)S(1)} %gather_fusion) | copy-start | bytes 3145732
  82.6 51.7 %copy-start.12 = (f32[512,16]{1,0:T(8,128)}, f32[512,16]{1,0:T(8,128)S(1)}, u32[]{:S(2)}) copy-start(f32[512,16]{1,0:T(8,128)S(1)} %copy.240) | copy-start | bytes 98308
  132.3 52.9 %copy-start.28 = (f32[128]{0:T(128)}, f32[128]{0:T(128)S(1)}, u32[]{:S(2)}) copy-start(f32[128]{0:T(128)S(1)} %add_rsqrt_fusion.1) | copy-start | bytes 1540
  179.8 5.4 copy-start.11
  185.2 10.3 copy-start.18
  185.2 11.7 copy-start.19
  186.7 12.7 %copy-start.26 = (f32[100,128]{1,0:T(8,128)S(1)}, f32[100,128]{1,0:T(8,128)}, u32[]{:S(2)}) copy-start(f32[100,128]{1,0:T(8,128)} %param.20) | copy-start | bytes 153604
  188.2 9.6 collective-permute-start.4
  191.5 6.4 collective-permute-start.3
  192.7 5.2 collective-permute-start.2
  223.2 591.8 %reduce-scatter.10.cloned.1.call-start = ((), (), s32[]{:S(2)}) async-start(), calls=%async_computation.4 | async-start | bytes 4259840
  225.8 11.2 copy-start.23
  225.8 11.2 copy-start.25
  246.0 6.4 copy-start.4
  252.4 14.6 %copy-start.17 = (bf16[2,32,1024]{2,1,0:T(8,128)(2,1)S(1)}, bf16[2,32,1024]{2,1,0:T(8,128)(2,1)}, u32[]{:S(2)}) copy-start(bf16[2,32,1024]{2,1,0:T(8,128)(2,1)} %param.16) | copy-start | bytes 393220
  260.0 6.1 collective-permute-start.5
  275.2 860.7 %reduce-scatter.12.cloned.1.call-start = ((), (), s32[]{:S(2)}) async-start(), calls=%async_computation.5 | async-start | bytes 4259840
  300.3 6.6 collective-permute-start.6
  315.0 917.7 %all-reduce.3.cloned.1.call-start = ((), (), s32[]{:S(2)}) async-start(), calls=%async_computation.6 | async-start | bytes 1056768 | tf_op jit(solution)/shard_map/psum | solution.py:180
  (21 other events, 70.7 us)
Sparse Core Ops, SparseCore 0:
  223.3 266.8 reduce-scatter.7
  492.9 322.1 reduce-scatter.9
  817.5 318.2 reduce-scatter.11
  1139.4 93.2 all-reduce.2
where the time goes:
time: 1260 us; the launch traced here: 1240 us
  waiting for transfers between devices  913 us (72%)
  other arithmetic  167 us (13%)
  local copies, waits for them, and re-layouts  113 us (9%)
  starting transfers between devices  19.4 us (2%)
  matrix products  17.3 us (1%)
  between operations  14.9 us (1%)
    unnamed x6, waiting for transfers between devices  643 us
    reduce_scatter x1, waiting for transfers between devices, on_device(): lax.psum_scatter(out_grad, 'grid', scatter_dimension=0, tiled=True)  174 us
    psum x1, waiting for transfers between devices, on_device(): lax.psum(shares[0].astype(jnp.bfloat16), 'ens').astype(jnp.float32)  92.1 us
    scatter-add x2, other arithmetic, attend_forward(): jax.ops.segment_sum(weights[:, :, None] * value_edge, target_rows, num_se...  82.4 us
  transfers between devices with their start and end apart: 11, of which 6 were waited for; matrix products, arithmetic and copies ran while one was open for 8% of the time, Pallas kernels for 0%

commit v1 on v0

v1 whole, which is shorter than its diff:
```python
import jax
import jax.numpy as jnp
from jax import lax
from jax.experimental import pallas as pl
from jax.experimental.pallas import tpu as pltpu
from jax.sharding import Mesh
from jax.sharding import PartitionSpec as P

HEAD_DIM = 64
CAP = 5.0
DELTA_SQ = 0.0625
EPS = 1e-06

MEMBERS = 8
HELD = 2
GRID_DEV = 128
LAT_DEV = 32
WINDOW = 64
D = 1024
VARS = 100
VARS_PAD = 128
GROUP = 256
GROUPS = D // GROUP
BAND = ("z", "x", "y")
SPLIT = ("ens", "x")
REST = ("z", "y")
PEERS = 16
COLS = 2 * D // PEERS

F32 = jnp.float32
LOW = jnp.bfloat16


def slope(offset):
    return offset * lax.rsqrt(offset * offset + DELTA_SQ)


def dot(a, b, a_dim, b_dim):
    return lax.dot_general(a, b, (((a_dim,), (b_dim,)), ((), ())), preferred_element_type=F32)


def same_head():
    rows = lax.broadcasted_iota(jnp.int32, (GROUP, GROUP), 0) // HEAD_DIM
    cols = lax.broadcasted_iota(jnp.int32, (GROUP, GROUP), 1) // HEAD_DIM
    return rows == cols


def by_head(rows, same):
    return jnp.where(same, jnp.concatenate([rows] * 4, axis=0), jnp.zeros((), LOW))


def from_head(blocks):
    head = lax.broadcasted_iota(jnp.int32, (WINDOW, GROUP), 1) // HEAD_DIM
    total = blocks[:WINDOW]
    for h in range(1, 4):
        total = jnp.where(head == h, blocks[h * WINDOW : (h + 1) * WINDOW], total)
    return total


def forward_kernel(
    embed, lat_own, lat_up, key_weight, value_weight, out_weight, edges,
    preds, preds_low, normed_low, inverse, exps, damps, values, keys, mixed,
):
    rows = jnp.concatenate([lat_own[0], lat_up[0], lat_own[1], lat_up[1]], axis=0)
    keys[...] = dot(rows, key_weight[...], 1, 0).astype(LOW)
    values[...] = dot(rows, value_weight[...], 1, 0).astype(LOW)
    target = edges[0:1, :]
    local = jnp.where(target >= 0, target & (GRID_DEV - 1), -1)
    source = edges[1:2, :] - (target >> 7) * LAT_DEV
    slots = edges.shape[1]
    into = (lax.broadcasted_iota(jnp.int32, (GRID_DEV, slots), 0) == local).astype(F32).astype(LOW)
    node = lax.broadcasted_iota(jnp.int32, (GROUP, slots), 0) & (WINDOW - 1)
    out_of = (node == source).astype(F32).astype(LOW)
    count = dot(into, out_of, 1, 1)
    same = same_head()
    ones = same.astype(F32).astype(LOW)
    for m in range(HELD):
        square = jnp.zeros((GRID_DEV, 1), F32)
        for j in range(GROUPS):
            cols = slice(j * GROUP, (j + 1) * GROUP)
            query = embed[m, :, cols]
            key = by_head(keys[m * WINDOW : (m + 1) * WINDOW, cols], same)
            value = by_head(values[m * WINDOW : (m + 1) * WINDOW, cols], same)
            bent = jnp.tanh(dot(query, key, 1, 1) * (HEAD_DIM**-0.5 / CAP))
            exp = (count * jnp.exp(CAP * bent)).astype(LOW)
            exps[m, :, cols] = exp
            damps[m, :, cols] = ((1.0 - bent * bent) * HEAD_DIM**-0.5).astype(LOW)
            attended = dot(exp, value, 1, 0) / dot(exp, ones, 1, 0)
            sums = query.astype(F32) + attended
            mixed[:, cols] = sums
            square = square + jnp.sum(sums * sums, axis=1, keepdims=True)
        inv = lax.rsqrt(square * (1.0 / D) + EPS)
        low = (mixed[...] * inv).astype(LOW)
        normed_low[m] = low
        inverse[m] = jnp.broadcast_to(inv, (GRID_DEV, 128))
        pred = dot(out_weight[...], low, 1, 1)
        preds[m] = pred
        preds_low[m] = pred.astype(LOW)


def backward_kernel(
    embed, out_weight, target, preds, every, normed_low, inverse, exps, damps, values,
    own, upper, out_grad, grad,
):
    same = same_head()
    ones = same.astype(F32).astype(LOW)
    pred_grads = []
    for m in range(HELD):
        pred = preds[m]
        pair = jnp.zeros((VARS_PAD, GRID_DEV), F32)
        for e in range(MEMBERS // HELD):
            for k in range(HELD):
                pair = pair + slope(pred - every[e, k].astype(F32))
        for k in range(HELD):
            pair = pair - slope(pred - preds[k].astype(LOW).astype(F32))
            if k != m:
                pair = pair + slope(pred - preds[k])
        base = slope(pred - target[...]) * (1.0 / MEMBERS)
        pred_grads.append((base - pair * (1.0 / (MEMBERS * (MEMBERS - 1)))).astype(LOW))
    both = jnp.concatenate(pred_grads, axis=1)
    lows = jnp.concatenate([normed_low[0], normed_low[1]], axis=0)
    out_grad[...] = jnp.transpose(dot(both, lows, 1, 0)).astype(LOW)
    for m in range(HELD):
        slant = jnp.zeros((GRID_DEV, 1), F32)
        for j in range(GROUPS):
            cols = slice(j * GROUP, (j + 1) * GROUP)
            part = dot(pred_grads[m], out_weight[:, cols], 0, 0)
            grad[:, cols] = part
            slant = slant + jnp.sum(part * normed_low[m, :, cols].astype(F32), axis=1, keepdims=True)
        slant = slant * (1.0 / D)
        inv = inverse[m][:, :1]
        for j in range(GROUPS):
            cols = slice(j * GROUP, (j + 1) * GROUP)
            mixed_grad = (inv * (grad[:, cols] - normed_low[m, :, cols].astype(F32) * slant)).astype(LOW)
            value = by_head(values[m * WINDOW : (m + 1) * WINDOW, cols], same)
            exp = exps[m, :, cols]
            weight = exp.astype(F32) / dot(exp, ones, 1, 0)
            weight_grad = dot(mixed_grad, value, 1, 1)
            term = weight * weight_grad
            high = term.astype(LOW)
            rest = (term - high.astype(F32)).astype(LOW)
            inner = dot(high, ones, 1, 0) + dot(rest, ones, 1, 0)
            raw_grad = (weight * (weight_grad - inner) * damps[m, :, cols].astype(F32)).astype(LOW)
            key_part = from_head(dot(raw_grad, embed[m, :, cols], 0, 0))
            value_part = from_head(dot(weight.astype(LOW), mixed_grad, 0, 0))
            own[0, m, :, cols] = key_part[:LAT_DEV]
            own[1, m, :, cols] = value_part[:LAT_DEV]
            upper[0, m, :, cols] = key_part[LAT_DEV:].astype(LOW)
            upper[1, m, :, cols] = value_part[LAT_DEV:].astype(LOW)


def join_kernel(own, lower, send):
    for which in range(2):
        for m in range(HELD):
            total = (own[which, m] + lower[which, m].astype(F32)).astype(LOW)
            for p in range(PEERS // 2):
                send[which * (PEERS // 2) + p, m * LAT_DEV : (m + 1) * LAT_DEV, :] = total[
                    :, p * COLS : (p + 1) * COLS
                ]


def latent_kernel(joined, key_weight, value_weight, grad_latent):
    half = PEERS // 2
    key_grad = jnp.concatenate([joined[p] for p in range(half)], axis=1)
    value_grad = jnp.concatenate([joined[half + p] for p in range(half)], axis=1)
    total = dot(key_grad, key_weight[...], 1, 1) + dot(value_grad, value_weight[...], 1, 1)
    for m in range(HELD):
        grad_latent[m] = total[m * LAT_DEV : (m + 1) * LAT_DEV]


def weight_kernel(parts, nodes, out_grad, send):
    rows = jnp.concatenate([parts[p] for p in range(PEERS)], axis=0)
    product = jnp.transpose(dot(rows, nodes[...], 0, 0)).astype(LOW)
    for z in range(8):
        for x in range(4):
            for y in range(2):
                start = ((z * 4 + x) * 2 + y) * 16
                send[z * 2 + y, x * 16 : (x + 1) * 16, :COLS] = product[start : start + 16]
                send[z * 2 + y, x * 16 : (x + 1) * 16, COLS:] = out_grad[start : start + 16]


def sum_kernel(parts, send):
    total = parts[0].astype(F32)
    for p in range(1, PEERS):
        total = total + parts[p].astype(F32)
    total = total.astype(LOW)
    for e in range(4):
        for x in range(4):
            send[e * 4 + x] = total[x * 16 : (x + 1) * 16]


def finish_kernel(parts, key_weight_grad, value_weight_grad, out_weight_grad):
    half = PEERS // 2
    total = parts[0, :, COLS:].astype(F32)
    for p in range(1, PEERS):
        total = total + parts[p, :, COLS:].astype(F32)
    out_weight_grad[...] = total[:, :VARS]
    for p in range(half):
        key_weight_grad[:, p * COLS : (p + 1) * COLS] = parts[p, :, :COLS].astype(F32)
        value_weight_grad[:, p * COLS : (p + 1) * COLS] = parts[half + p, :, :COLS].astype(F32)


def call(kernel, outs, scratch=(), flops=10**8, bytes_accessed=4 * 10**6):
    def run(*operands):
        return pl.pallas_call(
            kernel,
            out_shape=[jax.ShapeDtypeStruct(shape, kind) for shape, kind in outs],
            scratch_shapes=[pltpu.VMEM(shape, kind) for shape, kind in scratch],
            compiler_params=pltpu.CompilerParams(vmem_limit_bytes=48 * 2**20),
            cost_estimate=pl.CostEstimate(
                flops=flops, bytes_accessed=bytes_accessed, transcendentals=0
            ),
            name=kernel.__name__,
        )(*operands)

    return run


def band_shift(value, by):
    return lax.ppermute(value, BAND, [(i, i + by) for i in range(64) if 0 <= i + by < 64])


def on_device(grid_embed, latent, key_weight, value_weight, out_weight, target, edges):
    out_rows = jnp.pad(out_weight, ((0, VARS_PAD - VARS), (0, 0)))
    target = jnp.pad(target, ((0, VARS_PAD - VARS), (0, 0)))
    nodes = lax.all_gather(latent.reshape(HELD * LAT_DEV, D), SPLIT, axis=0, tiled=True)
    upper_latent = band_shift(latent, -1)
    preds, preds_low, normed_low, inverse, exps, damps, values = call(
        forward_kernel,
        [
            ((HELD, VARS_PAD, GRID_DEV), F32),
            ((HELD, VARS_PAD, GRID_DEV), LOW),
            ((HELD, GRID_DEV, D), LOW),
            ((HELD, GRID_DEV, 128), F32),
            ((HELD, GRID_DEV, D), LOW),
            ((HELD, GRID_DEV, D), LOW),
            ((HELD * WINDOW, D), LOW),
        ],
        [((HELD * WINDOW, D), LOW), ((GRID_DEV, D), F32)],
    )(grid_embed, latent, upper_latent, key_weight, value_weight, out_rows, edges)
    every = lax.all_gather(preds_low, "ens", axis=0)
    own, upper, out_grad = call(
        backward_kernel,
        [
            ((2, HELD, LAT_DEV, D), F32),
            ((2, HELD, LAT_DEV, D), LOW),
            ((D, VARS_PAD), LOW),
        ],
        [((GRID_DEV, D), F32)],
    )(grid_embed, out_rows, target, preds, every, normed_low, inverse, exps, damps, values)
    lower = band_shift(upper, 1)
    (joined,) = call(join_kernel, [((PEERS, HELD * LAT_DEV, COLS), LOW)])(own, lower)
    (grad_latent,) = call(latent_kernel, [((HELD, LAT_DEV, D), F32)])(
        joined, key_weight, value_weight
    )
    parts = lax.all_to_all(joined, SPLIT, 0, 0, tiled=True)
    (send,) = call(weight_kernel, [((PEERS, 64, 2 * COLS), LOW)])(parts, nodes, out_grad)
    parts = lax.all_to_all(send, REST, 0, 0, tiled=True)
    (send,) = call(sum_kernel, [((PEERS, 16, 2 * COLS), LOW)])(parts)
    parts = lax.all_to_all(send, SPLIT, 0, 0, tiled=True)
    results = call(finish_kernel, [((16, D), F32), ((16, D), F32), ((16, VARS), F32)])(parts)
    return (results[0], results[1], results[2], grad_latent)


def solution(mesh):
    wide = Mesh(mesh.devices.reshape(4, 8, 4, 2), ("ens", "z", "x", "y"))
    in_specs = (
        P("ens", BAND, None),
        P("ens", BAND, None),
        P(),
        P(),
        P(),
        P(None, BAND),
        P(None, BAND),
    )
    out_specs = (P(BAND, None), P(BAND, None), P(BAND, None), P("ens", BAND, None))
    return jax.shard_map(
        on_device, mesh=wide, in_specs=in_specs, out_specs=out_specs, check_vma=False
    )
```

time: 1260 us -> 119 us (0.09); the launches traced: 1240 us -> 119 us
  waiting for transfers between devices: 913 us -> 17.4 us
  other arithmetic: 167 us -> 0 us
  local copies, waits for them, and re-layouts: 113 us -> 9.17 us
  blocking collectives: 0 us -> 53.7 us
  matrix products: 17.3 us -> 0 us
  Pallas kernels: 0 us -> 12.7 us
    unnamed x6 -> x1, waiting for transfers between devices: 643 us -> 0.68 us
    reduce_scatter x1 -> x0, waiting for transfers between devices: 174 us -> none  [on_device(): lax.psum_scatter(out_grad, 'grid', scatter_dimension=0, tiled=True)]
    scatter-add x8 -> x0, other arithmetic: 114 us -> none  [the longest x2 82.4 us: attend_forward(): jax.ops.segment_sum(weights[:, :, None] * value_edge, target_rows, num_se...]
    psum x1 -> x0, waiting for transfers between devices: 92.1 us -> none  [on_device(): lax.psum(shares[0].astype(jnp.bfloat16), 'ens').astype(jnp.float32)]
    all_to_all x0 -> x2, blocking collectives: none -> 41.8 us  [the longest x1 23.8 us: on_device(): parts = lax.all_to_all(send, REST, 0, 0, tiled=True)]
    reshape x10 -> x0, local copies, waits for them, and re-layouts: 30.4 us -> none  [the longest x4 15.6 us: edge_rows(): jnp.take(value_rows, sources, axis=0).astype(jnp.float32)]
    gather x16 -> x0, local copies, waits for them, and re-layouts: 29 us -> none  [the longest x2 8.38 us: attend_backward(): edge_grad = jnp.take(attn_grad, target_rows, axis=0)]
    mul x10 -> x0, local copies, waits for them, and re-layouts: 26.7 us -> none  [the longest x4 9.02 us: attend_backward(): key_edge_grad = (raw_grad[:, :, None] * query_edge).reshape(-1, features)]
  transfers between devices with their start and end apart: 11 -> 4, of which waited for: 6 -> 4; matrix products, arithmetic and copies ran while one was open for 8% -> 1% of each run, Pallas kernels for 0% -> 9%
where the time goes in v1:
time: 119 us
  blocking collectives  53.7 us (45%)
  waiting for transfers between devices  17.4 us (15%)
  between operations  14.1 us (12%)
  Pallas kernels  12.7 us (11%)
  starting transfers between devices  11.7 us (10%)
  local copies, waits for them, and re-layouts  9.17 us (8%)
    all_to_all x1, blocking collectives, on_device(): parts = lax.all_to_all(send, REST, 0, 0, tiled=True)  23.8 us
    all_to_all x1, blocking collectives, on_device(): parts = lax.all_to_all(joined, SPLIT, 0, 0, tiled=True)  18 us
    pallas_call x7, Pallas kernels, run(): pl.pallas_call(kernel, out_shape=[jax.ShapeDtypeStruct(shape, kind) for s...  12.7 us
    all_gather x1, blocking collectives, on_device(): every = lax.all_gather(preds_low, 'ens', axis=0)  11.9 us
    ppermute x2, waiting for transfers between devices, band_shift(): lax.ppermute(value, BAND, [(i, i + by) for i in range(64) if 0 <= i + by...  9.04 us
    all_to_all x1, starting transfers between devices, on_device(): parts = lax.all_to_all(send, SPLIT, 0, 0, tiled=True)  8.13 us
    unnamed x14, local copies, waits for them, and re-layouts  7.4 us
    all_to_all x1, waiting for transfers between devices, on_device(): parts = lax.all_to_all(send, SPLIT, 0, 0, tiled=True)  3.87 us
  transfers between devices with their start and end apart: 4, of which 4 were waited for; matrix products, arithmetic and copies ran while one was open for 1% of the time, Pallas kernels for 9%

profile of v1, /device:TPU:1, one launch (start us, length us, event | category | flops | bytes accessed | tf_op | source)
XLA Modules:
  0.0 118.9 jit_solution(2335291386960503606)
XLA Ops:
  7.2 0.7 all-gather.3.cloned.1.call-update
  7.9 1.3 %collective-permute-start = (bf16[2,32,1024]{2,1,0:T(8,128)(2,1)}, bf16[2,32,1024]{2,1,0:T(8,128)(2,1)S(1)}, u32[]{:S(2)}, u32[]{:S(2)}) collective-permute-start(bf16[2,32,1024]{2,1,0:T(8,128)(2,1)} %lat_own.1), channel_id=1, source_target_pairs={{1,0},{2,1},{3,2},{4,3},{5,4},{6,5},{7,6},{8,7},{9,8},{10,9},{11,1... | collective-permute-start | bytes 393224 | tf_op jit(solution)/shard_map/ppermute | solution.py:220
  9.2 1.0 pad.8.out_weight
  10.2 0.8 pad.9.target
  11.0 3.5 %collective-permute-done.lat_up = bf16[2,32,1024]{2,1,0:T(8,128)(2,1)S(1)} collective-permute-done((bf16[2,32,1024]{2,1,0:T(8,128)(2,1)}, bf16[2,32,1024]{2,1,0:T(8,128)(2,1)S(1)}, u32[]{:S(2)}, u32[]{:S(2)}) %collective-permute-start) | collective-permute-done | bytes 131104 | tf_op jit(solution)/shard_map/ppermute | solution.py:220
  14.5 1.6 %copy-done = bf16[1024,1024]{1,0:T(8,128)(2,1)S(1)} copy-done((bf16[1024,1024]{1,0:T(8,128)(2,1)S(1)}, bf16[1024,1024]{1,0:T(8,128)(2,1)}, u32[]{:S(2)}) %copy-start) | copy-done | bytes 2097176
  16.1 1.0 copy-done.3
  17.1 0.9 copy-done.5
  18.0 0.7 copy-done.6
  18.7 4.1 %forward_kernel.1 = (f32[2,128,128]{2,1,0:T(8,128)S(1)}, bf16[2,128,128]{2,1,0:T(8,128)(2,1)S(1)}, bf16[2,128,1024]{2,1,0:T(8,128)(2,1)S(1)}, f32[2,128,128]{2,1...) custom-call(bf16[2,128,1024]{2,1,0:T(8,128)(2,1)S(1)} %copy-done.3, ...), custom_call_target="tpu_custom_call" | custom-call | flops 100000000 | bytes 4000000 | tf_op jit(solution)/shard_map/forward_kernel/pallas_call | solution.py:205
  22.8 11.9 %all-gather = bf16[8,128,128]{2,1,0:T(8,128)(2,1)S(1)} all-gather(bf16[2,128,128]{2,1,0:T(8,128)(2,1)S(1)} %get-tuple-element.18), channel_id=2, replica_groups=mesh['ens'=4,'z'=8,'x'=4,'y'=2] {'ens'}, dimensions={0}, use_global_device_ids=true | all-gather | bytes 327680 | tf_op jit(solution)/shard_map/all_gather | solution.py:241
  34.7 4.6 %backward_kernel.1 = (f32[2,2,32,1024]{3,2,1,0:T(8,128)S(1)}, bf16[2,2,32,1024]{3,2,1,0:T(8,128)(2,1)S(1)}, bf16[1024,128]{1,0:T(8,128)(2,1)S(1)}) custom-call(bf16[2,128,1024]{2,1,0:T(8,128)(2,1)S(1)} %copy-done.3, bf16[128,1024]{1,0:T(8,128)(2,1)S(1)} %pad.8.out_weight, f32[128,128]{1,0:T(8,128)S(1)} %pad.9.target, ...), custom_call_target="tpu_custom_call" | custom-call | flops 100000000 | bytes 4000000 | tf_op jit(solution)/shard_map/backward_kernel/pallas_call | solution.py:205
  39.3 2.2 %collective-permute-start.1 = (bf16[2,2,32,1024]{3,2,1,0:T(8,128)(2,1)S(1)}, bf16[2,2,32,1024]{3,2,1,0:T(8,128)(2,1)S(1)}, u32[]{:S(2)}, u32[]{:S(2)}) collective-permute-start(bf16[2,2,32,1024]{3,2,1,0:T(8,128)(2,1)S(1)} %get-tuple-element.25), channel_id=1, source_target_pairs={{0,1},{1,2},{2,3},{3,4},{4,5},{5,6},{6,7},{7,8},{8,9},{9,10},{10,1... | collective-permute-start | bytes 786440 | tf_op jit(solution)/shard_map/ppermute | solution.py:220
  41.6 5.5 %collective-permute-done.1.lower = bf16[2,2,32,1024]{3,2,1,0:T(8,128)(2,1)S(1)} collective-permute-done((bf16[2,2,32,1024]{3,2,1,0:T(8,128)(2,1)S(1)}, bf16[2,2,32,1024]{3,2,1,0:T(8,128)(2,1)S(1)}, u32[]{:S(2)}, u32[]{:S(2)}) %collective-permute-start.1) | collective-permute-done | bytes 262176 | tf_op jit(solution)/shard_map/ppermute | solution.py:220
  47.2 18.0 %all_to_all.15.parts = bf16[16,64,128]{2,1,0:T(8,128)(2,1)S(1)} all-to-all(bf16[16,64,128]{2,1,0:T(8,128)(2,1)S(1)} %join_kernel.1.joined), channel_id=1, replica_groups=mesh['ens'=4,'z'=8,'x'=4,'y'=2] {'ens','x'}, dimensions={0} | all-to-all | bytes 524288 | tf_op jit(solution)/shard_map/all_to_all | solution.py:256
  65.2 3.8 %all-gather.3.cloned.1.call-done.nodes = bf16[1024,1024]{1,0:T(8,128)(2,1)} async-done(((bf16[64,1024]{1,0:T(8,128)(2,1)}), bf16[1024,1024]{1,0:T(8,128)(2,1)}) %all-gather.3.cloned.1.call-update) | async-done | bytes 2097168 | tf_op jit(solution)/shard_map/all_gather | solution.py:226
  69.0 1.6 %copy-done.4 = bf16[1024,1024]{1,0:T(8,128)(2,1)S(1)} copy-done((bf16[1024,1024]{1,0:T(8,128)(2,1)S(1)}, bf16[1024,1024]{1,0:T(8,128)(2,1)}, u32[]{:S(2)}) %copy-start.4) | copy-done | bytes 2097176
  71.2 23.8 %all_to_all.16.parts = bf16[16,64,256]{2,1,0:T(8,128)(2,1)S(1)} all-to-all(bf16[16,64,256]{2,1,0:T(8,128)(2,1)S(1)} %weight_kernel.1), channel_id=1, replica_groups=mesh['ens'=4,'z'=8,'x'=4,'y'=2] {'z','y'}, dimensions={0} | all-to-all | bytes 1048576 | tf_op jit(solution)/shard_map/all_to_all | solution.py:258
  94.9 0.7 sum_kernel.1
  95.7 8.1 %all-to-all-start.2 = ((bf16[16,16,256]{2,1,0:T(8,128)(2,1)}), bf16[16,16,256]{2,1,0:T(8,128)(2,1)S(1)}, u32[]{:S(2)}, u32[]{:S(2)}) async-start(bf16[16,16,256]{2,1,0:T(8,128)(2,1)} %sum_kernel.1), calls=%async_computation.2 | async-start | bytes 262144 | tf_op jit(solution)/shard_map/all_to_all | solution.py:260
  103.8 1.6 %copy-done.2 = bf16[1024,1024]{1,0:T(8,128)(2,1)S(1)} copy-done((bf16[1024,1024]{1,0:T(8,128)(2,1)S(1)}, bf16[1024,1024]{1,0:T(8,128)(2,1)}, u32[]{:S(2)}) %copy-start.2) | copy-done | bytes 2097176
  105.4 2.1 %latent_kernel.1 = f32[2,32,1024]{2,1,0:T(8,128)} custom-call(bf16[16,64,128]{2,1,0:T(8,128)(2,1)S(1)} %join_kernel.1.joined, bf16[1024,1024]{1,0:T(8,128)(2,1)S(1)} %copy-done.1, bf16[1024,1024]{1,0:T(8,128)(2,1)S(1)} %copy-done.2), custom_call_target="tpu_custom_call" | custom-call | flops 100000000 | bytes 4000000 | tf_op jit(solution)/shard_map/latent_kernel/pallas_call | solution.py:205
  107.5 3.9 %all-to-all-done.2.parts = bf16[16,16,256]{2,1,0:T(8,128)(2,1)S(1)} async-done(((bf16[16,16,256]{2,1,0:T(8,128)(2,1)}), bf16[16,16,256]{2,1,0:T(8,128)(2,1)S(1)}, u32[]{:S(2)}, u32[]{:S(2)}) %all-to-all-start.2) | async-done | bytes 131104 | tf_op jit(solution)/shard_map/all_to_all | solution.py:260
  111.4 0.7 finish_kernel.1
  (11 shorter events, 0.6 us)
Async XLA Ops:
  7.2 61.9 %all-gather.3.cloned.1.call-start = ((), (), s32[]{:S(2)}) async-start(), calls=%async_computation.3 | async-start | bytes 2228224 | tf_op jit(solution)/shard_map/all_gather | solution.py:226
  7.9 6.6 %collective-permute-start = (bf16[2,32,1024]{2,1,0:T(8,128)(2,1)}, bf16[2,32,1024]{2,1,0:T(8,128)(2,1)S(1)}, u32[]{:S(2)}, u32[]{:S(2)}) collective-permute-start(bf16[2,32,1024]{2,1,0:T(8,128)(2,1)} %lat_own.1), channel_id=1, source_target_pairs={{1,0},{2,1},{3,2},{4,3},{5,4},{6,5},{7,6},{8,7},{9,8},{10,9},{11,1... | collective-permute-start | bytes 393224 | tf_op jit(solution)/shard_map/ppermute | solution.py:220
  14.5 1.6 %copy-start = (bf16[1024,1024]{1,0:T(8,128)(2,1)S(1)}, bf16[1024,1024]{1,0:T(8,128)(2,1)}, u32[]{:S(2)}) copy-start(bf16[1024,1024]{1,0:T(8,128)(2,1)} %key_weight.3) | copy-start | bytes 6291460
  16.1 1.0 copy-start.3
  17.1 0.9 copy-start.5
  18.0 0.7 copy-start.6
  39.3 7.8 %collective-permute-start.1 = (bf16[2,2,32,1024]{3,2,1,0:T(8,128)(2,1)S(1)}, bf16[2,2,32,1024]{3,2,1,0:T(8,128)(2,1)S(1)}, u32[]{:S(2)}, u32[]{:S(2)}) collective-permute-start(bf16[2,2,32,1024]{3,2,1,0:T(8,128)(2,1)S(1)} %get-tuple-element.25), channel_id=1, source_target_pairs={{0,1},{1,2},{2,3},{3,4},{4,5},{5,6},{6,7},{7,8},{8,9},{9,10},{10,1... | collective-permute-start | bytes 786440 | tf_op jit(solution)/shard_map/ppermute | solution.py:220
  69.0 1.6 %copy-start.4 = (bf16[1024,1024]{1,0:T(8,128)(2,1)S(1)}, bf16[1024,1024]{1,0:T(8,128)(2,1)}, u32[]{:S(2)}) copy-start(bf16[1024,1024]{1,0:T(8,128)(2,1)} %all-gather.3.cloned.1.call-done.nodes) | copy-start | bytes 6291460
  70.6 33.2 %copy-start.1 = (bf16[1024,1024]{1,0:T(8,128)(2,1)S(1)}, bf16[1024,1024]{1,0:T(8,128)(2,1)}, u32[]{:S(2)}) copy-start(bf16[1024,1024]{1,0:T(8,128)(2,1)} %key_weight.3) | copy-start | bytes 6291460
  95.7 15.7 %all-to-all-start.2 = ((bf16[16,16,256]{2,1,0:T(8,128)(2,1)}), bf16[16,16,256]{2,1,0:T(8,128)(2,1)S(1)}, u32[]{:S(2)}, u32[]{:S(2)}) async-start(bf16[16,16,256]{2,1,0:T(8,128)(2,1)} %sum_kernel.1), calls=%async_computation.2 | async-start | bytes 262144 | tf_op jit(solution)/shard_map/all_to_all | solution.py:260
  103.8 1.6 %copy-start.2 = (bf16[1024,1024]{1,0:T(8,128)(2,1)S(1)}, bf16[1024,1024]{1,0:T(8,128)(2,1)}, u32[]{:S(2)}) copy-start(bf16[1024,1024]{1,0:T(8,128)(2,1)} %value_weight.3) | copy-start | bytes 6291460
Sparse Core Ops, SparseCore 0:
  10.7 58.2 all-gather.2

commit v2 on v1

--- a/solution.py
+++ b/solution.py
@@ -22,10 +22,11 @@
 GROUP = 256
 GROUPS = D // GROUP
 BAND = ("z", "x", "y")
-SPLIT = ("ens", "x")
-REST = ("z", "y")
-PEERS = 16
-COLS = 2 * D // PEERS
+ENS = 4
+PLANE = 8
+SHARE = 16
+COLS = 2 * D // ENS
+PRED_ROW = 2 * LAT_DEV * GROUPS
 
 F32 = jnp.float32
 LOW = jnp.bfloat16
@@ -57,11 +58,8 @@
     return total
 
 
-def forward_kernel(
-    embed, lat_own, lat_up, key_weight, value_weight, out_weight, edges,
-    preds, preds_low, normed_low, inverse, exps, damps, values, keys, mixed,
-):
-    rows = jnp.concatenate([lat_own[0], lat_up[0], lat_own[1], lat_up[1]], axis=0)
+def own_kernel(latent, key_weight, value_weight, edges, keys, values, count):
+    rows = jnp.concatenate([latent[0], latent[1]], axis=0)
     keys[...] = dot(rows, key_weight[...], 1, 0).astype(LOW)
     values[...] = dot(rows, value_weight[...], 1, 0).astype(LOW)
     target = edges[0:1, :]
@@ -71,13 +69,29 @@
     into = (lax.broadcasted_iota(jnp.int32, (GRID_DEV, slots), 0) == local).astype(F32).astype(LOW)
     node = lax.broadcasted_iota(jnp.int32, (GROUP, slots), 0) & (WINDOW - 1)
     out_of = (node == source).astype(F32).astype(LOW)
-    count = dot(into, out_of, 1, 1)
+    count[...] = dot(into, out_of, 1, 1)
+
+
+def forward_kernel(
+    embed, latent, lat_up, key_weight, value_weight, out_weight, own_keys, own_values, edge_count,
+    preds, share, normed_low, inverse, exps, damps, values,
+    keys, mixed,
+):
+    rows = jnp.concatenate([lat_up[0], lat_up[1]], axis=0)
+    for own_rows, weight, window in ((own_keys, key_weight, keys), (own_values, value_weight, values)):
+        upper_rows = dot(rows, weight[...], 1, 0).astype(LOW)
+        for m in range(HELD):
+            window[m * WINDOW : m * WINDOW + LAT_DEV] = own_rows[m * LAT_DEV : (m + 1) * LAT_DEV]
+            window[m * WINDOW + LAT_DEV : (m + 1) * WINDOW] = upper_rows[m * LAT_DEV : (m + 1) * LAT_DEV]
+    count = edge_count[...]
     same = same_head()
     ones = same.astype(F32).astype(LOW)
     for m in range(HELD):
         square = jnp.zeros((GRID_DEV, 1), F32)
         for j in range(GROUPS):
             cols = slice(j * GROUP, (j + 1) * GROUP)
+            start = j * HELD * LAT_DEV + m * LAT_DEV
+            share[start : start + LAT_DEV] = latent[m, :, cols]
             query = embed[m, :, cols]
             key = by_head(keys[m * WINDOW : (m + 1) * WINDOW, cols], same)
             value = by_head(values[m * WINDOW : (m + 1) * WINDOW, cols], same)
@@ -95,13 +109,16 @@
         inverse[m] = jnp.broadcast_to(inv, (GRID_DEV, 128))
         pred = dot(out_weight[...], low, 1, 1)
         preds[m] = pred
-        preds_low[m] = pred.astype(LOW)
+        share[PRED_ROW:, m * GRID_DEV : (m + 1) * GRID_DEV] = pred.astype(LOW)
 
 
 def backward_kernel(
     embed, out_weight, target, preds, every, normed_low, inverse, exps, damps, values,
-    own, upper, out_grad, grad,
+    own, upper, out_grad,
+    grad, truth,
 ):
+    truth[...] = jnp.zeros((VARS_PAD, GRID_DEV), F32)
+    truth[:VARS, :] = target[...]
     same = same_head()
     ones = same.astype(F32).astype(LOW)
     pred_grads = []
@@ -110,12 +127,12 @@
         pair = jnp.zeros((VARS_PAD, GRID_DEV), F32)
         for e in range(MEMBERS // HELD):
             for k in range(HELD):
-                pair = pair + slope(pred - every[e, k].astype(F32))
+                pair = pair + slope(pred - every[e, :, k * GRID_DEV : (k + 1) * GRID_DEV].astype(F32))
         for k in range(HELD):
             pair = pair - slope(pred - preds[k].astype(LOW).astype(F32))
             if k != m:
                 pair = pair + slope(pred - preds[k])
-        base = slope(pred - target[...]) * (1.0 / MEMBERS)
+        base = slope(pred - truth[...]) * (1.0 / MEMBERS)
         pred_grads.append((base - pair * (1.0 / (MEMBERS * (MEMBERS - 1)))).astype(LOW))
     both = jnp.concatenate(pred_grads, axis=1)
     lows = jnp.concatenate([normed_low[0], normed_low[1]], axis=0)
@@ -153,60 +170,73 @@
     for which in range(2):
         for m in range(HELD):
             total = (own[which, m] + lower[which, m].astype(F32)).astype(LOW)
-            for p in range(PEERS // 2):
-                send[which * (PEERS // 2) + p, m * LAT_DEV : (m + 1) * LAT_DEV, :] = total[
+            for p in range(2):
+                send[2 * which + p, m * LAT_DEV : (m + 1) * LAT_DEV, :] = total[
                     :, p * COLS : (p + 1) * COLS
                 ]
 
 
 def latent_kernel(joined, key_weight, value_weight, grad_latent):
-    half = PEERS // 2
-    key_grad = jnp.concatenate([joined[p] for p in range(half)], axis=1)
-    value_grad = jnp.concatenate([joined[half + p] for p in range(half)], axis=1)
+    key_grad = jnp.concatenate([joined[0], joined[1]], axis=1)
+    value_grad = jnp.concatenate([joined[2], joined[3]], axis=1)
     total = dot(key_grad, key_weight[...], 1, 1) + dot(value_grad, value_weight[...], 1, 1)
     for m in range(HELD):
         grad_latent[m] = total[m * LAT_DEV : (m + 1) * LAT_DEV]
 
 
-def weight_kernel(parts, nodes, out_grad, send):
-    rows = jnp.concatenate([parts[p] for p in range(PEERS)], axis=0)
-    product = jnp.transpose(dot(rows, nodes[...], 0, 0)).astype(LOW)
-    for z in range(8):
-        for x in range(4):
-            for y in range(2):
-                start = ((z * 4 + x) * 2 + y) * 16
-                send[z * 2 + y, x * 16 : (x + 1) * 16, :COLS] = product[start : start + 16]
-                send[z * 2 + y, x * 16 : (x + 1) * 16, COLS:] = out_grad[start : start + 16]
-
-
-def sum_kernel(parts, send):
-    total = parts[0].astype(F32)
-    for p in range(1, PEERS):
-        total = total + parts[p].astype(F32)
-    total = total.astype(LOW)
-    for e in range(4):
-        for x in range(4):
-            send[e * 4 + x] = total[x * 16 : (x + 1) * 16]
+def weight_kernel(parts, shares, out_grad, send):
+    rows = jnp.concatenate([parts[e] for e in range(ENS)], axis=0)
+    held = HELD * LAT_DEV
+    for j in range(GROUPS):
+        nodes = jnp.concatenate([shares[e, j * held : (j + 1) * held] for e in range(ENS)], axis=0)
+        product = dot(nodes, rows, 0, 0).astype(LOW)
+        for b in range(GROUP // SHARE):
+            r = j * (GROUP // SHARE) + b
+            z, xy = r // PLANE, r % PLANE
+            at = slice(z * SHARE, (z + 1) * SHARE)
+            send[xy, at, :COLS] = product[b * SHARE : (b + 1) * SHARE]
+            send[xy, at, COLS:] = out_grad[r * SHARE : (r + 1) * SHARE]
+
+
+def sum_kernel(parts, total):
+    value = parts[0].astype(F32)
+    for p in range(1, PLANE):
+        value = value + parts[p].astype(F32)
+    total[...] = value.astype(LOW)
+
+
+def last_sum_kernel(parts, grad_latent, total):
+    value = parts[0].astype(F32)
+    for p in range(1, PLANE):
+        value = value + parts[p].astype(F32)
+    total[...] = value.astype(LOW)
 
 
 def finish_kernel(parts, key_weight_grad, value_weight_grad, out_weight_grad):
-    half = PEERS // 2
     total = parts[0, :, COLS:].astype(F32)
-    for p in range(1, PEERS):
-        total = total + parts[p, :, COLS:].astype(F32)
+    for e in range(1, ENS):
+        total = total + parts[e, :, COLS:].astype(F32)
     out_weight_grad[...] = total[:, :VARS]
-    for p in range(half):
+    for p in range(2):
         key_weight_grad[:, p * COLS : (p + 1) * COLS] = parts[p, :, :COLS].astype(F32)
-        value_weight_grad[:, p * COLS : (p + 1) * COLS] = parts[half + p, :, :COLS].astype(F32)
-
-
-def call(kernel, outs, scratch=(), flops=10**8, bytes_accessed=4 * 10**6):
+        value_weight_grad[:, p * COLS : (p + 1) * COLS] = parts[2 + p, :, :COLS].astype(F32)
+
+
+def whole(shape):
+    return pl.BlockSpec(shape, lambda i: (0,) * len(shape))
+
+
+def call(kernel, outs, scratch=(), specs=None, flops=10**8, bytes_accessed=4 * 10**6):
     def run(*operands):
+        places = specs or {}
         return pl.pallas_call(
             kernel,
+            grid=(1,),
+            in_specs=[places.get(i, whole(value.shape)) for i, value in enumerate(operands)],
+            out_specs=[whole(shape) for shape, _ in outs],
             out_shape=[jax.ShapeDtypeStruct(shape, kind) for shape, kind in outs],
             scratch_shapes=[pltpu.VMEM(shape, kind) for shape, kind in scratch],
-            compiler_params=pltpu.CompilerParams(vmem_limit_bytes=48 * 2**20),
+            compiler_params=pltpu.CompilerParams(vmem_limit_bytes=40 * 2**20),
             cost_estimate=pl.CostEstimate(
                 flops=flops, bytes_accessed=bytes_accessed, transcendentals=0
             ),
@@ -221,15 +251,17 @@
 
 
 def on_device(grid_embed, latent, key_weight, value_weight, out_weight, target, edges):
+    held = HELD * LAT_DEV
     out_rows = jnp.pad(out_weight, ((0, VARS_PAD - VARS), (0, 0)))
-    target = jnp.pad(target, ((0, VARS_PAD - VARS), (0, 0)))
-    nodes = lax.all_gather(latent.reshape(HELD * LAT_DEV, D), SPLIT, axis=0, tiled=True)
     upper_latent = band_shift(latent, -1)
-    preds, preds_low, normed_low, inverse, exps, damps, values = call(
+    own_keys, own_values, count = call(
+        own_kernel, [((held, D), LOW), ((held, D), LOW), ((GRID_DEV, GROUP), F32)]
+    )(latent, key_weight, value_weight, edges)
+    preds, share, normed_low, inverse, exps, damps, values = call(
         forward_kernel,
         [
             ((HELD, VARS_PAD, GRID_DEV), F32),
-            ((HELD, VARS_PAD, GRID_DEV), LOW),
+            ((PRED_ROW + VARS_PAD, GROUP), LOW),
             ((HELD, GRID_DEV, D), LOW),
             ((HELD, GRID_DEV, 128), F32),
             ((HELD, GRID_DEV, D), LOW),
@@ -237,8 +269,11 @@
             ((HELD * WINDOW, D), LOW),
         ],
         [((HELD * WINDOW, D), LOW), ((GRID_DEV, D), F32)],
-    )(grid_embed, latent, upper_latent, key_weight, value_weight, out_rows, edges)
-    every = lax.all_gather(preds_low, "ens", axis=0)
+    )(
+        grid_embed, latent, upper_latent, key_weight, value_weight, out_rows,
+        own_keys, own_values, count,
+    )
+    shares = lax.all_gather(share, "ens", axis=0)
     own, upper, out_grad = call(
         backward_kernel,
         [
@@ -246,18 +281,29 @@
             ((2, HELD, LAT_DEV, D), LOW),
             ((D, VARS_PAD), LOW),
         ],
-        [((GRID_DEV, D), F32)],
-    )(grid_embed, out_rows, target, preds, every, normed_low, inverse, exps, damps, values)
+        [((GRID_DEV, D), F32), ((VARS_PAD, GRID_DEV), F32)],
+        {4: pl.BlockSpec((ENS, VARS_PAD, GROUP), lambda i: (0, PRED_ROW // VARS_PAD, 0))},
+    )(grid_embed, out_rows, target, preds, shares, normed_low, inverse, exps, damps, values)
     lower = band_shift(upper, 1)
-    (joined,) = call(join_kernel, [((PEERS, HELD * LAT_DEV, COLS), LOW)])(own, lower)
+    (joined,) = call(join_kernel, [((ENS, held, COLS), LOW)])(own, lower)
     (grad_latent,) = call(latent_kernel, [((HELD, LAT_DEV, D), F32)])(
         joined, key_weight, value_weight
     )
-    parts = lax.all_to_all(joined, SPLIT, 0, 0, tiled=True)
-    (send,) = call(weight_kernel, [((PEERS, 64, 2 * COLS), LOW)])(parts, nodes, out_grad)
-    parts = lax.all_to_all(send, REST, 0, 0, tiled=True)
-    (send,) = call(sum_kernel, [((PEERS, 16, 2 * COLS), LOW)])(parts)
-    parts = lax.all_to_all(send, SPLIT, 0, 0, tiled=True)
+    parts = lax.all_to_all(joined, "ens", 0, 0, tiled=True)
+    (send,) = call(
+        weight_kernel,
+        [((PLANE, 8 * SHARE, COLS + VARS_PAD), LOW)],
+        specs={1: pl.BlockSpec((ENS, PRED_ROW, GROUP), lambda i: (0, 0, 0))},
+    )(parts, shares, out_grad)
+    parts = lax.all_to_all(send, ("x", "y"), 0, 0, tiled=True)
+    (total,) = call(sum_kernel, [((8 * SHARE, COLS + VARS_PAD), LOW)])(parts)
+    parts = lax.all_to_all(total.reshape(8, SHARE, COLS + VARS_PAD), "z", 0, 0, tiled=True)
+    (total,) = call(
+        last_sum_kernel,
+        [((SHARE, COLS + VARS_PAD), LOW)],
+        specs={1: pl.BlockSpec(memory_space=pl.ANY)},
+    )(parts, grad_latent)
+    parts = lax.all_gather(total, "ens", axis=0)
     results = call(finish_kernel, [((16, D), F32), ((16, D), F32), ((16, VARS), F32)])(parts)
     return (results[0], results[1], results[2], grad_latent)
 

time: 119 us -> 106 us (0.89)
  between operations: 14.1 us -> 0.73 us
  waiting for transfers between devices: 17.4 us -> 10.2 us
  starting transfers between devices: 11.7 us -> 17.7 us
  blocking collectives: 53.7 us -> 55.9 us
    all_gather x1 -> x2, blocking collectives: 11.9 us -> 21.8 us  [the longest x1 11.8 us: on_device(): shares = lax.all_gather(share, 'ens', axis=0)]
    all_to_all x2, blocking collectives: 41.8 us -> 34.1 us  [the longest x1 23.1 us: on_device(): parts = lax.all_to_all(send, ('x', 'y'), 0, 0, tiled=True)]
    all_to_all x1, starting transfers between devices: 8.13 us -> 12.1 us  [on_device(): lax.all_to_all(total.reshape(8, SHARE, COLS + VARS_PAD), 'z', 0, 0, tiled...]
    all_gather x1 -> x0, waiting for transfers between devices: 3.84 us -> none  [on_device(): lax.all_gather(latent.reshape(HELD * LAT_DEV, D), SPLIT, axis=0, tiled=True)]
    ppermute x2, waiting for transfers between devices: 9.04 us -> 5.52 us  [band_shift(): lax.ppermute(value, BAND, [(i, i + by) for i in range(64) if 0 <= i + by...]
    ppermute x2, starting transfers between devices: 3.53 us -> 5.58 us  [band_shift(): lax.ppermute(value, BAND, [(i, i + by) for i in range(64) if 0 <= i + by...]
    pallas_call x7 -> x9, Pallas kernels: 12.7 us -> 12.2 us  [run(): pl.pallas_call(kernel, grid=(1,), in_specs=[places.get(i, whole(value.sha...]
    unnamed x14 -> x18, local copies, waits for them, and re-layouts: 7.4 us -> 7.39 us
  transfers between devices with their start and end apart: 4 -> 3, of which waited for: 4 -> 2; matrix products, arithmetic and copies ran while one was open for 1% -> 1% of each run, Pallas kernels for 9% -> 3%
where the time goes in v2:
time: 106 us; the launch traced here: 105 us
  blocking collectives  55.9 us (53%)
  starting transfers between devices  17.7 us (17%)
  Pallas kernels  12.2 us (12%)
  waiting for transfers between devices  10.2 us (10%)
  local copies, waits for them, and re-layouts  8.34 us (8%)
    all_to_all x1, blocking collectives, on_device(): parts = lax.all_to_all(send, ('x', 'y'), 0, 0, tiled=True)  23.1 us
    pallas_call x9, Pallas kernels, run(): pl.pallas_call(kernel, grid=(1,), in_specs=[places.get(i, whole(value.sha...  12.2 us
    all_to_all x1, starting transfers between devices, on_device(): lax.all_to_all(total.reshape(8, SHARE, COLS + VARS_PAD), 'z', 0, 0, tiled...  12.1 us
    all_gather x1, blocking collectives, on_device(): shares = lax.all_gather(share, 'ens', axis=0)  11.8 us
    all_to_all x1, blocking collectives, on_device(): parts = lax.all_to_all(joined, 'ens', 0, 0, tiled=True)  11 us
    all_gather x1, blocking collectives, on_device(): parts = lax.all_gather(total, 'ens', axis=0)  10 us
    unnamed x18, local copies, waits for them, and re-layouts  7.39 us
    ppermute x2, starting transfers between devices, band_shift(): lax.ppermute(value, BAND, [(i, i + by) for i in range(64) if 0 <= i + by...  5.58 us
  transfers between devices with their start and end apart: 3, of which 2 were waited for; matrix products, arithmetic and copies ran while one was open for 1% of the time, Pallas kernels for 3%

profile of v2, /device:TPU:1, one launch (start us, length us, event | category | flops | bytes accessed | tf_op | source)
XLA Modules:
  0.0 105.0 jit_solution(2586494323838117857)
XLA Ops:
  0.6 1.3 %collective-permute-start = (bf16[2,32,1024]{2,1,0:T(8,128)(2,1)}, bf16[2,32,1024]{2,1,0:T(8,128)(2,1)S(1)}, u32[]{:S(2)}, u32[]{:S(2)}) collective-permute-start(bf16[2,32,1024]{2,1,0:T(8,128)(2,1)} %latent.3), channel_id=1, source_target_pairs={{1,0},{2,1},{3,2},{4,3},{5,4},{6,5},{7,6},{8,7},{9,8},{10,9},{11,1... | collective-permute-start | bytes 393224 | tf_op jit(solution)/shard_map/ppermute | solution.py:250
  1.9 1.0 pad.4.out_weight
  2.9 1.6 %copy-done = bf16[1024,1024]{1,0:T(8,128)(2,1)S(1)} copy-done((bf16[1024,1024]{1,0:T(8,128)(2,1)S(1)}, bf16[1024,1024]{1,0:T(8,128)(2,1)}, u32[]{:S(2)}) %copy-start) | copy-done | bytes 2097176
  4.5 1.6 %copy-done.2 = bf16[1024,1024]{1,0:T(8,128)(2,1)S(1)} copy-done((bf16[1024,1024]{1,0:T(8,128)(2,1)S(1)}, bf16[1024,1024]{1,0:T(8,128)(2,1)}, u32[]{:S(2)}) %copy-start.2) | copy-done | bytes 2097176
  6.1 0.9 copy-done.6
  7.0 0.7 copy-done.8
  7.7 0.9 own_kernel.1
  8.6 0.1 copy-done.4
  8.7 2.5 %forward_kernel.1 = (f32[2,128,128]{2,1,0:T(8,128)S(1)}, bf16[384,256]{1,0:T(8,128)(2,1)S(1)}, bf16[2,128,1024]{2,1,0:T(8,128)(2,1)S(1)}, f32[2,128,128]{2,1,0:T...) custom-call(bf16[2,128,1024]{2,1,0:T(8,128)(2,1)S(1)} %copy-done.4, ...), custom_call_target="tpu_custom_call" | custom-call | flops 100000000 | bytes 4000000 | tf_op jit(solution)/shard_map/forward_kernel/pallas_call | solution.py:232
  11.2 11.8 %all-gather = bf16[1536,256]{1,0:T(8,128)(2,1)S(1)} all-gather(bf16[384,256]{1,0:T(8,128)(2,1)S(1)} %get-tuple-element.24), channel_id=2, replica_groups=mesh['ens'=4,'z'=8,'x'=4,'y'=2] {'ens'}, dimensions={0}, use_global_device_ids=true | all-gather | bytes 983040 | tf_op jit(solution)/shard_map/all_gather | solution.py:276
  23.0 4.6 %backward_kernel.1 = (f32[2,2,32,1024]{3,2,1,0:T(8,128)S(1)}, bf16[2,2,32,1024]{3,2,1,0:T(8,128)(2,1)S(1)}, bf16[1024,128]{1,0:T(8,128)(2,1)S(1)}) custom-call(bf16[2,128,1024]{2,1,0:T(8,128)(2,1)S(1)} %copy-done.4, bf16[128,1024]{1,0:T(8,128)(2,1)S(1)} %pad.4.out_weight, f32[100,128]{1,0:T(8,128)S(1)} %copy-done.7, ...), custom_call_target="tpu_custom_call" | custom-call | flops 100000000 | bytes 4000000 | tf_op jit(solution)/shard_map/backward_kernel/pallas_call | solution.py:232
  27.6 4.3 %collective-permute-start.1 = (bf16[2,2,32,1024]{3,2,1,0:T(8,128)(2,1)S(1)}, bf16[2,2,32,1024]{3,2,1,0:T(8,128)(2,1)S(1)}, u32[]{:S(2)}, u32[]{:S(2)}) collective-permute-start(bf16[2,2,32,1024]{3,2,1,0:T(8,128)(2,1)S(1)} %get-tuple-element.31), channel_id=1, source_target_pairs={{0,1},{1,2},{2,3},{3,4},{4,5},{5,6},{6,7},{7,8},{8,9},{9,10},{10,1... | collective-permute-start | bytes 786440 | tf_op jit(solution)/shard_map/ppermute | solution.py:250
  31.9 5.5 %collective-permute-done.1.lower = bf16[2,2,32,1024]{3,2,1,0:T(8,128)(2,1)S(1)} collective-permute-done((bf16[2,2,32,1024]{3,2,1,0:T(8,128)(2,1)S(1)}, bf16[2,2,32,1024]{3,2,1,0:T(8,128)(2,1)S(1)}, u32[]{:S(2)}, u32[]{:S(2)}) %collective-permute-start.1) | collective-permute-done | bytes 262176 | tf_op jit(solution)/shard_map/ppermute | solution.py:250
  37.5 11.0 %all_to_all.15.parts = bf16[4,64,512]{2,1,0:T(8,128)(2,1)S(1)} all-to-all(bf16[4,64,512]{2,1,0:T(8,128)(2,1)S(1)} %join_kernel.1.joined), channel_id=1, replica_groups=mesh['ens'=4,'z'=8,'x'=4,'y'=2] {'ens'}, dimensions={0} | all-to-all | bytes 524288 | tf_op jit(solution)/shard_map/all_to_all | solution.py:292
  48.5 0.5 weight_kernel.1
  49.0 23.1 %all_to_all.16.parts = bf16[8,128,640]{2,1,0:T(8,128)(2,1)S(1)} all-to-all(bf16[8,128,640]{2,1,0:T(8,128)(2,1)S(1)} %weight_kernel.1), channel_id=1, replica_groups=mesh['ens'=4,'z'=8,'x'=4,'y'=2] {'x','y'}, dimensions={0} | all-to-all | bytes 2621440 | tf_op jit(solution)/shard_map/all_to_all | solution.py:298
  72.1 0.8 sum_kernel.1
  72.9 12.1 %all-to-all-start.2 = ((bf16[8,16,640]{2,1,0:T(8,128)(2,1)}), bf16[8,16,640]{2,1,0:T(8,128)(2,1)S(1)}, u32[]{:S(2)}, u32[]{:S(2)}) async-start(bf16[8,16,640]{2,1,0:T(8,128)(2,1)} %bitcast.1), calls=%async_computation.2 | async-start | bytes 327680 | tf_op jit(solution)/shard_map/all_to_all | solution.py:300
  85.0 1.6 %copy-done.3 = bf16[1024,1024]{1,0:T(8,128)(2,1)S(1)} copy-done((bf16[1024,1024]{1,0:T(8,128)(2,1)S(1)}, bf16[1024,1024]{1,0:T(8,128)(2,1)}, u32[]{:S(2)}) %copy-start.3) | copy-done | bytes 2097176
  86.6 2.1 %latent_kernel.1.grad_latent = f32[2,32,1024]{2,1,0:T(8,128)} custom-call(bf16[4,64,512]{2,1,0:T(8,128)(2,1)S(1)} %join_kernel.1.joined, bf16[1024,1024]{1,0:T(8,128)(2,1)S(1)} %copy-done.1, bf16[1024,1024]{1,0:T(8,128)(2,1)S(1)} %copy-done.3), custom_call_target="tpu_custom_call" | custom-call | flops 100000000 | bytes 4000000 | tf_op jit(solution)/shard_map/latent_kernel/pallas_call | solution.py:232
  88.7 4.7 %all-to-all-done.2.parts = bf16[8,16,640]{2,1,0:T(8,128)(2,1)S(1)} async-done(((bf16[8,16,640]{2,1,0:T(8,128)(2,1)}), bf16[8,16,640]{2,1,0:T(8,128)(2,1)S(1)}, u32[]{:S(2)}, u32[]{:S(2)}) %all-to-all-start.2) | async-done | bytes 163872 | tf_op jit(solution)/shard_map/all_to_all | solution.py:300
  93.4 0.9 copy-done.5
  94.4 10.0 %all-gather.1 = bf16[64,640]{1,0:T(8,128)(2,1)S(1)} all-gather(bf16[16,640]{1,0:T(8,128)(2,1)S(1)} %last_sum_kernel.1), channel_id=3, replica_groups=mesh['ens'=4,'z'=8,'x'=4,'y'=2] {'ens'}, dimensions={0}, use_global_device_ids=true | all-gather | bytes 102400 | tf_op jit(solution)/shard_map/all_gather | solution.py:306
  104.4 0.7 finish_kernel.1
  (14 shorter events, 0.1 us)
Async XLA Ops:
  0.6 8.0 %collective-permute-start = (bf16[2,32,1024]{2,1,0:T(8,128)(2,1)}, bf16[2,32,1024]{2,1,0:T(8,128)(2,1)S(1)}, u32[]{:S(2)}, u32[]{:S(2)}) collective-permute-start(bf16[2,32,1024]{2,1,0:T(8,128)(2,1)} %latent.3), channel_id=1, source_target_pairs={{1,0},{2,1},{3,2},{4,3},{5,4},{6,5},{7,6},{8,7},{9,8},{10,9},{11,1... | collective-permute-start | bytes 393224 | tf_op jit(solution)/shard_map/ppermute | solution.py:250
  2.9 1.6 %copy-start = (bf16[1024,1024]{1,0:T(8,128)(2,1)S(1)}, bf16[1024,1024]{1,0:T(8,128)(2,1)}, u32[]{:S(2)}) copy-start(bf16[1024,1024]{1,0:T(8,128)(2,1)} %key_weight.5) | copy-start | bytes 6291460
  4.5 1.6 %copy-start.2 = (bf16[1024,1024]{1,0:T(8,128)(2,1)S(1)}, bf16[1024,1024]{1,0:T(8,128)(2,1)}, u32[]{:S(2)}) copy-start(bf16[1024,1024]{1,0:T(8,128)(2,1)} %value_weight.5) | copy-start | bytes 6291460
  6.1 0.9 copy-start.6
  7.0 0.7 copy-start.8
  7.7 1.0 copy-start.4
  8.7 14.3 %copy-start.7 = (f32[100,128]{1,0:T(8,128)S(1)}, f32[100,128]{1,0:T(8,128)}, u32[]{:S(2)}) copy-start(f32[100,128]{1,0:T(8,128)} %target.1) | copy-start | bytes 153604
  27.6 9.8 %collective-permute-start.1 = (bf16[2,2,32,1024]{3,2,1,0:T(8,128)(2,1)S(1)}, bf16[2,2,32,1024]{3,2,1,0:T(8,128)(2,1)S(1)}, u32[]{:S(2)}, u32[]{:S(2)}) collective-permute-start(bf16[2,2,32,1024]{3,2,1,0:T(8,128)(2,1)S(1)} %get-tuple-element.31), channel_id=1, source_target_pairs={{0,1},{1,2},{2,3},{3,4},{4,5},{5,6},{6,7},{7,8},{8,9},{9,10},{10,1... | collective-permute-start | bytes 786440 | tf_op jit(solution)/shard_map/ppermute | solution.py:250
  49.0 36.0 %copy-start.1 = (bf16[1024,1024]{1,0:T(8,128)(2,1)S(1)}, bf16[1024,1024]{1,0:T(8,128)(2,1)}, u32[]{:S(2)}) copy-start(bf16[1024,1024]{1,0:T(8,128)(2,1)} %key_weight.5) | copy-start | bytes 6291460
  72.9 20.5 %all-to-all-start.2 = ((bf16[8,16,640]{2,1,0:T(8,128)(2,1)}), bf16[8,16,640]{2,1,0:T(8,128)(2,1)S(1)}, u32[]{:S(2)}, u32[]{:S(2)}) async-start(bf16[8,16,640]{2,1,0:T(8,128)(2,1)} %bitcast.1), calls=%async_computation.2 | async-start | bytes 327680 | tf_op jit(solution)/shard_map/all_to_all | solution.py:300
  85.0 1.6 %copy-start.3 = (bf16[1024,1024]{1,0:T(8,128)(2,1)S(1)}, bf16[1024,1024]{1,0:T(8,128)(2,1)}, u32[]{:S(2)}) copy-start(bf16[1024,1024]{1,0:T(8,128)(2,1)} %value_weight.5) | copy-start | bytes 6291460
  93.4 1.0 copy-start.5

commit v3 on v2

--- a/solution.py
+++ b/solution.py
@@ -23,10 +23,11 @@
 GROUPS = D // GROUP
 BAND = ("z", "x", "y")
 ENS = 4
-PLANE = 8
+NEAR = 8
+FAR = 8
 SHARE = 16
 COLS = 2 * D // ENS
-PRED_ROW = 2 * LAT_DEV * GROUPS
+HELD_ROWS = HELD * LAT_DEV
 
 F32 = jnp.float32
 LOW = jnp.bfloat16
@@ -58,10 +59,10 @@
     return total
 
 
-def own_kernel(latent, key_weight, value_weight, edges, keys, values, count):
+def own_kernel(latent, weights, edges, keys, values, count):
     rows = jnp.concatenate([latent[0], latent[1]], axis=0)
-    keys[...] = dot(rows, key_weight[...], 1, 0).astype(LOW)
-    values[...] = dot(rows, value_weight[...], 1, 0).astype(LOW)
+    keys[...] = dot(rows, weights[:D], 1, 0).astype(LOW)
+    values[...] = dot(rows, weights[D:], 1, 0).astype(LOW)
     target = edges[0:1, :]
     local = jnp.where(target >= 0, target & (GRID_DEV - 1), -1)
     source = edges[1:2, :] - (target >> 7) * LAT_DEV
@@ -73,13 +74,13 @@
 
 
 def forward_kernel(
-    embed, latent, lat_up, key_weight, value_weight, out_weight, own_keys, own_values, edge_count,
+    embed, lat_up, weights, out_weight, own_keys, own_values, edge_count,
     preds, share, normed_low, inverse, exps, damps, values,
     keys, mixed,
 ):
     rows = jnp.concatenate([lat_up[0], lat_up[1]], axis=0)
-    for own_rows, weight, window in ((own_keys, key_weight, keys), (own_values, value_weight, values)):
-        upper_rows = dot(rows, weight[...], 1, 0).astype(LOW)
+    for own_rows, weight, window in ((own_keys, 0, keys), (own_values, D, values)):
+        upper_rows = dot(rows, weights[weight : weight + D], 1, 0).astype(LOW)
         for m in range(HELD):
             window[m * WINDOW : m * WINDOW + LAT_DEV] = own_rows[m * LAT_DEV : (m + 1) * LAT_DEV]
             window[m * WINDOW + LAT_DEV : (m + 1) * WINDOW] = upper_rows[m * LAT_DEV : (m + 1) * LAT_DEV]
@@ -90,8 +91,6 @@
         square = jnp.zeros((GRID_DEV, 1), F32)
         for j in range(GROUPS):
             cols = slice(j * GROUP, (j + 1) * GROUP)
-            start = j * HELD * LAT_DEV + m * LAT_DEV
-            share[start : start + LAT_DEV] = latent[m, :, cols]
             query = embed[m, :, cols]
             key = by_head(keys[m * WINDOW : (m + 1) * WINDOW, cols], same)
             value = by_head(values[m * WINDOW : (m + 1) * WINDOW, cols], same)
@@ -109,7 +108,7 @@
         inverse[m] = jnp.broadcast_to(inv, (GRID_DEV, 128))
         pred = dot(out_weight[...], low, 1, 1)
         preds[m] = pred
-        share[PRED_ROW:, m * GRID_DEV : (m + 1) * GRID_DEV] = pred.astype(LOW)
+        share[m] = pred.astype(LOW)
 
 
 def backward_kernel(
@@ -127,7 +126,7 @@
         pair = jnp.zeros((VARS_PAD, GRID_DEV), F32)
         for e in range(MEMBERS // HELD):
             for k in range(HELD):
-                pair = pair + slope(pred - every[e, :, k * GRID_DEV : (k + 1) * GRID_DEV].astype(F32))
+                pair = pair + slope(pred - every[e, k].astype(F32))
         for k in range(HELD):
             pair = pair - slope(pred - preds[k].astype(LOW).astype(F32))
             if k != m:
@@ -166,48 +165,50 @@
             upper[1, m, :, cols] = value_part[LAT_DEV:].astype(LOW)
 
 
-def join_kernel(own, lower, send):
+def join_kernel(me, own, lower, joined, next1, next2, next3):
     for which in range(2):
         for m in range(HELD):
             total = (own[which, m] + lower[which, m].astype(F32)).astype(LOW)
             for p in range(2):
-                send[2 * which + p, m * LAT_DEV : (m + 1) * LAT_DEV, :] = total[
+                joined[2 * which + p, m * LAT_DEV : (m + 1) * LAT_DEV, :] = total[
                     :, p * COLS : (p + 1) * COLS
                 ]
-
-
-def latent_kernel(joined, key_weight, value_weight, grad_latent):
+    for k, block in ((1, next1), (2, next2), (3, next3)):
+        block[...] = joined[(me[0] + k) & (ENS - 1)]
+
+
+def latent_kernel(joined, key_weight, value_weight, grad_latent, token):
     key_grad = jnp.concatenate([joined[0], joined[1]], axis=1)
     value_grad = jnp.concatenate([joined[2], joined[3]], axis=1)
     total = dot(key_grad, key_weight[...], 1, 1) + dot(value_grad, value_weight[...], 1, 1)
     for m in range(HELD):
         grad_latent[m] = total[m * LAT_DEV : (m + 1) * LAT_DEV]
-
-
-def weight_kernel(parts, shares, out_grad, send):
-    rows = jnp.concatenate([parts[e] for e in range(ENS)], axis=0)
-    held = HELD * LAT_DEV
+    token[...] = total[:8, :128]
+
+
+def weight_kernel(
+    me, joined, last1, last2, last3, nodes, nodes1, nodes2, nodes3, out_grad, token, send
+):
+    rows = jnp.concatenate([joined[me[0]], last1[...], last2[...], last3[...]], axis=0)
     for j in range(GROUPS):
-        nodes = jnp.concatenate([shares[e, j * held : (j + 1) * held] for e in range(ENS)], axis=0)
-        product = dot(nodes, rows, 0, 0).astype(LOW)
+        cols = slice(j * GROUP, (j + 1) * GROUP)
+        held = [nodes[0, :, cols], nodes[1, :, cols]]
+        left = jnp.concatenate(
+            held + [block[m, :, cols] for block in (nodes1, nodes2, nodes3) for m in range(HELD)],
+            axis=0,
+        )
+        product = dot(left, rows, 0, 0).astype(LOW)
         for b in range(GROUP // SHARE):
             r = j * (GROUP // SHARE) + b
-            z, xy = r // PLANE, r % PLANE
-            at = slice(z * SHARE, (z + 1) * SHARE)
-            send[xy, at, :COLS] = product[b * SHARE : (b + 1) * SHARE]
-            send[xy, at, COLS:] = out_grad[r * SHARE : (r + 1) * SHARE]
+            far, near = r // NEAR, r % NEAR
+            at = slice(far * SHARE, (far + 1) * SHARE)
+            send[near, at, :COLS] = product[b * SHARE : (b + 1) * SHARE]
+            send[near, at, COLS:] = out_grad[r * SHARE : (r + 1) * SHARE]
 
 
 def sum_kernel(parts, total):
     value = parts[0].astype(F32)
-    for p in range(1, PLANE):
-        value = value + parts[p].astype(F32)
-    total[...] = value.astype(LOW)
-
-
-def last_sum_kernel(parts, grad_latent, total):
-    value = parts[0].astype(F32)
-    for p in range(1, PLANE):
+    for p in range(1, parts.shape[0]):
         value = value + parts[p].astype(F32)
     total[...] = value.astype(LOW)
 
@@ -250,18 +251,23 @@
     return lax.ppermute(value, BAND, [(i, i + by) for i in range(64) if 0 <= i + by < 64])
 
 
+def ens_shift(value, by):
+    return lax.ppermute(value, "ens", [(e, (e + by) % ENS) for e in range(ENS)])
+
+
 def on_device(grid_embed, latent, key_weight, value_weight, out_weight, target, edges):
-    held = HELD * LAT_DEV
     out_rows = jnp.pad(out_weight, ((0, VARS_PAD - VARS), (0, 0)))
     upper_latent = band_shift(latent, -1)
+    nodes1, nodes2, nodes3 = (ens_shift(latent, k) for k in (1, 2, 3))
+    weights = jnp.concatenate([key_weight, value_weight], axis=0)
     own_keys, own_values, count = call(
-        own_kernel, [((held, D), LOW), ((held, D), LOW), ((GRID_DEV, GROUP), F32)]
-    )(latent, key_weight, value_weight, edges)
+        own_kernel, [((HELD_ROWS, D), LOW), ((HELD_ROWS, D), LOW), ((GRID_DEV, GROUP), F32)]
+    )(latent, weights, edges)
     preds, share, normed_low, inverse, exps, damps, values = call(
         forward_kernel,
         [
             ((HELD, VARS_PAD, GRID_DEV), F32),
-            ((PRED_ROW + VARS_PAD, GROUP), LOW),
+            ((HELD, VARS_PAD, GRID_DEV), LOW),
             ((HELD, GRID_DEV, D), LOW),
             ((HELD, GRID_DEV, 128), F32),
             ((HELD, GRID_DEV, D), LOW),
@@ -270,9 +276,10 @@
         ],
         [((HELD * WINDOW, D), LOW), ((GRID_DEV, D), F32)],
     )(
-        grid_embed, latent, upper_latent, key_weight, value_weight, out_rows,
+        grid_embed, upper_latent, weights, out_rows,
         own_keys, own_values, count,
     )
+    me = lax.axis_index("ens").reshape(1)
     shares = lax.all_gather(share, "ens", axis=0)
     own, upper, out_grad = call(
         backward_kernel,
@@ -282,34 +289,33 @@
             ((D, VARS_PAD), LOW),
         ],
         [((GRID_DEV, D), F32), ((VARS_PAD, GRID_DEV), F32)],
-        {4: pl.BlockSpec((ENS, VARS_PAD, GROUP), lambda i: (0, PRED_ROW // VARS_PAD, 0))},
     )(grid_embed, out_rows, target, preds, shares, normed_low, inverse, exps, damps, values)
     lower = band_shift(upper, 1)
-    (joined,) = call(join_kernel, [((ENS, held, COLS), LOW)])(own, lower)
-    (grad_latent,) = call(latent_kernel, [((HELD, LAT_DEV, D), F32)])(
+    scalar = {0: pl.BlockSpec(memory_space=pltpu.SMEM)}
+    block = (HELD_ROWS, COLS)
+    joined, next1, next2, next3 = call(
+        join_kernel,
+        [((ENS, *block), LOW)] + [(block, LOW)] * 3,
+        specs=scalar,
+    )(me, own, lower)
+    last1, last2, last3 = (ens_shift(v, k) for k, v in ((1, next1), (2, next2), (3, next3)))
+    grad_latent, token = call(latent_kernel, [((HELD, LAT_DEV, D), F32), ((8, 128), F32)])(
         joined, key_weight, value_weight
     )
-    parts = lax.all_to_all(joined, "ens", 0, 0, tiled=True)
-    (send,) = call(
-        weight_kernel,
-        [((PLANE, 8 * SHARE, COLS + VARS_PAD), LOW)],
-        specs={1: pl.BlockSpec((ENS, PRED_ROW, GROUP), lambda i: (0, 0, 0))},
-    )(parts, shares, out_grad)
+    (send,) = call(weight_kernel, [((NEAR, FAR * SHARE, COLS + VARS_PAD), LOW)], specs=scalar)(
+        me, joined, last1, last2, last3, latent, nodes1, nodes2, nodes3, out_grad, token
+    )
     parts = lax.all_to_all(send, ("x", "y"), 0, 0, tiled=True)
-    (total,) = call(sum_kernel, [((8 * SHARE, COLS + VARS_PAD), LOW)])(parts)
-    parts = lax.all_to_all(total.reshape(8, SHARE, COLS + VARS_PAD), "z", 0, 0, tiled=True)
-    (total,) = call(
-        last_sum_kernel,
-        [((SHARE, COLS + VARS_PAD), LOW)],
-        specs={1: pl.BlockSpec(memory_space=pl.ANY)},
-    )(parts, grad_latent)
+    (total,) = call(sum_kernel, [((FAR * SHARE, COLS + VARS_PAD), LOW)])(parts)
+    parts = lax.all_to_all(total.reshape(FAR, SHARE, COLS + VARS_PAD), "z", 0, 0, tiled=True)
+    (total,) = call(sum_kernel, [((SHARE, COLS + VARS_PAD), LOW)])(parts)
     parts = lax.all_gather(total, "ens", axis=0)
     results = call(finish_kernel, [((16, D), F32), ((16, D), F32), ((16, VARS), F32)])(parts)
     return (results[0], results[1], results[2], grad_latent)
 
 
 def solution(mesh):
-    wide = Mesh(mesh.devices.reshape(4, 8, 4, 2), ("ens", "z", "x", "y"))
+    wide = Mesh(mesh.devices.reshape(4, 8, 4, 2), ("ens", *BAND))
     in_specs = (
         P("ens", BAND, None),
         P("ens", BAND, None),

time: 106 us -> 98.3 us (0.927)
  local copies, waits for them, and re-layouts: 8.34 us -> 3.58 us
  blocking collectives: 55.9 us -> 59.9 us
  waiting for transfers between devices: 10.2 us -> 6.41 us
  starting transfers between devices: 17.7 us -> 14.1 us
    all_to_all x1 -> x0, starting transfers between devices: 12.1 us -> none  [on_device(): lax.all_to_all(total.reshape(8, SHARE, COLS + VARS_PAD), 'z', 0, 0, tiled...]
    ppermute x0 -> x6, starting transfers between devices: none -> 9.93 us  [ens_shift(): return lax.ppermute(value, 'ens', [(e, (e + by) % ENS) for e in range(ENS)])]
    all_to_all x1, blocking collectives: 11 us -> 15.9 us  [on_device(): lax.all_to_all(total.reshape(FAR, SHARE, COLS + VARS_PAD), 'z', 0, 0, til...]
    all_to_all x1 -> x0, waiting for transfers between devices: 4.7 us -> none  [on_device(): lax.all_to_all(total.reshape(8, SHARE, COLS + VARS_PAD), 'z', 0, 0, tiled...]
    unnamed x18 -> x17, local copies, waits for them, and re-layouts: 7.39 us -> 3.39 us
    ppermute x0 -> x6, waiting for transfers between devices: none -> 1.81 us  [ens_shift(): return lax.ppermute(value, 'ens', [(e, (e + by) % ENS) for e in range(ENS)])]
    ppermute x2, starting transfers between devices: 5.58 us -> 4.18 us  [band_shift(): lax.ppermute(value, BAND, [(i, i + by) for i in range(64) if 0 <= i + by...]
  transfers between devices with their start and end apart: 3 -> 8, of which waited for: 2 -> 4; matrix products, arithmetic and copies ran while one was open for 1% -> 2% of each run, Pallas kernels for 3% -> 3%
where the time goes in v3:
time: 98.3 us; the launch traced here: 98 us
  blocking collectives  59.9 us (61%)
  starting transfers between devices  14.1 us (14%)
  Pallas kernels  13.2 us (13%)
  waiting for transfers between devices  6.41 us (7%)
  local copies, waits for them, and re-layouts  3.58 us (4%)
    all_to_all x1, blocking collectives, on_device(): parts = lax.all_to_all(send, ('x', 'y'), 0, 0, tiled=True)  22.8 us
    all_to_all x1, blocking collectives, on_device(): lax.all_to_all(total.reshape(FAR, SHARE, COLS + VARS_PAD), 'z', 0, 0, til...  15.9 us
    pallas_call x9, Pallas kernels, run(): pl.pallas_call(kernel, grid=(1,), in_specs=[places.get(i, whole(value.sha...  13.2 us
    all_gather x1, blocking collectives, on_device(): shares = lax.all_gather(share, 'ens', axis=0)  10.8 us
    all_gather x1, blocking collectives, on_device(): parts = lax.all_gather(total, 'ens', axis=0)  10.4 us
    ppermute x6, starting transfers between devices, ens_shift(): return lax.ppermute(value, 'ens', [(e, (e + by) % ENS) for e in range(ENS)])  9.93 us
    ppermute x2, waiting for transfers between devices, band_shift(): lax.ppermute(value, BAND, [(i, i + by) for i in range(64) if 0 <= i + by...  4.6 us
    ppermute x2, starting transfers between devices, band_shift(): lax.ppermute(value, BAND, [(i, i + by) for i in range(64) if 0 <= i + by...  4.18 us
  transfers between devices with their start and end apart: 8, of which 4 were waited for; matrix products, arithmetic and copies ran while one was open for 2% of the time, Pallas kernels for 3%

profile of v3, /device:TPU:1, one launch (start us, length us, event | category | flops | bytes accessed | tf_op | source)
XLA Modules:
  0.0 98.0 jit_solution(8105228303410246322)
XLA Ops:
  0.7 1.6 %collective-permute-start = (bf16[2,32,1024]{2,1,0:T(8,128)(2,1)}, bf16[2,32,1024]{2,1,0:T(8,128)(2,1)S(1)}, u32[]{:S(2)}, u32[]{:S(2)}) collective-permute-start(bf16[2,32,1024]{2,1,0:T(8,128)(2,1)} %nodes.1), channel_id=1, source_target_pairs={{1,0},{2,1},{3,2},{4,3},{5,4},{6,5},{7,6},{8,7},{9,8},{10,9},{11,1... | collective-permute-start | bytes 393224 | tf_op jit(solution)/shard_map/ppermute | solution.py:251
  2.2 1.8 %constant_dynamic-update-slice_fusion.1 = bf16[2048,1024]{1,0:T(8,128)(2,1)S(1)} fusion(bf16[1024,1024]{1,0:T(8,128)(2,1)} %key_weight.1), kind=kLoop, calls=%fused_computation.1 | loop fusion | bytes 4194304
  4.1 0.2 constant_dynamic-update-slice_fusion.weights
  4.3 0.9 own_kernel.1
  5.2 2.3 %collective-permute-done.lat_up = bf16[2,32,1024]{2,1,0:T(8,128)(2,1)S(1)} collective-permute-done((bf16[2,32,1024]{2,1,0:T(8,128)(2,1)}, bf16[2,32,1024]{2,1,0:T(8,128)(2,1)S(1)}, u32[]{:S(2)}, u32[]{:S(2)}) %collective-permute-start) | collective-permute-done | bytes 131104 | tf_op jit(solution)/shard_map/ppermute | solution.py:251
  7.5 2.5 %forward_kernel.1 = (f32[2,128,128]{2,1,0:T(8,128)S(1)}, bf16[2,128,128]{2,1,0:T(8,128)(2,1)S(1)}, bf16[2,128,1024]{2,1,0:T(8,128)(2,1)S(1)}, f32[2,128,128]{2,1...) custom-call(bf16[2,128,1024]{2,1,0:T(8,128)(2,1)S(1)} %copy-done.3, ...), custom_call_target="tpu_custom_call" | custom-call | flops 100000000 | bytes 4000000 | tf_op jit(solution)/shard_map/forward_kernel/pallas_call | solution.py:233
  10.0 10.8 %all-gather = bf16[8,128,128]{2,1,0:T(8,128)(2,1)S(1)} all-gather(bf16[2,128,128]{2,1,0:T(8,128)(2,1)S(1)} %get-tuple-element.30), channel_id=2, replica_groups=mesh['ens'=4,'z'=8,'x'=4,'y'=2] {'ens'}, dimensions={0}, use_global_device_ids=true | all-gather | bytes 327680 | tf_op jit(solution)/shard_map/all_gather | solution.py:283
  20.9 5.3 %backward_kernel.1 = (f32[2,2,32,1024]{3,2,1,0:T(8,128)S(1)}, bf16[2,2,32,1024]{3,2,1,0:T(8,128)(2,1)}, bf16[1024,128]{1,0:T(8,128)(2,1)S(1)}) custom-call(bf16[2,128,1024]{2,1,0:T(8,128)(2,1)S(1)} %copy-done.3, bf16[128,1024]{1,0:T(8,128)(2,1)S(1)} %pad.4.out_weight, f32[100,128]{1,0:T(8,128)S(1)} %copy-done.5, f32[2,128,128]{2,1,0:T(8,128)S(1)} %get-tuple-element.29.preds, ...), custom_call_target="tpu_custom_call" | custom-call | flops 100000000 | bytes 4000000 | tf_op jit(solution)/shard_map/backward_kernel/pallas_call | solution.py:233
  26.2 2.6 %collective-permute-start.1 = (bf16[2,2,32,1024]{3,2,1,0:T(8,128)(2,1)}, bf16[2,2,32,1024]{3,2,1,0:T(8,128)(2,1)S(1)}, u32[]{:S(2)}, u32[]{:S(2)}) collective-permute-start(bf16[2,2,32,1024]{3,2,1,0:T(8,128)(2,1)} %get-tuple-element.37), channel_id=1, source_target_pairs={{0,1},{1,2},{2,3},{3,4},{4,5},{5,6},{6,7},{7,8},{8,9},{9,10},{10,1... | collective-permute-start | bytes 786440 | tf_op jit(solution)/shard_map/ppermute | solution.py:251
  28.8 3.0 %collective-permute-start.5 = (bf16[2,32,1024]{2,1,0:T(8,128)(2,1)S(1)}, bf16[2,32,1024]{2,1,0:T(8,128)(2,1)S(1)}, u32[]{:S(2)}, u32[]{:S(2)}) collective-permute-start(bf16[2,32,1024]{2,1,0:T(8,128)(2,1)S(1)} %copy-done.4), channel_id=1, source_target_pairs={{0,64},{64,128},{128,192},{192,0},{1,65},{65,129},{129,193},{193,1... | collective-permute-start | bytes 393224 | tf_op jit(solution)/shard_map/ppermute | solution.py:255
  31.9 0.4 collective-permute-start.6
  32.4 2.3 %collective-permute-done.1.lower = bf16[2,2,32,1024]{3,2,1,0:T(8,128)(2,1)S(1)} collective-permute-done((bf16[2,2,32,1024]{3,2,1,0:T(8,128)(2,1)}, bf16[2,2,32,1024]{3,2,1,0:T(8,128)(2,1)S(1)}, u32[]{:S(2)}, u32[]{:S(2)}) %collective-permute-start.1) | collective-permute-done | bytes 262176 | tf_op jit(solution)/shard_map/ppermute | solution.py:251
  34.7 4.1 %collective-permute-start.2 = (bf16[64,512]{1,0:T(8,128)(2,1)S(1)}, bf16[64,512]{1,0:T(8,128)(2,1)S(1)}, u32[]{:S(2)}, u32[]{:S(2)}) collective-permute-start(bf16[64,512]{1,0:T(8,128)(2,1)S(1)} %get-tuple-element.39), channel_id=1, source_target_pairs={{0,64},{64,128},{128,192},{192,0},{1,65},{65,129},{129,193},{193,1... | collective-permute-start | bytes 196616 | tf_op jit(solution)/shard_map/ppermute | solution.py:255
  38.9 0.3 collective-permute-start.3
  39.2 1.9 %collective-permute-start.4 = (bf16[64,512]{1,0:T(8,128)(2,1)S(1)}, bf16[64,512]{1,0:T(8,128)(2,1)S(1)}, u32[]{:S(2)}, u32[]{:S(2)}) collective-permute-start(bf16[64,512]{1,0:T(8,128)(2,1)S(1)} %get-tuple-element.41), channel_id=1, source_target_pairs={{0,192},{64,0},{128,64},{192,128},{1,193},{65,1},{129,65},{193,129... | collective-permute-start | bytes 196616 | tf_op jit(solution)/shard_map/ppermute | solution.py:255
  41.1 1.6 %copy-done.2 = bf16[1024,1024]{1,0:T(8,128)(2,1)S(1)} copy-done((bf16[1024,1024]{1,0:T(8,128)(2,1)S(1)}, bf16[1024,1024]{1,0:T(8,128)(2,1)}, u32[]{:S(2)}) %copy-start.2) | copy-done | bytes 2097176
  42.7 2.1 %latent_kernel.1 = (f32[2,32,1024]{2,1,0:T(8,128)}, f32[8,128]{1,0:T(8,128)S(1)}) custom-call(bf16[4,64,512]{2,1,0:T(8,128)(2,1)S(1)} %get-tuple-element.38.joined, bf16[1024,1024]{1,0:T(8,128)(2,1)S(1)} %copy-done, bf16[1024,1024]{1,0:T(8,128)(2,1)S(1)} %copy-done.2), custom_call_target="tpu_custom_call" | custom-call | flops 100000000 | bytes 4000000 | tf_op jit(solution)/shard_map/latent_kernel/pallas_call | solution.py:233
  44.8 1.3 %collective-permute-done.3.last2 = bf16[64,512]{1,0:T(8,128)(2,1)S(1)} collective-permute-done((bf16[64,512]{1,0:T(8,128)(2,1)S(1)}, bf16[64,512]{1,0:T(8,128)(2,1)S(1)}, u32[]{:S(2)}, u32[]{:S(2)}) %collective-permute-start.3) | collective-permute-done | bytes 65568 | tf_op jit(solution)/shard_map/ppermute | solution.py:255
  46.1 0.5 collective-permute-done.4.last3
  46.6 1.4 %weight_kernel.1 = bf16[8,128,640]{2,1,0:T(8,128)(2,1)S(1)} custom-call(s32[1]{0:T(128)} %bitcast.me, bf16[4,64,512]{2,1,0:T(8,128)(2,1)S(1)} %get-tuple-element.38.joined, bf16[64,512]{1,0:T(8,128)(2,1)S(1)} %collective-permute-done.2.last1, bf16[64,512]{1,0:T(8,128)(2,1)S(1)} %collective-permute-done.3.last2, ...), custom_call_target="tpu_custom_call" | custom-call | flops 100000000 | bytes 4000000 | tf_op jit(solution)/shard_map/weight_kernel/pallas_call | solution.py:233
  48.1 22.8 %all_to_all.10.parts = bf16[8,128,640]{2,1,0:T(8,128)(2,1)S(1)} all-to-all(bf16[8,128,640]{2,1,0:T(8,128)(2,1)S(1)} %weight_kernel.1), channel_id=1, replica_groups=mesh['ens'=4,'z'=8,'x'=4,'y'=2] {'x','y'}, dimensions={0} | all-to-all | bytes 2621440 | tf_op jit(solution)/shard_map/all_to_all | solution.py:308
  71.0 15.9 %all_to_all.11.parts = bf16[8,16,640]{2,1,0:T(8,128)(2,1)S(1)} all-to-all(bf16[8,16,640]{2,1,0:T(8,128)(2,1)S(1)} %bitcast.5), channel_id=1, replica_groups=mesh['ens'=4,'z'=8,'x'=4,'y'=2] {'z'}, dimensions={0} | all-to-all | bytes 327680 | tf_op jit(solution)/shard_map/all_to_all | solution.py:310
  86.9 10.4 %all-gather.1 = bf16[64,640]{1,0:T(8,128)(2,1)S(1)} all-gather(bf16[16,640]{1,0:T(8,128)(2,1)S(1)} %sum_kernel.3), channel_id=3, replica_groups=mesh['ens'=4,'z'=8,'x'=4,'y'=2] {'ens'}, dimensions={0}, use_global_device_ids=true | all-gather | bytes 102400 | tf_op jit(solution)/shard_map/all_gather | solution.py:312
  97.4 0.7 finish_kernel.1
  (24 shorter events, 0.5 us)
Async XLA Ops:
  0.6 3.6 %copy-start.4 = (bf16[2,32,1024]{2,1,0:T(8,128)(2,1)S(1)}, bf16[2,32,1024]{2,1,0:T(8,128)(2,1)}, u32[]{:S(2)}) copy-start(bf16[2,32,1024]{2,1,0:T(8,128)(2,1)} %nodes.1) | copy-start | bytes 393220
  0.6 3.4 %copy-start.7 = (bf16[100,1024]{1,0:T(8,128)(2,1)S(1)}, bf16[100,1024]{1,0:T(8,128)(2,1)}, u32[]{:S(2)}) copy-start(bf16[100,1024]{1,0:T(8,128)(2,1)} %param.11) | copy-start | bytes 614404
  0.7 3.4 %copy-start.1 = (bf16[1024,1024]{1,0:T(8,128)(2,1)S(1)}, bf16[1024,1024]{1,0:T(8,128)(2,1)}, u32[]{:S(2)}) copy-start(bf16[1024,1024]{1,0:T(8,128)(2,1)} %value_weight.1) | copy-start | bytes 6291460
  0.7 3.6 %copy-start.6 = (s32[2,512]{1,0:T(2,128)S(1)}, s32[2,512]{1,0:T(2,128)}, u32[]{:S(2)}) copy-start(s32[2,512]{1,0:T(2,128)} %edges.1) | copy-start | bytes 12292
  0.7 6.9 %collective-permute-start = (bf16[2,32,1024]{2,1,0:T(8,128)(2,1)}, bf16[2,32,1024]{2,1,0:T(8,128)(2,1)S(1)}, u32[]{:S(2)}, u32[]{:S(2)}) collective-permute-start(bf16[2,32,1024]{2,1,0:T(8,128)(2,1)} %nodes.1), channel_id=1, source_target_pairs={{1,0},{2,1},{3,2},{4,3},{5,4},{6,5},{7,6},{8,7},{9,8},{10,9},{11,1... | collective-permute-start | bytes 393224 | tf_op jit(solution)/shard_map/ppermute | solution.py:251
  4.1 3.5 %copy-start.3 = (bf16[2,128,1024]{2,1,0:T(8,128)(2,1)S(1)}, bf16[2,128,1024]{2,1,0:T(8,128)(2,1)}, u32[]{:S(2)}) copy-start(bf16[2,128,1024]{2,1,0:T(8,128)(2,1)} %embed.3) | copy-start | bytes 1572868
  4.3 16.6 %copy-start.5 = (f32[100,128]{1,0:T(8,128)S(1)}, f32[100,128]{1,0:T(8,128)}, u32[]{:S(2)}) copy-start(f32[100,128]{1,0:T(8,128)} %target.1) | copy-start | bytes 153604
  7.5 33.6 %copy-start = (bf16[1024,1024]{1,0:T(8,128)(2,1)S(1)}, bf16[1024,1024]{1,0:T(8,128)(2,1)}, u32[]{:S(2)}) copy-start(bf16[1024,1024]{1,0:T(8,128)(2,1)} %key_weight.1) | copy-start | bytes 6291460
  26.2 8.5 %collective-permute-start.1 = (bf16[2,2,32,1024]{3,2,1,0:T(8,128)(2,1)}, bf16[2,2,32,1024]{3,2,1,0:T(8,128)(2,1)S(1)}, u32[]{:S(2)}, u32[]{:S(2)}) collective-permute-start(bf16[2,2,32,1024]{3,2,1,0:T(8,128)(2,1)} %get-tuple-element.37), channel_id=1, source_target_pairs={{0,1},{1,2},{2,3},{3,4},{4,5},{5,6},{6,7},{7,8},{8,9},{9,10},{10,1... | collective-permute-start | bytes 786440 | tf_op jit(solution)/shard_map/ppermute | solution.py:251
  28.8 10.4 %collective-permute-start.5 = (bf16[2,32,1024]{2,1,0:T(8,128)(2,1)S(1)}, bf16[2,32,1024]{2,1,0:T(8,128)(2,1)S(1)}, u32[]{:S(2)}, u32[]{:S(2)}) collective-permute-start(bf16[2,32,1024]{2,1,0:T(8,128)(2,1)S(1)} %copy-done.4), channel_id=1, source_target_pairs={{0,64},{64,128},{128,192},{192,0},{1,65},{65,129},{129,193},{193,1... | collective-permute-start | bytes 393224 | tf_op jit(solution)/shard_map/ppermute | solution.py:255
  31.9 13.0 %collective-permute-start.6 = (bf16[2,32,1024]{2,1,0:T(8,128)(2,1)S(1)}, bf16[2,32,1024]{2,1,0:T(8,128)(2,1)S(1)}, u32[]{:S(2)}, u32[]{:S(2)}) collective-permute-start(bf16[2,32,1024]{2,1,0:T(8,128)(2,1)S(1)} %copy-done.4), channel_id=1, source_target_pairs={{0,128},{64,192},{128,0},{192,64},{1,129},{65,193},{129,1},{193,65... | collective-permute-start | bytes 393224 | tf_op jit(solution)/shard_map/ppermute | solution.py:255
  32.2 12.6 %collective-permute-start.7 = (bf16[2,32,1024]{2,1,0:T(8,128)(2,1)S(1)}, bf16[2,32,1024]{2,1,0:T(8,128)(2,1)}, u32[]{:S(2)}, u32[]{:S(2)}) collective-permute-start(bf16[2,32,1024]{2,1,0:T(8,128)(2,1)S(1)} %copy-done.4), channel_id=1, source_target_pairs={{0,192},{64,0},{128,64},{192,128},{1,193},{65,1},{129,65},{193,129... | collective-permute-start | bytes 393224 | tf_op jit(solution)/shard_map/ppermute | solution.py:255
  34.7 10.1 %collective-permute-start.2 = (bf16[64,512]{1,0:T(8,128)(2,1)S(1)}, bf16[64,512]{1,0:T(8,128)(2,1)S(1)}, u32[]{:S(2)}, u32[]{:S(2)}) collective-permute-start(bf16[64,512]{1,0:T(8,128)(2,1)S(1)} %get-tuple-element.39), channel_id=1, source_target_pairs={{0,64},{64,128},{128,192},{192,0},{1,65},{65,129},{129,193},{193,1... | collective-permute-start | bytes 196616 | tf_op jit(solution)/shard_map/ppermute | solution.py:255
  38.9 7.2 %collective-permute-start.3 = (bf16[64,512]{1,0:T(8,128)(2,1)S(1)}, bf16[64,512]{1,0:T(8,128)(2,1)S(1)}, u32[]{:S(2)}, u32[]{:S(2)}) collective-permute-start(bf16[64,512]{1,0:T(8,128)(2,1)S(1)} %get-tuple-element.40), channel_id=1, source_target_pairs={{0,128},{64,192},{128,0},{192,64},{1,129},{65,193},{129,1},{193,65... | collective-permute-start | bytes 196616 | tf_op jit(solution)/shard_map/ppermute | solution.py:255
  39.2 7.4 %collective-permute-start.4 = (bf16[64,512]{1,0:T(8,128)(2,1)S(1)}, bf16[64,512]{1,0:T(8,128)(2,1)S(1)}, u32[]{:S(2)}, u32[]{:S(2)}) collective-permute-start(bf16[64,512]{1,0:T(8,128)(2,1)S(1)} %get-tuple-element.41), channel_id=1, source_target_pairs={{0,192},{64,0},{128,64},{192,128},{1,193},{65,1},{129,65},{193,129... | collective-permute-start | bytes 196616 | tf_op jit(solution)/shard_map/ppermute | solution.py:255
  41.1 1.6 %copy-start.2 = (bf16[1024,1024]{1,0:T(8,128)(2,1)S(1)}, bf16[1024,1024]{1,0:T(8,128)(2,1)}, u32[]{:S(2)}) copy-start(bf16[1024,1024]{1,0:T(8,128)(2,1)} %value_weight.1) | copy-start | bytes 6291460

commit v4 on v3

--- a/solution.py
+++ b/solution.py
@@ -28,6 +28,7 @@
 SHARE = 16
 COLS = 2 * D // ENS
 HELD_ROWS = HELD * LAT_DEV
+PRED_ROW = HELD_ROWS * GROUPS
 
 F32 = jnp.float32
 LOW = jnp.bfloat16
@@ -91,6 +92,8 @@
         square = jnp.zeros((GRID_DEV, 1), F32)
         for j in range(GROUPS):
             cols = slice(j * GROUP, (j + 1) * GROUP)
+            start = j * HELD_ROWS + m * LAT_DEV
+            share[start : start + LAT_DEV] = lat_up[m, :, cols]
             query = embed[m, :, cols]
             key = by_head(keys[m * WINDOW : (m + 1) * WINDOW, cols], same)
             value = by_head(values[m * WINDOW : (m + 1) * WINDOW, cols], same)
@@ -108,12 +111,12 @@
         inverse[m] = jnp.broadcast_to(inv, (GRID_DEV, 128))
         pred = dot(out_weight[...], low, 1, 1)
         preds[m] = pred
-        share[m] = pred.astype(LOW)
+        share[PRED_ROW:, m * GRID_DEV : (m + 1) * GRID_DEV] = pred.astype(LOW)
 
 
 def backward_kernel(
-    embed, out_weight, target, preds, every, normed_low, inverse, exps, damps, values,
-    own, upper, out_grad,
+    me, embed, out_weight, target, preds, every, normed_low, inverse, exps, damps, values,
+    halves, next1, next2, next3, out_grad,
     grad, truth,
 ):
     truth[...] = jnp.zeros((VARS_PAD, GRID_DEV), F32)
@@ -126,7 +129,7 @@
         pair = jnp.zeros((VARS_PAD, GRID_DEV), F32)
         for e in range(MEMBERS // HELD):
             for k in range(HELD):
-                pair = pair + slope(pred - every[e, k].astype(F32))
+                pair = pair + slope(pred - every[e, :, k * GRID_DEV : (k + 1) * GRID_DEV].astype(F32))
         for k in range(HELD):
             pair = pair - slope(pred - preds[k].astype(LOW).astype(F32))
             if k != m:
@@ -159,44 +162,35 @@
             raw_grad = (weight * (weight_grad - inner) * damps[m, :, cols].astype(F32)).astype(LOW)
             key_part = from_head(dot(raw_grad, embed[m, :, cols], 0, 0))
             value_part = from_head(dot(weight.astype(LOW), mixed_grad, 0, 0))
-            own[0, m, :, cols] = key_part[:LAT_DEV]
-            own[1, m, :, cols] = value_part[:LAT_DEV]
-            upper[0, m, :, cols] = key_part[LAT_DEV:].astype(LOW)
-            upper[1, m, :, cols] = value_part[LAT_DEV:].astype(LOW)
-
-
-def join_kernel(me, own, lower, joined, next1, next2, next3):
-    for which in range(2):
-        for m in range(HELD):
-            total = (own[which, m] + lower[which, m].astype(F32)).astype(LOW)
-            for p in range(2):
-                joined[2 * which + p, m * LAT_DEV : (m + 1) * LAT_DEV, :] = total[
-                    :, p * COLS : (p + 1) * COLS
-                ]
+            at = slice(j % 2 * GROUP, (j % 2 + 1) * GROUP)
+            for p, part in ((j // 2, key_part), (2 + j // 2, value_part)):
+                start = m * LAT_DEV
+                halves[p, start : start + LAT_DEV, at] = part[:LAT_DEV].astype(LOW)
+                start = start + HELD_ROWS
+                halves[p, start : start + LAT_DEV, at] = part[LAT_DEV:].astype(LOW)
     for k, block in ((1, next1), (2, next2), (3, next3)):
-        block[...] = joined[(me[0] + k) & (ENS - 1)]
-
-
-def latent_kernel(joined, key_weight, value_weight, grad_latent, token):
-    key_grad = jnp.concatenate([joined[0], joined[1]], axis=1)
-    value_grad = jnp.concatenate([joined[2], joined[3]], axis=1)
+        block[...] = halves[me[0] ^ k]
+
+
+def latent_kernel(halves, key_weight, value_weight, own, upper):
+    key_grad = jnp.concatenate([halves[0], halves[1]], axis=1)
+    value_grad = jnp.concatenate([halves[2], halves[3]], axis=1)
     total = dot(key_grad, key_weight[...], 1, 1) + dot(value_grad, value_weight[...], 1, 1)
-    for m in range(HELD):
-        grad_latent[m] = total[m * LAT_DEV : (m + 1) * LAT_DEV]
-    token[...] = total[:8, :128]
+    own[...] = total[:HELD_ROWS]
+    upper[...] = total[HELD_ROWS:].astype(LOW)
 
 
 def weight_kernel(
-    me, joined, last1, last2, last3, nodes, nodes1, nodes2, nodes3, out_grad, token, send
+    me, halves, last1, last2, last3, nodes, nodes1, nodes2, nodes3, shares, out_grad, upper, send
 ):
-    rows = jnp.concatenate([joined[me[0]], last1[...], last2[...], last3[...]], axis=0)
+    rows = jnp.concatenate([halves[me[0]], last1[...], last2[...], last3[...]], axis=0)
     for j in range(GROUPS):
         cols = slice(j * GROUP, (j + 1) * GROUP)
-        held = [nodes[0, :, cols], nodes[1, :, cols]]
-        left = jnp.concatenate(
-            held + [block[m, :, cols] for block in (nodes1, nodes2, nodes3) for m in range(HELD)],
-            axis=0,
-        )
+        at = slice(j * HELD_ROWS, (j + 1) * HELD_ROWS)
+        left = []
+        for k, block in enumerate((nodes, nodes1, nodes2, nodes3)):
+            left += [block[0, :, cols], block[1, :, cols], shares[me[0] ^ k, at]]
+        left = jnp.concatenate(left, axis=0)
         product = dot(left, rows, 0, 0).astype(LOW)
         for b in range(GROUP // SHARE):
             r = j * (GROUP // SHARE) + b
@@ -213,7 +207,12 @@
     total[...] = value.astype(LOW)
 
 
-def finish_kernel(parts, key_weight_grad, value_weight_grad, out_weight_grad):
+def finish_kernel(
+    parts, own, lower, key_weight_grad, value_weight_grad, out_weight_grad, grad_latent
+):
+    for m in range(HELD):
+        rows = slice(m * LAT_DEV, (m + 1) * LAT_DEV)
+        grad_latent[m] = own[rows] + lower[rows].astype(F32)
     total = parts[0, :, COLS:].astype(F32)
     for e in range(1, ENS):
         total = total + parts[e, :, COLS:].astype(F32)
@@ -251,14 +250,15 @@
     return lax.ppermute(value, BAND, [(i, i + by) for i in range(64) if 0 <= i + by < 64])
 
 
-def ens_shift(value, by):
-    return lax.ppermute(value, "ens", [(e, (e + by) % ENS) for e in range(ENS)])
+def ens_swap(value, k):
+    return lax.ppermute(value, "ens", [(e, e ^ k) for e in range(ENS)])
 
 
 def on_device(grid_embed, latent, key_weight, value_weight, out_weight, target, edges):
     out_rows = jnp.pad(out_weight, ((0, VARS_PAD - VARS), (0, 0)))
     upper_latent = band_shift(latent, -1)
-    nodes1, nodes2, nodes3 = (ens_shift(latent, k) for k in (1, 2, 3))
+    nodes1, nodes2 = ens_swap(latent, 1), ens_swap(latent, 2)
+    nodes3 = ens_swap(nodes2, 1)
     weights = jnp.concatenate([key_weight, value_weight], axis=0)
     own_keys, own_values, count = call(
         own_kernel, [((HELD_ROWS, D), LOW), ((HELD_ROWS, D), LOW), ((GRID_DEV, GROUP), F32)]
@@ -267,7 +267,7 @@
         forward_kernel,
         [
             ((HELD, VARS_PAD, GRID_DEV), F32),
-            ((HELD, VARS_PAD, GRID_DEV), LOW),
+            ((PRED_ROW + VARS_PAD, GROUP), LOW),
             ((HELD, GRID_DEV, D), LOW),
             ((HELD, GRID_DEV, 128), F32),
             ((HELD, GRID_DEV, D), LOW),
@@ -281,37 +281,41 @@
     )
     me = lax.axis_index("ens").reshape(1)
     shares = lax.all_gather(share, "ens", axis=0)
-    own, upper, out_grad = call(
+    block = (2 * HELD_ROWS, COLS)
+    scalar = {0: pl.BlockSpec(memory_space=pltpu.SMEM)}
+    halves, next1, next2, next3, out_grad = call(
         backward_kernel,
-        [
-            ((2, HELD, LAT_DEV, D), F32),
-            ((2, HELD, LAT_DEV, D), LOW),
-            ((D, VARS_PAD), LOW),
-        ],
+        [((ENS, *block), LOW)] + [(block, LOW)] * 3 + [((D, VARS_PAD), LOW)],
         [((GRID_DEV, D), F32), ((VARS_PAD, GRID_DEV), F32)],
-    )(grid_embed, out_rows, target, preds, shares, normed_low, inverse, exps, damps, values)
+        {**scalar, 5: pl.BlockSpec((ENS, VARS_PAD, GROUP), lambda i: (0, PRED_ROW // VARS_PAD, 0))},
+    )(me, grid_embed, out_rows, target, preds, shares, normed_low, inverse, exps, damps, values)
+    last1, last2, last3 = (ens_swap(v, k) for k, v in ((1, next1), (2, next2), (3, next3)))
+    own, upper = call(latent_kernel, [((HELD_ROWS, D), F32), ((HELD_ROWS, D), LOW)])(
+        halves, key_weight, value_weight
+    )
     lower = band_shift(upper, 1)
-    scalar = {0: pl.BlockSpec(memory_space=pltpu.SMEM)}
-    block = (HELD_ROWS, COLS)
-    joined, next1, next2, next3 = call(
-        join_kernel,
-        [((ENS, *block), LOW)] + [(block, LOW)] * 3,
-        specs=scalar,
-    )(me, own, lower)
-    last1, last2, last3 = (ens_shift(v, k) for k, v in ((1, next1), (2, next2), (3, next3)))
-    grad_latent, token = call(latent_kernel, [((HELD, LAT_DEV, D), F32), ((8, 128), F32)])(
-        joined, key_weight, value_weight
-    )
-    (send,) = call(weight_kernel, [((NEAR, FAR * SHARE, COLS + VARS_PAD), LOW)], specs=scalar)(
-        me, joined, last1, last2, last3, latent, nodes1, nodes2, nodes3, out_grad, token
+    (send,) = call(
+        weight_kernel,
+        [((NEAR, FAR * SHARE, COLS + VARS_PAD), LOW)],
+        specs={
+            **scalar,
+            9: pl.BlockSpec((ENS, PRED_ROW, GROUP), lambda i: (0, 0, 0)),
+            11: pl.BlockSpec((16, 128), lambda i: (0, 0)),
+        },
+    )(
+        me, halves, last1, last2, last3, latent, nodes1, nodes2, nodes3, shares, out_grad, upper
     )
     parts = lax.all_to_all(send, ("x", "y"), 0, 0, tiled=True)
     (total,) = call(sum_kernel, [((FAR * SHARE, COLS + VARS_PAD), LOW)])(parts)
     parts = lax.all_to_all(total.reshape(FAR, SHARE, COLS + VARS_PAD), "z", 0, 0, tiled=True)
     (total,) = call(sum_kernel, [((SHARE, COLS + VARS_PAD), LOW)])(parts)
     parts = lax.all_gather(total, "ens", axis=0)
-    results = call(finish_kernel, [((16, D), F32), ((16, D), F32), ((16, VARS), F32)])(parts)
-    return (results[0], results[1], results[2], grad_latent)
+    return tuple(
+        call(
+            finish_kernel,
+            [((16, D), F32), ((16, D), F32), ((16, VARS), F32), ((HELD, LAT_DEV, D), F32)],
+        )(parts, own, lower)
+    )
 
 
 def solution(mesh):

time: 98.3 us -> 94.9 us (0.965)
  blocking collectives: 59.9 us -> 43.2 us
  starting transfers between devices: 14.1 us -> 22.2 us
  local copies, waits for them, and re-layouts: 3.58 us -> 6.85 us
  waiting for transfers between devices: 6.41 us -> 9.58 us
  Pallas kernels: 13.2 us -> 12 us
    all_to_all x1 -> x0, blocking collectives: 15.9 us -> none  [on_device(): lax.all_to_all(total.reshape(FAR, SHARE, COLS + VARS_PAD), 'z', 0, 0, til...]
    all_to_all x0 -> x1, starting transfers between devices: none -> 9.13 us  [on_device(): lax.all_to_all(total.reshape(FAR, SHARE, COLS + VARS_PAD), 'z', 0, 0, til...]
    all_to_all x0 -> x1, waiting for transfers between devices: none -> 5.05 us  [on_device(): lax.all_to_all(total.reshape(FAR, SHARE, COLS + VARS_PAD), 'z', 0, 0, til...]
    ppermute x2, waiting for transfers between devices: 4.6 us -> 0.01 us  [band_shift(): lax.ppermute(value, BAND, [(i, i + by) for i in range(64) if 0 <= i + by...]
    ppermute x6, waiting for transfers between devices: 1.81 us -> 4.53 us  [ens_swap(): return lax.ppermute(value, 'ens', [(e, e ^ k) for e in range(ENS)])]
    unnamed x17, local copies, waits for them, and re-layouts: 3.39 us -> 5.35 us
    ppermute x6, starting transfers between devices: 9.93 us -> 8.52 us  [ens_swap(): return lax.ppermute(value, 'ens', [(e, e ^ k) for e in range(ENS)])]
    concatenate x1, local copies, waits for them, and re-layouts: 0.17 us -> 1.48 us  [on_device(): weights = jnp.concatenate([key_weight, value_weight], axis=0)]
  transfers between devices with their start and end apart: 8 -> 9, of which waited for: 4 -> 3; matrix products, arithmetic and copies ran while one was open for 2% -> 5% of each run, Pallas kernels for 3% -> 10%
where the time goes in v4:
time: 94.9 us; the launch traced here: 94.5 us
  blocking collectives  43.2 us (46%)
  starting transfers between devices  22.2 us (23%)
  Pallas kernels  12 us (13%)
  waiting for transfers between devices  9.58 us (10%)
  local copies, waits for them, and re-layouts  6.85 us (7%)
    all_to_all x1, blocking collectives, on_device(): parts = lax.all_to_all(send, ('x', 'y'), 0, 0, tiled=True)  23.7 us
    pallas_call x8, Pallas kernels, run(): pl.pallas_call(kernel, grid=(1,), in_specs=[places.get(i, whole(value.sha...  12 us
    all_gather x1, blocking collectives, on_device(): shares = lax.all_gather(share, 'ens', axis=0)  10.2 us
    all_gather x1, blocking collectives, on_device(): parts = lax.all_gather(total, 'ens', axis=0)  9.21 us
    all_to_all x1, starting transfers between devices, on_device(): lax.all_to_all(total.reshape(FAR, SHARE, COLS + VARS_PAD), 'z', 0, 0, til...  9.13 us
    ppermute x6, starting transfers between devices, ens_swap(): return lax.ppermute(value, 'ens', [(e, e ^ k) for e in range(ENS)])  8.52 us
    unnamed x17, local copies, waits for them, and re-layouts  5.35 us
    all_to_all x1, waiting for transfers between devices, on_device(): lax.all_to_all(total.reshape(FAR, SHARE, COLS + VARS_PAD), 'z', 0, 0, til...  5.05 us
  transfers between devices with their start and end apart: 9, of which 3 were waited for; matrix products, arithmetic and copies ran while one was open for 5% of the time, Pallas kernels for 10%

profile of v4, /device:TPU:1, one launch (start us, length us, event | category | flops | bytes accessed | tf_op | source)
XLA Modules:
  0.0 94.5 jit_solution(10164846148909914369)
XLA Ops:
  0.7 1.4 %collective-permute-start = (bf16[2,32,1024]{2,1,0:T(8,128)(2,1)}, bf16[2,32,1024]{2,1,0:T(8,128)(2,1)S(1)}, u32[]{:S(2)}, u32[]{:S(2)}) collective-permute-start(bf16[2,32,1024]{2,1,0:T(8,128)(2,1)} %nodes.1), channel_id=1, source_target_pairs={{1,0},{2,1},{3,2},{4,3},{5,4},{6,5},{7,6},{8,7},{9,8},{10,9},{11,1... | collective-permute-start | bytes 393224 | tf_op jit(solution)/shard_map/ppermute | solution.py:250
  2.1 3.8 %collective-permute-start.5 = (bf16[2,32,1024]{2,1,0:T(8,128)(2,1)}, bf16[2,32,1024]{2,1,0:T(8,128)(2,1)S(1)}, u32[]{:S(2)}, u32[]{:S(2)}) collective-permute-start(bf16[2,32,1024]{2,1,0:T(8,128)(2,1)} %nodes.1), channel_id=1, source_target_pairs={{0,128},{64,192},{128,0},{192,64},{1,129},{65,193},{129,1},{193,65... | collective-permute-start | bytes 393224 | tf_op jit(solution)/shard_map/ppermute | solution.py:254
  5.9 1.0 %collective-permute-start.4 = (bf16[2,32,1024]{2,1,0:T(8,128)(2,1)}, bf16[2,32,1024]{2,1,0:T(8,128)(2,1)S(1)}, u32[]{:S(2)}, u32[]{:S(2)}) collective-permute-start(bf16[2,32,1024]{2,1,0:T(8,128)(2,1)} %nodes.1), channel_id=1, source_target_pairs={{0,64},{64,0},{128,192},{192,128},{1,65},{65,1},{129,193},{193,129... | collective-permute-start | bytes 393224 | tf_op jit(solution)/shard_map/ppermute | solution.py:254
  6.9 3.1 %constant_dynamic-update-slice_fusion.1 = bf16[2048,1024]{1,0:T(8,128)(2,1)} fusion(bf16[1024,1024]{1,0:T(8,128)(2,1)} %key_weight.1), kind=kLoop, calls=%fused_computation.1 | loop fusion | bytes 4194304
  10.1 1.5 %constant_dynamic-update-slice_fusion.weights = bf16[2048,1024]{1,0:T(8,128)(2,1)} fusion(bf16[2048,1024]{1,0:T(8,128)(2,1)} %constant_dynamic-update-slice_fusion.1, bf16[1024,1024]{1,0:T(8,128)(2,1)S(1)} %copy-done.2), kind=kLoop, calls=%fused_computation | loop fusion | bytes 4194304 | tf_op jit(solution)/shard_map/concatenate | solution.py:262
  11.5 2.2 %copy-done = bf16[2048,1024]{1,0:T(8,128)(2,1)S(1)} copy-done((bf16[2048,1024]{1,0:T(8,128)(2,1)S(1)}, bf16[2048,1024]{1,0:T(8,128)(2,1)}, u32[]{:S(2)}) %copy-start) | copy-done | bytes 4194328
  13.7 0.9 own_kernel.1
  14.7 2.5 %forward_kernel.1 = (f32[2,128,128]{2,1,0:T(8,128)S(1)}, bf16[384,256]{1,0:T(8,128)(2,1)S(1)}, bf16[2,128,1024]{2,1,0:T(8,128)(2,1)S(1)}, f32[2,128,128]{2,1,0:T...) custom-call(bf16[2,128,1024]{2,1,0:T(8,128)(2,1)S(1)} %copy-done.3, ...), custom_call_target="tpu_custom_call" | custom-call | flops 100000000 | bytes 4000000 | tf_op jit(solution)/shard_map/forward_kernel/pallas_call | solution.py:232
  17.2 10.2 %all-gather = bf16[1536,256]{1,0:T(8,128)(2,1)S(1)} all-gather(bf16[384,256]{1,0:T(8,128)(2,1)S(1)} %get-tuple-element.25), channel_id=2, replica_groups=mesh['ens'=4,'z'=8,'x'=4,'y'=2] {'ens'}, dimensions={0}, use_global_device_ids=true | all-gather | bytes 983040 | tf_op jit(solution)/shard_map/all_gather | solution.py:283
  27.4 4.6 %backward_kernel.1 = (bf16[4,128,512]{2,1,0:T(8,128)(2,1)S(1)}, bf16[128,512]{1,0:T(8,128)(2,1)S(1)}, bf16[128,512]{1,0:T(8,128)(2,1)S(1)}, bf16[128,512]{1,0:T(8,128)(2,1)S(1)}, bf16[1024,128]{1,0:T(8,128)(2,1)S(1)}) custom-call(s32[1]{0:T(128)} %bitcast.me, bf16[2,128,1024]{2,1,0:T(8,128)(2,1)S(1)} %copy-done.3, bf16[128,1024]{1,0:T(8,128)(2,1)S(1)} %pad.4.out_weight, ...), custom_call_target="tpu_custom_call" | custom-call | flops 100000000 | bytes 4000000 | tf_op jit(solution)/shard_map/backward_kernel/pallas_call | solution.py:232
  32.1 0.2 collective-permute-start.1
  32.3 1.8 %collective-permute-start.2 = (bf16[128,512]{1,0:T(8,128)(2,1)S(1)}, bf16[128,512]{1,0:T(8,128)(2,1)S(1)}, u32[]{:S(2)}, u32[]{:S(2)}) collective-permute-start(bf16[128,512]{1,0:T(8,128)(2,1)S(1)} %get-tuple-element.33), channel_id=1, source_target_pairs={{0,128},{64,192},{128,0},{192,64},{1,129},{65,193},{129,1},{193,65... | collective-permute-start | bytes 393224 | tf_op jit(solution)/shard_map/ppermute | solution.py:254
  34.1 1.7 %collective-permute-start.3 = (bf16[128,512]{1,0:T(8,128)(2,1)S(1)}, bf16[128,512]{1,0:T(8,128)(2,1)S(1)}, u32[]{:S(2)}, u32[]{:S(2)}) collective-permute-start(bf16[128,512]{1,0:T(8,128)(2,1)S(1)} %get-tuple-element.34), channel_id=1, source_target_pairs={{0,192},{64,128},{128,64},{192,0},{1,193},{65,129},{129,65},{193,1... | collective-permute-start | bytes 393224 | tf_op jit(solution)/shard_map/ppermute | solution.py:254
  35.8 1.5 %latent_kernel.1 = (f32[64,1024]{1,0:T(8,128)S(1)}, bf16[64,1024]{1,0:T(8,128)(2,1)S(1)}) custom-call(bf16[4,128,512]{2,1,0:T(8,128)(2,1)S(1)} %get-tuple-element.31.halves, bf16[1024,1024]{1,0:T(8,128)(2,1)S(1)} %copy-done.1, bf16[1024,1024]{1,0:T(8,128)(2,1)S(1)} %copy-done.2), custom_call_target="tpu_custom_call" | custom-call | flops 100000000 | bytes 4000000 | tf_op jit(solution)/shard_map/latent_kernel/pallas_call | solution.py:232
  37.4 1.2 %collective-permute-done.2.last2 = bf16[128,512]{1,0:T(8,128)(2,1)S(1)} collective-permute-done((bf16[128,512]{1,0:T(8,128)(2,1)S(1)}, bf16[128,512]{1,0:T(8,128)(2,1)S(1)}, u32[]{:S(2)}, u32[]{:S(2)}) %collective-permute-start.2) | collective-permute-done | bytes 131104 | tf_op jit(solution)/shard_map/ppermute | solution.py:254
  38.6 3.3 %collective-permute-done.3.last3 = bf16[128,512]{1,0:T(8,128)(2,1)S(1)} collective-permute-done((bf16[128,512]{1,0:T(8,128)(2,1)S(1)}, bf16[128,512]{1,0:T(8,128)(2,1)S(1)}, u32[]{:S(2)}, u32[]{:S(2)}) %collective-permute-start.3) | collective-permute-done | bytes 131104 | tf_op jit(solution)/shard_map/ppermute | solution.py:254
  41.9 0.8 weight_kernel.1
  42.6 23.7 %all_to_all.10.parts = bf16[8,128,640]{2,1,0:T(8,128)(2,1)S(1)} all-to-all(bf16[8,128,640]{2,1,0:T(8,128)(2,1)S(1)} %weight_kernel.1), channel_id=1, replica_groups=mesh['ens'=4,'z'=8,'x'=4,'y'=2] {'x','y'}, dimensions={0} | all-to-all | bytes 2621440 | tf_op jit(solution)/shard_map/all_to_all | solution.py:308
  66.4 0.8 sum_kernel.2
  67.2 9.1 %all-to-all-start.1 = ((bf16[8,16,640]{2,1,0:T(8,128)(2,1)}), bf16[8,16,640]{2,1,0:T(8,128)(2,1)S(1)}, u32[]{:S(2)}, u32[]{:S(2)}) async-start(bf16[8,16,640]{2,1,0:T(8,128)(2,1)} %bitcast.2), calls=%async_computation.1 | async-start | bytes 327680 | tf_op jit(solution)/shard_map/all_to_all | solution.py:310
  76.4 3.1 %collective-permute-start.7 = (bf16[64,1024]{1,0:T(8,128)(2,1)S(1)}, bf16[64,1024]{1,0:T(8,128)(2,1)S(1)}, u32[]{:S(2)}, u32[]{:S(2)}) collective-permute-start(bf16[64,1024]{1,0:T(8,128)(2,1)S(1)} %get-tuple-element.36.upper), channel_id=1, source_target_pairs={{0,1},{1,2},{2,3},{3,4},{4,5},{5,6},{6,7},{7,8},{8,9},{9,10},{10,1... | collective-permute-start | bytes 393224 | tf_op jit(solution)/shard_map/ppermute | solution.py:250
  79.4 5.0 %all-to-all-done.1.parts = bf16[8,16,640]{2,1,0:T(8,128)(2,1)S(1)} async-done(((bf16[8,16,640]{2,1,0:T(8,128)(2,1)}), bf16[8,16,640]{2,1,0:T(8,128)(2,1)S(1)}, u32[]{:S(2)}, u32[]{:S(2)}) %all-to-all-start.1) | async-done | bytes 163872 | tf_op jit(solution)/shard_map/all_to_all | solution.py:310
  84.5 9.2 %all-gather.1 = bf16[64,640]{1,0:T(8,128)(2,1)S(1)} all-gather(bf16[16,640]{1,0:T(8,128)(2,1)S(1)} %sum_kernel.3), channel_id=3, replica_groups=mesh['ens'=4,'z'=8,'x'=4,'y'=2] {'ens'}, dimensions={0}, use_global_device_ids=true | all-gather | bytes 102400 | tf_op jit(solution)/shard_map/all_gather | solution.py:312
  93.7 0.8 finish_kernel.1
  (24 shorter events, 0.1 us)
Async XLA Ops:
  0.6 9.4 %copy-start.7 = (bf16[100,1024]{1,0:T(8,128)(2,1)S(1)}, bf16[100,1024]{1,0:T(8,128)(2,1)}, u32[]{:S(2)}) copy-start(bf16[100,1024]{1,0:T(8,128)(2,1)} %param.11) | copy-start | bytes 614404
  0.6 9.4 %copy-start.2 = (bf16[1024,1024]{1,0:T(8,128)(2,1)S(1)}, bf16[1024,1024]{1,0:T(8,128)(2,1)}, u32[]{:S(2)}) copy-start(bf16[1024,1024]{1,0:T(8,128)(2,1)} %value_weight.1) | copy-start | bytes 6291460
  0.7 14.0 %collective-permute-start = (bf16[2,32,1024]{2,1,0:T(8,128)(2,1)}, bf16[2,32,1024]{2,1,0:T(8,128)(2,1)S(1)}, u32[]{:S(2)}, u32[]{:S(2)}) collective-permute-start(bf16[2,32,1024]{2,1,0:T(8,128)(2,1)} %nodes.1), channel_id=1, source_target_pairs={{1,0},{2,1},{3,2},{4,3},{5,4},{6,5},{7,6},{8,7},{9,8},{10,9},{11,1... | collective-permute-start | bytes 393224 | tf_op jit(solution)/shard_map/ppermute | solution.py:250
  2.1 33.7 %collective-permute-start.5 = (bf16[2,32,1024]{2,1,0:T(8,128)(2,1)}, bf16[2,32,1024]{2,1,0:T(8,128)(2,1)S(1)}, u32[]{:S(2)}, u32[]{:S(2)}) collective-permute-start(bf16[2,32,1024]{2,1,0:T(8,128)(2,1)} %nodes.1), channel_id=1, source_target_pairs={{0,128},{64,192},{128,0},{192,64},{1,129},{65,193},{129,1},{193,65... | collective-permute-start | bytes 393224 | tf_op jit(solution)/shard_map/ppermute | solution.py:254
  5.9 31.4 %collective-permute-start.4 = (bf16[2,32,1024]{2,1,0:T(8,128)(2,1)}, bf16[2,32,1024]{2,1,0:T(8,128)(2,1)S(1)}, u32[]{:S(2)}, u32[]{:S(2)}) collective-permute-start(bf16[2,32,1024]{2,1,0:T(8,128)(2,1)} %nodes.1), channel_id=1, source_target_pairs={{0,64},{64,0},{128,192},{192,128},{1,65},{65,1},{129,193},{193,129... | collective-permute-start | bytes 393224 | tf_op jit(solution)/shard_map/ppermute | solution.py:254
  6.9 4.7 %copy-start.4 = (bf16[2,32,1024]{2,1,0:T(8,128)(2,1)S(1)}, bf16[2,32,1024]{2,1,0:T(8,128)(2,1)}, u32[]{:S(2)}) copy-start(bf16[2,32,1024]{2,1,0:T(8,128)(2,1)} %nodes.1) | copy-start | bytes 393220
  6.9 4.7 %copy-start.6 = (s32[2,512]{1,0:T(2,128)S(1)}, s32[2,512]{1,0:T(2,128)}, u32[]{:S(2)}) copy-start(s32[2,512]{1,0:T(2,128)} %edges.1) | copy-start | bytes 12292
  10.0 4.7 %copy-start.3 = (bf16[2,128,1024]{2,1,0:T(8,128)(2,1)S(1)}, bf16[2,128,1024]{2,1,0:T(8,128)(2,1)}, u32[]{:S(2)}) copy-start(bf16[2,128,1024]{2,1,0:T(8,128)(2,1)} %embed.3) | copy-start | bytes 1572868
  11.5 2.2 %copy-start = (bf16[2048,1024]{1,0:T(8,128)(2,1)S(1)}, bf16[2048,1024]{1,0:T(8,128)(2,1)}, u32[]{:S(2)}) copy-start(bf16[2048,1024]{1,0:T(8,128)(2,1)} %constant_dynamic-update-slice_fusion.weights) | copy-start | bytes 12582916
  14.7 12.8 %copy-start.5 = (f32[100,128]{1,0:T(8,128)S(1)}, f32[100,128]{1,0:T(8,128)}, u32[]{:S(2)}) copy-start(f32[100,128]{1,0:T(8,128)} %target.1) | copy-start | bytes 153604
  14.7 21.1 %copy-start.1 = (bf16[1024,1024]{1,0:T(8,128)(2,1)S(1)}, bf16[1024,1024]{1,0:T(8,128)(2,1)}, u32[]{:S(2)}) copy-start(bf16[1024,1024]{1,0:T(8,128)(2,1)} %key_weight.1) | copy-start | bytes 6291460
  32.1 5.3 %collective-permute-start.1 = (bf16[128,512]{1,0:T(8,128)(2,1)S(1)}, bf16[128,512]{1,0:T(8,128)(2,1)S(1)}, u32[]{:S(2)}, u32[]{:S(2)}) collective-permute-start(bf16[128,512]{1,0:T(8,128)(2,1)S(1)} %get-tuple-element.32), channel_id=1, source_target_pairs={{0,64},{64,0},{128,192},{192,128},{1,65},{65,1},{129,193},{193,129... | collective-permute-start | bytes 393224 | tf_op jit(solution)/shard_map/ppermute | solution.py:254
  32.3 6.2 %collective-permute-start.2 = (bf16[128,512]{1,0:T(8,128)(2,1)S(1)}, bf16[128,512]{1,0:T(8,128)(2,1)S(1)}, u32[]{:S(2)}, u32[]{:S(2)}) collective-permute-start(bf16[128,512]{1,0:T(8,128)(2,1)S(1)} %get-tuple-element.33), channel_id=1, source_target_pairs={{0,128},{64,192},{128,0},{192,64},{1,129},{65,193},{129,1},{193,65... | collective-permute-start | bytes 393224 | tf_op jit(solution)/shard_map/ppermute | solution.py:254
  34.1 7.7 %collective-permute-start.3 = (bf16[128,512]{1,0:T(8,128)(2,1)S(1)}, bf16[128,512]{1,0:T(8,128)(2,1)S(1)}, u32[]{:S(2)}, u32[]{:S(2)}) collective-permute-start(bf16[128,512]{1,0:T(8,128)(2,1)S(1)} %get-tuple-element.34), channel_id=1, source_target_pairs={{0,192},{64,128},{128,64},{192,0},{1,193},{65,129},{129,65},{193,1... | collective-permute-start | bytes 393224 | tf_op jit(solution)/shard_map/ppermute | solution.py:254
  35.8 6.0 %collective-permute-start.6 = (bf16[2,32,1024]{2,1,0:T(8,128)(2,1)S(1)}, bf16[2,32,1024]{2,1,0:T(8,128)(2,1)S(1)}, u32[]{:S(2)}, u32[]{:S(2)}) collective-permute-start(bf16[2,32,1024]{2,1,0:T(8,128)(2,1)S(1)} %collective-permute-done.5.nodes2), channel_id=1, source_target_pairs={{0,64},{64,0},{128,192},{192,128},{1,65},{65,1},{129,193},{193,129... | collective-permute-start | bytes 393224 | tf_op jit(solution)/shard_map/ppermute | solution.py:254
  67.2 17.3 %all-to-all-start.1 = ((bf16[8,16,640]{2,1,0:T(8,128)(2,1)}), bf16[8,16,640]{2,1,0:T(8,128)(2,1)S(1)}, u32[]{:S(2)}, u32[]{:S(2)}) async-start(bf16[8,16,640]{2,1,0:T(8,128)(2,1)} %bitcast.2), calls=%async_computation.1 | async-start | bytes 327680 | tf_op jit(solution)/shard_map/all_to_all | solution.py:310
  76.4 17.4 %collective-permute-start.7 = (bf16[64,1024]{1,0:T(8,128)(2,1)S(1)}, bf16[64,1024]{1,0:T(8,128)(2,1)S(1)}, u32[]{:S(2)}, u32[]{:S(2)}) collective-permute-start(bf16[64,1024]{1,0:T(8,128)(2,1)S(1)} %get-tuple-element.36.upper), channel_id=1, source_target_pairs={{0,1},{1,2},{2,3},{3,4},{4,5},{5,6},{6,7},{7,8},{8,9},{9,10},{10,1... | collective-permute-start | bytes 393224 | tf_op jit(solution)/shard_map/ppermute | solution.py:250

commit v5 on v4

--- a/solution.py
+++ b/solution.py
@@ -60,10 +60,10 @@
     return total
 
 
-def own_kernel(latent, weights, edges, keys, values, count):
+def own_kernel(latent, edges, key_left, key_right, keys, count):
     rows = jnp.concatenate([latent[0], latent[1]], axis=0)
-    keys[...] = dot(rows, weights[:D], 1, 0).astype(LOW)
-    values[...] = dot(rows, weights[D:], 1, 0).astype(LOW)
+    keys[:, : D // 2] = dot(rows, key_left[...], 1, 0).astype(LOW)
+    keys[:, D // 2 :] = dot(rows, key_right[...], 1, 0).astype(LOW)
     target = edges[0:1, :]
     local = jnp.where(target >= 0, target & (GRID_DEV - 1), -1)
     source = edges[1:2, :] - (target >> 7) * LAT_DEV
@@ -75,16 +75,20 @@
 
 
 def forward_kernel(
-    embed, lat_up, weights, out_weight, own_keys, own_values, edge_count,
+    embed, latent, lat_up, key_left, key_right, value_weight, out_weight, own_keys, edge_count,
     preds, share, normed_low, inverse, exps, damps, values,
     keys, mixed,
 ):
+    rows = jnp.concatenate([latent[0], lat_up[0], latent[1], lat_up[1]], axis=0)
+    values[...] = dot(rows, value_weight[...], 1, 0).astype(LOW)
     rows = jnp.concatenate([lat_up[0], lat_up[1]], axis=0)
-    for own_rows, weight, window in ((own_keys, 0, keys), (own_values, D, values)):
-        upper_rows = dot(rows, weights[weight : weight + D], 1, 0).astype(LOW)
+    for c, weight in enumerate((key_left, key_right)):
+        cols = slice(c * (D // 2), (c + 1) * (D // 2))
+        upper_rows = dot(rows, weight[...], 1, 0).astype(LOW)
         for m in range(HELD):
-            window[m * WINDOW : m * WINDOW + LAT_DEV] = own_rows[m * LAT_DEV : (m + 1) * LAT_DEV]
-            window[m * WINDOW + LAT_DEV : (m + 1) * WINDOW] = upper_rows[m * LAT_DEV : (m + 1) * LAT_DEV]
+            part = slice(m * LAT_DEV, (m + 1) * LAT_DEV)
+            keys[m * WINDOW : m * WINDOW + LAT_DEV, cols] = own_keys[part, cols]
+            keys[m * WINDOW + LAT_DEV : (m + 1) * WINDOW, cols] = upper_rows[part]
     count = edge_count[...]
     same = same_head()
     ones = same.astype(F32).astype(LOW)
@@ -259,10 +263,10 @@
     upper_latent = band_shift(latent, -1)
     nodes1, nodes2 = ens_swap(latent, 1), ens_swap(latent, 2)
     nodes3 = ens_swap(nodes2, 1)
-    weights = jnp.concatenate([key_weight, value_weight], axis=0)
-    own_keys, own_values, count = call(
-        own_kernel, [((HELD_ROWS, D), LOW), ((HELD_ROWS, D), LOW), ((GRID_DEV, GROUP), F32)]
-    )(latent, weights, edges)
+    halves_of_key = (key_weight[:, : D // 2], key_weight[:, D // 2 :])
+    own_keys, count = call(own_kernel, [((HELD_ROWS, D), LOW), ((GRID_DEV, GROUP), F32)])(
+        latent, edges, *halves_of_key
+    )
     preds, share, normed_low, inverse, exps, damps, values = call(
         forward_kernel,
         [
@@ -276,8 +280,7 @@
         ],
         [((HELD * WINDOW, D), LOW), ((GRID_DEV, D), F32)],
     )(
-        grid_embed, upper_latent, weights, out_rows,
-        own_keys, own_values, count,
+        grid_embed, latent, upper_latent, *halves_of_key, value_weight, out_rows, own_keys, count
     )
     me = lax.axis_index("ens").reshape(1)
     shares = lax.all_gather(share, "ens", axis=0)

time: 94.9 us -> 90.4 us (0.953)
  local copies, waits for them, and re-layouts: 6.85 us -> 2.81 us
    unnamed x17 -> x14, local copies, waits for them, and re-layouts: 5.35 us -> 1.12 us
    slice x0 -> x1, local copies, waits for them, and re-layouts: none -> 1.68 us  [on_device(): halves_of_key = (key_weight[:, :D // 2], key_weight[:, D // 2:])]
    concatenate x1 -> x0, local copies, waits for them, and re-layouts: 1.48 us -> none  [on_device(): weights = jnp.concatenate([key_weight, value_weight], axis=0)]
  transfers between devices with their start and end apart: 9 -> 9, of which waited for: 3 -> 3; matrix products, arithmetic and copies ran while one was open for 5% -> 2% of each run, Pallas kernels for 10% -> 10%
where the time goes in v5:
time: 90.4 us; the launch traced here: 90.1 us
  blocking collectives  43.4 us (48%)
  starting transfers between devices  21.9 us (24%)
  Pallas kernels  11.5 us (13%)
  waiting for transfers between devices  9.59 us (11%)
  local copies, waits for them, and re-layouts  2.81 us (3%)
    all_to_all x1, blocking collectives, on_device(): parts = lax.all_to_all(send, ('x', 'y'), 0, 0, tiled=True)  23.7 us
    pallas_call x8, Pallas kernels, run(): pl.pallas_call(kernel, grid=(1,), in_specs=[places.get(i, whole(value.sha...  11.5 us
    all_gather x1, blocking collectives, on_device(): shares = lax.all_gather(share, 'ens', axis=0)  10.6 us
    all_gather x1, blocking collectives, on_device(): parts = lax.all_gather(total, 'ens', axis=0)  9.2 us
    all_to_all x1, starting transfers between devices, on_device(): lax.all_to_all(total.reshape(FAR, SHARE, COLS + VARS_PAD), 'z', 0, 0, til...  8.86 us
    ppermute x6, starting transfers between devices, ens_swap(): return lax.ppermute(value, 'ens', [(e, e ^ k) for e in range(ENS)])  8.52 us
    all_to_all x1, waiting for transfers between devices, on_device(): lax.all_to_all(total.reshape(FAR, SHARE, COLS + VARS_PAD), 'z', 0, 0, til...  5.06 us
    ppermute x6, waiting for transfers between devices, ens_swap(): return lax.ppermute(value, 'ens', [(e, e ^ k) for e in range(ENS)])  4.53 us
  transfers between devices with their start and end apart: 9, of which 3 were waited for; matrix products, arithmetic and copies ran while one was open for 2% of the time, Pallas kernels for 10%

profile of v5, /device:TPU:1, one launch (start us, length us, event | category | flops | bytes accessed | tf_op | source)
XLA Modules:
  0.0 90.1 jit_solution(6732664168613924252)
XLA Ops:
  0.7 1.4 %collective-permute-start = (bf16[2,32,1024]{2,1,0:T(8,128)(2,1)}, bf16[2,32,1024]{2,1,0:T(8,128)(2,1)S(1)}, u32[]{:S(2)}, u32[]{:S(2)}) collective-permute-start(bf16[2,32,1024]{2,1,0:T(8,128)(2,1)} %nodes.1), channel_id=1, source_target_pairs={{1,0},{2,1},{3,2},{4,3},{5,4},{6,5},{7,6},{8,7},{9,8},{10,9},{11,1... | collective-permute-start | bytes 393224 | tf_op jit(solution)/shard_map/ppermute | solution.py:254
  2.1 3.8 %collective-permute-start.5 = (bf16[2,32,1024]{2,1,0:T(8,128)(2,1)}, bf16[2,32,1024]{2,1,0:T(8,128)(2,1)S(1)}, u32[]{:S(2)}, u32[]{:S(2)}) collective-permute-start(bf16[2,32,1024]{2,1,0:T(8,128)(2,1)} %nodes.1), channel_id=1, source_target_pairs={{0,128},{64,192},{128,0},{192,64},{1,129},{65,193},{129,1},{193,65... | collective-permute-start | bytes 393224 | tf_op jit(solution)/shard_map/ppermute | solution.py:258
  5.9 1.0 %collective-permute-start.4 = (bf16[2,32,1024]{2,1,0:T(8,128)(2,1)}, bf16[2,32,1024]{2,1,0:T(8,128)(2,1)S(1)}, u32[]{:S(2)}, u32[]{:S(2)}) collective-permute-start(bf16[2,32,1024]{2,1,0:T(8,128)(2,1)} %nodes.1), channel_id=1, source_target_pairs={{0,64},{64,0},{128,192},{192,128},{1,65},{65,1},{129,193},{193,129... | collective-permute-start | bytes 393224 | tf_op jit(solution)/shard_map/ppermute | solution.py:258
  6.9 1.7 %fusion = (bf16[1024,512]{1,0:T(8,128)(2,1)S(1)}, bf16[1024,512]{1,0:T(8,128)(2,1)S(1)}) fusion(bf16[1024,1024]{1,0:T(8,128)(2,1)} %key_weight.1), kind=kLoop, calls=%fused_computation | loop fusion | bytes 4194304 | tf_op jit(solution)/shard_map/slice | solution.py:266
  8.6 0.6 own_kernel.1
  9.2 0.4 copy-done.2
  9.6 0.7 copy-done.1
  10.3 2.4 %forward_kernel.1 = (f32[2,128,128]{2,1,0:T(8,128)S(1)}, bf16[384,256]{1,0:T(8,128)(2,1)S(1)}, bf16[2,128,1024]{2,1,0:T(8,128)(2,1)S(1)}, f32[2,128,128]{2,1,0:T...) custom-call(bf16[2,128,1024]{2,1,0:T(8,128)(2,1)S(1)} %copy-done.2, ...), custom_call_target="tpu_custom_call" | custom-call | flops 100000000 | bytes 4000000 | tf_op jit(solution)/shard_map/forward_kernel/pallas_call | solution.py:236
  12.8 10.6 %all-gather = bf16[1536,256]{1,0:T(8,128)(2,1)S(1)} all-gather(bf16[384,256]{1,0:T(8,128)(2,1)S(1)} %get-tuple-element.23), channel_id=2, replica_groups=mesh['ens'=4,'z'=8,'x'=4,'y'=2] {'ens'}, dimensions={0}, use_global_device_ids=true | all-gather | bytes 983040 | tf_op jit(solution)/shard_map/all_gather | solution.py:286
  23.4 4.6 %backward_kernel.1 = (bf16[4,128,512]{2,1,0:T(8,128)(2,1)S(1)}, bf16[128,512]{1,0:T(8,128)(2,1)S(1)}, bf16[128,512]{1,0:T(8,128)(2,1)S(1)}, bf16[128,512]{1,0:T(8,128)(2,1)S(1)}, bf16[1024,128]{1,0:T(8,128)(2,1)S(1)}) custom-call(s32[1]{0:T(128)} %bitcast.me, bf16[2,128,1024]{2,1,0:T(8,128)(2,1)S(1)} %copy-done.2, bf16[128,1024]{1,0:T(8,128)(2,1)S(1)} %pad.4.out_weight, ...), custom_call_target="tpu_custom_call" | custom-call | flops 100000000 | bytes 4000000 | tf_op jit(solution)/shard_map/backward_kernel/pallas_call | solution.py:236
  28.0 0.2 collective-permute-start.1
  28.2 1.4 %collective-permute-start.2 = (bf16[128,512]{1,0:T(8,128)(2,1)S(1)}, bf16[128,512]{1,0:T(8,128)(2,1)S(1)}, u32[]{:S(2)}, u32[]{:S(2)}) collective-permute-start(bf16[128,512]{1,0:T(8,128)(2,1)S(1)} %get-tuple-element.31), channel_id=1, source_target_pairs={{0,128},{64,192},{128,0},{192,64},{1,129},{65,193},{129,1},{193,65... | collective-permute-start | bytes 393224 | tf_op jit(solution)/shard_map/ppermute | solution.py:258
  29.7 2.1 %collective-permute-start.3 = (bf16[128,512]{1,0:T(8,128)(2,1)S(1)}, bf16[128,512]{1,0:T(8,128)(2,1)S(1)}, u32[]{:S(2)}, u32[]{:S(2)}) collective-permute-start(bf16[128,512]{1,0:T(8,128)(2,1)S(1)} %get-tuple-element.32), channel_id=1, source_target_pairs={{0,192},{64,128},{128,64},{192,0},{1,193},{65,129},{129,65},{193,1... | collective-permute-start | bytes 393224 | tf_op jit(solution)/shard_map/ppermute | solution.py:258
  31.7 1.5 %latent_kernel.1 = (f32[64,1024]{1,0:T(8,128)S(1)}, bf16[64,1024]{1,0:T(8,128)(2,1)S(1)}) custom-call(bf16[4,128,512]{2,1,0:T(8,128)(2,1)S(1)} %get-tuple-element.29.halves, bf16[1024,1024]{1,0:T(8,128)(2,1)S(1)} %copy-done, bf16[1024,1024]{1,0:T(8,128)(2,1)S(1)} %copy-done.1), custom_call_target="tpu_custom_call" | custom-call | flops 100000000 | bytes 4000000 | tf_op jit(solution)/shard_map/latent_kernel/pallas_call | solution.py:236
  33.3 1.2 %collective-permute-done.2.last2 = bf16[128,512]{1,0:T(8,128)(2,1)S(1)} collective-permute-done((bf16[128,512]{1,0:T(8,128)(2,1)S(1)}, bf16[128,512]{1,0:T(8,128)(2,1)S(1)}, u32[]{:S(2)}, u32[]{:S(2)}) %collective-permute-start.2) | collective-permute-done | bytes 131104 | tf_op jit(solution)/shard_map/ppermute | solution.py:258
  34.5 3.3 %collective-permute-done.3.last3 = bf16[128,512]{1,0:T(8,128)(2,1)S(1)} collective-permute-done((bf16[128,512]{1,0:T(8,128)(2,1)S(1)}, bf16[128,512]{1,0:T(8,128)(2,1)S(1)}, u32[]{:S(2)}, u32[]{:S(2)}) %collective-permute-start.3) | collective-permute-done | bytes 131104 | tf_op jit(solution)/shard_map/ppermute | solution.py:258
  37.8 0.8 weight_kernel.1
  38.6 23.7 %all_to_all.10.parts = bf16[8,128,640]{2,1,0:T(8,128)(2,1)S(1)} all-to-all(bf16[8,128,640]{2,1,0:T(8,128)(2,1)S(1)} %weight_kernel.1), channel_id=1, replica_groups=mesh['ens'=4,'z'=8,'x'=4,'y'=2] {'x','y'}, dimensions={0} | all-to-all | bytes 2621440 | tf_op jit(solution)/shard_map/all_to_all | solution.py:311
  62.2 0.8 sum_kernel.2
  63.1 8.9 %all-to-all-start.1 = ((bf16[8,16,640]{2,1,0:T(8,128)(2,1)}), bf16[8,16,640]{2,1,0:T(8,128)(2,1)S(1)}, u32[]{:S(2)}, u32[]{:S(2)}) async-start(bf16[8,16,640]{2,1,0:T(8,128)(2,1)} %bitcast.2), calls=%async_computation.1 | async-start | bytes 327680 | tf_op jit(solution)/shard_map/all_to_all | solution.py:313
  71.9 3.1 %collective-permute-start.7 = (bf16[64,1024]{1,0:T(8,128)(2,1)S(1)}, bf16[64,1024]{1,0:T(8,128)(2,1)S(1)}, u32[]{:S(2)}, u32[]{:S(2)}) collective-permute-start(bf16[64,1024]{1,0:T(8,128)(2,1)S(1)} %get-tuple-element.34.upper), channel_id=1, source_target_pairs={{0,1},{1,2},{2,3},{3,4},{4,5},{5,6},{6,7},{7,8},{8,9},{9,10},{10,1... | collective-permute-start | bytes 393224 | tf_op jit(solution)/shard_map/ppermute | solution.py:254
  75.0 5.1 %all-to-all-done.1.parts = bf16[8,16,640]{2,1,0:T(8,128)(2,1)S(1)} async-done(((bf16[8,16,640]{2,1,0:T(8,128)(2,1)}), bf16[8,16,640]{2,1,0:T(8,128)(2,1)S(1)}, u32[]{:S(2)}, u32[]{:S(2)}) %all-to-all-start.1) | async-done | bytes 163872 | tf_op jit(solution)/shard_map/all_to_all | solution.py:313
  80.1 9.2 %all-gather.1 = bf16[64,640]{1,0:T(8,128)(2,1)S(1)} all-gather(bf16[16,640]{1,0:T(8,128)(2,1)S(1)} %sum_kernel.3), channel_id=3, replica_groups=mesh['ens'=4,'z'=8,'x'=4,'y'=2] {'ens'}, dimensions={0}, use_global_device_ids=true | all-gather | bytes 102400 | tf_op jit(solution)/shard_map/all_gather | solution.py:315
  89.3 0.8 finish_kernel.1
  (21 shorter events, 0.1 us)
Async XLA Ops:
  0.6 8.0 %copy-start.3 = (bf16[2,32,1024]{2,1,0:T(8,128)(2,1)S(1)}, bf16[2,32,1024]{2,1,0:T(8,128)(2,1)}, u32[]{:S(2)}) copy-start(bf16[2,32,1024]{2,1,0:T(8,128)(2,1)} %nodes.1) | copy-start | bytes 393220
  0.6 7.9 %copy-start.6 = (bf16[100,1024]{1,0:T(8,128)(2,1)S(1)}, bf16[100,1024]{1,0:T(8,128)(2,1)}, u32[]{:S(2)}) copy-start(bf16[100,1024]{1,0:T(8,128)(2,1)} %param.11) | copy-start | bytes 614404
  0.7 8.0 %copy-start.5 = (s32[2,512]{1,0:T(2,128)S(1)}, s32[2,512]{1,0:T(2,128)}, u32[]{:S(2)}) copy-start(s32[2,512]{1,0:T(2,128)} %edges.1) | copy-start | bytes 12292
  0.7 8.6 %collective-permute-start = (bf16[2,32,1024]{2,1,0:T(8,128)(2,1)}, bf16[2,32,1024]{2,1,0:T(8,128)(2,1)S(1)}, u32[]{:S(2)}, u32[]{:S(2)}) collective-permute-start(bf16[2,32,1024]{2,1,0:T(8,128)(2,1)} %nodes.1), channel_id=1, source_target_pairs={{1,0},{2,1},{3,2},{4,3},{5,4},{6,5},{7,6},{8,7},{9,8},{10,9},{11,1... | collective-permute-start | bytes 393224 | tf_op jit(solution)/shard_map/ppermute | solution.py:254
  2.1 29.6 %collective-permute-start.5 = (bf16[2,32,1024]{2,1,0:T(8,128)(2,1)}, bf16[2,32,1024]{2,1,0:T(8,128)(2,1)S(1)}, u32[]{:S(2)}, u32[]{:S(2)}) collective-permute-start(bf16[2,32,1024]{2,1,0:T(8,128)(2,1)} %nodes.1), channel_id=1, source_target_pairs={{0,128},{64,192},{128,0},{192,64},{1,129},{65,193},{129,1},{193,65... | collective-permute-start | bytes 393224 | tf_op jit(solution)/shard_map/ppermute | solution.py:258
  5.9 27.3 %collective-permute-start.4 = (bf16[2,32,1024]{2,1,0:T(8,128)(2,1)}, bf16[2,32,1024]{2,1,0:T(8,128)(2,1)S(1)}, u32[]{:S(2)}, u32[]{:S(2)}) collective-permute-start(bf16[2,32,1024]{2,1,0:T(8,128)(2,1)} %nodes.1), channel_id=1, source_target_pairs={{0,64},{64,0},{128,192},{192,128},{1,65},{65,1},{129,193},{193,129... | collective-permute-start | bytes 393224 | tf_op jit(solution)/shard_map/ppermute | solution.py:258
  8.6 1.0 %copy-start.2 = (bf16[2,128,1024]{2,1,0:T(8,128)(2,1)S(1)}, bf16[2,128,1024]{2,1,0:T(8,128)(2,1)}, u32[]{:S(2)}) copy-start(bf16[2,128,1024]{2,1,0:T(8,128)(2,1)} %embed.3) | copy-start | bytes 1572868
  8.6 1.8 %copy-start.1 = (bf16[1024,1024]{1,0:T(8,128)(2,1)S(1)}, bf16[1024,1024]{1,0:T(8,128)(2,1)}, u32[]{:S(2)}) copy-start(bf16[1024,1024]{1,0:T(8,128)(2,1)} %value_weight.3) | copy-start | bytes 6291460
  10.3 13.0 %copy-start.4 = (f32[100,128]{1,0:T(8,128)S(1)}, f32[100,128]{1,0:T(8,128)}, u32[]{:S(2)}) copy-start(f32[100,128]{1,0:T(8,128)} %target.1) | copy-start | bytes 153604
  23.4 8.4 %copy-start = (bf16[1024,1024]{1,0:T(8,128)(2,1)S(1)}, bf16[1024,1024]{1,0:T(8,128)(2,1)}, u32[]{:S(2)}) copy-start(bf16[1024,1024]{1,0:T(8,128)(2,1)} %key_weight.1) | copy-start | bytes 6291460
  28.0 5.3 %collective-permute-start.1 = (bf16[128,512]{1,0:T(8,128)(2,1)S(1)}, bf16[128,512]{1,0:T(8,128)(2,1)S(1)}, u32[]{:S(2)}, u32[]{:S(2)}) collective-permute-start(bf16[128,512]{1,0:T(8,128)(2,1)S(1)} %get-tuple-element.30), channel_id=1, source_target_pairs={{0,64},{64,0},{128,192},{192,128},{1,65},{65,1},{129,193},{193,129... | collective-permute-start | bytes 393224 | tf_op jit(solution)/shard_map/ppermute | solution.py:258
  28.2 6.2 %collective-permute-start.2 = (bf16[128,512]{1,0:T(8,128)(2,1)S(1)}, bf16[128,512]{1,0:T(8,128)(2,1)S(1)}, u32[]{:S(2)}, u32[]{:S(2)}) collective-permute-start(bf16[128,512]{1,0:T(8,128)(2,1)S(1)} %get-tuple-element.31), channel_id=1, source_target_pairs={{0,128},{64,192},{128,0},{192,64},{1,129},{65,193},{129,1},{193,65... | collective-permute-start | bytes 393224 | tf_op jit(solution)/shard_map/ppermute | solution.py:258
  29.7 8.1 %collective-permute-start.3 = (bf16[128,512]{1,0:T(8,128)(2,1)S(1)}, bf16[128,512]{1,0:T(8,128)(2,1)S(1)}, u32[]{:S(2)}, u32[]{:S(2)}) collective-permute-start(bf16[128,512]{1,0:T(8,128)(2,1)S(1)} %get-tuple-element.32), channel_id=1, source_target_pairs={{0,192},{64,128},{128,64},{192,0},{1,193},{65,129},{129,65},{193,1... | collective-permute-start | bytes 393224 | tf_op jit(solution)/shard_map/ppermute | solution.py:258
  31.7 6.0 %collective-permute-start.6 = (bf16[2,32,1024]{2,1,0:T(8,128)(2,1)S(1)}, bf16[2,32,1024]{2,1,0:T(8,128)(2,1)S(1)}, u32[]{:S(2)}, u32[]{:S(2)}) collective-permute-start(bf16[2,32,1024]{2,1,0:T(8,128)(2,1)S(1)} %collective-permute-done.5.nodes2), channel_id=1, source_target_pairs={{0,64},{64,0},{128,192},{192,128},{1,65},{65,1},{129,193},{193,129... | collective-permute-start | bytes 393224 | tf_op jit(solution)/shard_map/ppermute | solution.py:258
  63.1 17.0 %all-to-all-start.1 = ((bf16[8,16,640]{2,1,0:T(8,128)(2,1)}), bf16[8,16,640]{2,1,0:T(8,128)(2,1)S(1)}, u32[]{:S(2)}, u32[]{:S(2)}) async-start(bf16[8,16,640]{2,1,0:T(8,128)(2,1)} %bitcast.2), calls=%async_computation.1 | async-start | bytes 327680 | tf_op jit(solution)/shard_map/all_to_all | solution.py:313
  71.9 17.4 %collective-permute-start.7 = (bf16[64,1024]{1,0:T(8,128)(2,1)S(1)}, bf16[64,1024]{1,0:T(8,128)(2,1)S(1)}, u32[]{:S(2)}, u32[]{:S(2)}) collective-permute-start(bf16[64,1024]{1,0:T(8,128)(2,1)S(1)} %get-tuple-element.34.upper), channel_id=1, source_target_pairs={{0,1},{1,2},{2,3},{3,4},{4,5},{5,6},{6,7},{7,8},{8,9},{9,10},{10,1... | collective-permute-start | bytes 393224 | tf_op jit(solution)/shard_map/ppermute | solution.py:254

commit v6 on v5

--- a/solution.py
+++ b/solution.py
@@ -52,6 +52,16 @@
     return jnp.where(same, jnp.concatenate([rows] * 4, axis=0), jnp.zeros((), LOW))
 
 
+def head_sums(values):
+    heads = values.reshape(GROUP // WINDOW, WINDOW, GRID_DEV)
+    return heads, jnp.sum(heads, axis=1, keepdims=True)
+
+
+def shares_of(exp):
+    heads, totals = head_sums(exp.astype(F32))
+    return (heads * (1.0 / totals)).reshape(GROUP, GRID_DEV)
+
+
 def from_head(blocks):
     head = lax.broadcasted_iota(jnp.int32, (WINDOW, GROUP), 1) // HEAD_DIM
     total = blocks[:WINDOW]
@@ -71,7 +81,7 @@
     into = (lax.broadcasted_iota(jnp.int32, (GRID_DEV, slots), 0) == local).astype(F32).astype(LOW)
     node = lax.broadcasted_iota(jnp.int32, (GROUP, slots), 0) & (WINDOW - 1)
     out_of = (node == source).astype(F32).astype(LOW)
-    count[...] = dot(into, out_of, 1, 1)
+    count[...] = dot(out_of, into, 1, 1)
 
 
 def forward_kernel(
@@ -91,7 +101,9 @@
             keys[m * WINDOW + LAT_DEV : (m + 1) * WINDOW, cols] = upper_rows[part]
     count = edge_count[...]
     same = same_head()
-    ones = same.astype(F32).astype(LOW)
+    rows = lax.broadcasted_iota(jnp.int32, (GRID_DEV, GRID_DEV), 0)
+    cols = lax.broadcasted_iota(jnp.int32, (GRID_DEV, GRID_DEV), 1)
+    identity = (rows == cols).astype(F32).astype(LOW)
     for m in range(HELD):
         square = jnp.zeros((GRID_DEV, 1), F32)
         for j in range(GROUPS):
@@ -101,11 +113,12 @@
             query = embed[m, :, cols]
             key = by_head(keys[m * WINDOW : (m + 1) * WINDOW, cols], same)
             value = by_head(values[m * WINDOW : (m + 1) * WINDOW, cols], same)
-            bent = jnp.tanh(dot(query, key, 1, 1) * (HEAD_DIM**-0.5 / CAP))
+            bent = jnp.tanh(dot(key, query, 1, 1) * (HEAD_DIM**-0.5 / CAP))
             exp = (count * jnp.exp(CAP * bent)).astype(LOW)
-            exps[m, :, cols] = exp
-            damps[m, :, cols] = ((1.0 - bent * bent) * HEAD_DIM**-0.5).astype(LOW)
-            attended = dot(exp, value, 1, 0) / dot(exp, ones, 1, 0)
+            exps[m, j] = exp
+            damps[m, j] = ((1.0 - bent * bent) * HEAD_DIM**-0.5).astype(LOW)
+            turned = dot(identity, shares_of(exp).astype(LOW), 1, 1).astype(LOW)
+            attended = dot(turned, value, 1, 0)
             sums = query.astype(F32) + attended
             mixed[:, cols] = sums
             square = square + jnp.sum(sums * sums, axis=1, keepdims=True)
@@ -126,7 +139,6 @@
     truth[...] = jnp.zeros((VARS_PAD, GRID_DEV), F32)
     truth[:VARS, :] = target[...]
     same = same_head()
-    ones = same.astype(F32).astype(LOW)
     pred_grads = []
     for m in range(HELD):
         pred = preds[m]
@@ -145,9 +157,10 @@
     out_grad[...] = jnp.transpose(dot(both, lows, 1, 0)).astype(LOW)
     for m in range(HELD):
         slant = jnp.zeros((GRID_DEV, 1), F32)
+        turned = jnp.transpose(pred_grads[m].astype(F32)).astype(LOW)
         for j in range(GROUPS):
             cols = slice(j * GROUP, (j + 1) * GROUP)
-            part = dot(pred_grads[m], out_weight[:, cols], 0, 0)
+            part = dot(turned, out_weight[:, cols], 1, 0)
             grad[:, cols] = part
             slant = slant + jnp.sum(part * normed_low[m, :, cols].astype(F32), axis=1, keepdims=True)
         slant = slant * (1.0 / D)
@@ -156,16 +169,13 @@
             cols = slice(j * GROUP, (j + 1) * GROUP)
             mixed_grad = (inv * (grad[:, cols] - normed_low[m, :, cols].astype(F32) * slant)).astype(LOW)
             value = by_head(values[m * WINDOW : (m + 1) * WINDOW, cols], same)
-            exp = exps[m, :, cols]
-            weight = exp.astype(F32) / dot(exp, ones, 1, 0)
-            weight_grad = dot(mixed_grad, value, 1, 1)
-            term = weight * weight_grad
-            high = term.astype(LOW)
-            rest = (term - high.astype(F32)).astype(LOW)
-            inner = dot(high, ones, 1, 0) + dot(rest, ones, 1, 0)
-            raw_grad = (weight * (weight_grad - inner) * damps[m, :, cols].astype(F32)).astype(LOW)
-            key_part = from_head(dot(raw_grad, embed[m, :, cols], 0, 0))
-            value_part = from_head(dot(weight.astype(LOW), mixed_grad, 0, 0))
+            weight = shares_of(exps[m, j])
+            weight_grad = dot(value, mixed_grad, 1, 1)
+            inner = head_sums(weight * weight_grad)[1]
+            centred = weight_grad.reshape(GROUP // WINDOW, WINDOW, GRID_DEV) - inner
+            raw_grad = weight * centred.reshape(GROUP, GRID_DEV) * damps[m, j].astype(F32)
+            key_part = from_head(dot(raw_grad.astype(LOW), embed[m, :, cols], 1, 0))
+            value_part = from_head(dot(weight.astype(LOW), mixed_grad, 1, 0))
             at = slice(j % 2 * GROUP, (j % 2 + 1) * GROUP)
             for p, part in ((j // 2, key_part), (2 + j // 2, value_part)):
                 start = m * LAT_DEV
@@ -173,7 +183,12 @@
                 start = start + HELD_ROWS
                 halves[p, start : start + LAT_DEV, at] = part[LAT_DEV:].astype(LOW)
     for k, block in ((1, next1), (2, next2), (3, next3)):
-        block[...] = halves[me[0] ^ k]
+        block[: 2 * HELD_ROWS] = halves[me[0] ^ k]
+    for f in range(FAR // 2):
+        start = pl.multiple_of(((me[0] & 1) ^ 1) * (D // 2) + f * NEAR * SHARE, NEAR * SHARE)
+        next1[2 * HELD_ROWS :, f * VARS_PAD : (f + 1) * VARS_PAD] = out_grad[
+            pl.ds(start, NEAR * SHARE), :
+        ]
 
 
 def latent_kernel(halves, key_weight, value_weight, own, upper):
@@ -187,7 +202,9 @@
 def weight_kernel(
     me, halves, last1, last2, last3, nodes, nodes1, nodes2, nodes3, shares, out_grad, upper, send
 ):
-    rows = jnp.concatenate([halves[me[0]], last1[...], last2[...], last3[...]], axis=0)
+    rows = jnp.concatenate(
+        [halves[me[0]], last1[: 2 * HELD_ROWS], last2[...], last3[...]], axis=0
+    )
     for j in range(GROUPS):
         cols = slice(j * GROUP, (j + 1) * GROUP)
         at = slice(j * HELD_ROWS, (j + 1) * HELD_ROWS)
@@ -200,8 +217,26 @@
             r = j * (GROUP // SHARE) + b
             far, near = r // NEAR, r % NEAR
             at = slice(far * SHARE, (far + 1) * SHARE)
-            send[near, at, :COLS] = product[b * SHARE : (b + 1) * SHARE]
-            send[near, at, COLS:] = out_grad[r * SHARE : (r + 1) * SHARE]
+            send[near, at] = product[b * SHARE : (b + 1) * SHARE]
+    for f in range(FAR // 2):
+        start = pl.multiple_of((me[0] & 1) * (D // 2) + f * NEAR * SHARE, NEAR * SHARE)
+        cols = slice(f * VARS_PAD, (f + 1) * VARS_PAD)
+        pair = out_grad[pl.ds(start, NEAR * SHARE), :].astype(F32)
+        pair = (pair + last1[2 * HELD_ROWS :, cols].astype(F32)).astype(LOW)
+        for near in range(NEAR):
+            send[near, FAR * SHARE :, cols] = pair[near * SHARE : (near + 1) * SHARE]
+
+
+def near_sum_kernel(me, parts, total):
+    value = parts[0].astype(F32)
+    for p in range(1, NEAR):
+        value = value + parts[p].astype(F32)
+    for far in range(FAR):
+        total[far, :, :COLS] = value[far * SHARE : (far + 1) * SHARE].astype(LOW)
+        f = far % (FAR // 2)
+        held = jnp.where((me[0] & 1) == far // (FAR // 2), 1.0, 0.0)
+        block = value[FAR * SHARE :, f * VARS_PAD : (f + 1) * VARS_PAD]
+        total[far, :, COLS:] = (block * held).astype(LOW)
 
 
 def sum_kernel(parts, total):
@@ -264,7 +299,7 @@
     nodes1, nodes2 = ens_swap(latent, 1), ens_swap(latent, 2)
     nodes3 = ens_swap(nodes2, 1)
     halves_of_key = (key_weight[:, : D // 2], key_weight[:, D // 2 :])
-    own_keys, count = call(own_kernel, [((HELD_ROWS, D), LOW), ((GRID_DEV, GROUP), F32)])(
+    own_keys, count = call(own_kernel, [((HELD_ROWS, D), LOW), ((GROUP, GRID_DEV), F32)])(
         latent, edges, *halves_of_key
     )
     preds, share, normed_low, inverse, exps, damps, values = call(
@@ -274,8 +309,8 @@
             ((PRED_ROW + VARS_PAD, GROUP), LOW),
             ((HELD, GRID_DEV, D), LOW),
             ((HELD, GRID_DEV, 128), F32),
-            ((HELD, GRID_DEV, D), LOW),
-            ((HELD, GRID_DEV, D), LOW),
+            ((HELD, GROUPS, GROUP, GRID_DEV), LOW),
+            ((HELD, GROUPS, GROUP, GRID_DEV), LOW),
             ((HELD * WINDOW, D), LOW),
         ],
         [((HELD * WINDOW, D), LOW), ((GRID_DEV, D), F32)],
@@ -288,7 +323,9 @@
     scalar = {0: pl.BlockSpec(memory_space=pltpu.SMEM)}
     halves, next1, next2, next3, out_grad = call(
         backward_kernel,
-        [((ENS, *block), LOW)] + [(block, LOW)] * 3 + [((D, VARS_PAD), LOW)],
+        [((ENS, *block), LOW), ((2 * HELD_ROWS + NEAR * SHARE, COLS), LOW)]
+        + [(block, LOW)] * 2
+        + [((D, VARS_PAD), LOW)],
         [((GRID_DEV, D), F32), ((VARS_PAD, GRID_DEV), F32)],
         {**scalar, 5: pl.BlockSpec((ENS, VARS_PAD, GROUP), lambda i: (0, PRED_ROW // VARS_PAD, 0))},
     )(me, grid_embed, out_rows, target, preds, shares, normed_low, inverse, exps, damps, values)
@@ -299,7 +336,7 @@
     lower = band_shift(upper, 1)
     (send,) = call(
         weight_kernel,
-        [((NEAR, FAR * SHARE, COLS + VARS_PAD), LOW)],
+        [((NEAR, (FAR + 1) * SHARE, COLS), LOW)],
         specs={
             **scalar,
             9: pl.BlockSpec((ENS, PRED_ROW, GROUP), lambda i: (0, 0, 0)),
@@ -309,8 +346,8 @@
         me, halves, last1, last2, last3, latent, nodes1, nodes2, nodes3, shares, out_grad, upper
     )
     parts = lax.all_to_all(send, ("x", "y"), 0, 0, tiled=True)
-    (total,) = call(sum_kernel, [((FAR * SHARE, COLS + VARS_PAD), LOW)])(parts)
-    parts = lax.all_to_all(total.reshape(FAR, SHARE, COLS + VARS_PAD), "z", 0, 0, tiled=True)
+    (total,) = call(near_sum_kernel, [((FAR, SHARE, COLS + VARS_PAD), LOW)], specs=scalar)(me, parts)
+    parts = lax.all_to_all(total, "z", 0, 0, tiled=True)
     (total,) = call(sum_kernel, [((SHARE, COLS + VARS_PAD), LOW)])(parts)
     parts = lax.all_gather(total, "ens", axis=0)
     return tuple(

time: 90.4 us -> 87.9 us (0.972)
  starting transfers between devices: 21.9 us -> 20.4 us
  Pallas kernels: 11.5 us -> 10.5 us
    all_to_all x1, blocking collectives: 23.7 us -> 21.9 us  [on_device(): parts = lax.all_to_all(send, ('x', 'y'), 0, 0, tiled=True)]
    pallas_call x8, Pallas kernels: 11.5 us -> 10.5 us  [run(): pl.pallas_call(kernel, grid=(1,), in_specs=[places.get(i, whole(value.sha...]
    all_gather x1, blocking collectives: 10.6 us -> 11.6 us  [on_device(): shares = lax.all_gather(share, 'ens', axis=0)]
  transfers between devices with their start and end apart: 9 -> 9, of which waited for: 3 -> 3; matrix products, arithmetic and copies ran while one was open for 2% -> 2% of each run, Pallas kernels for 10% -> 9%
where the time goes in v6:
time: 87.9 us; the launch traced here: 87.5 us
  blocking collectives  43.1 us (49%)
  starting transfers between devices  20.4 us (23%)
  Pallas kernels  10.5 us (12%)
  waiting for transfers between devices  9.97 us (11%)
  local copies, waits for them, and re-layouts  2.81 us (3%)
    all_to_all x1, blocking collectives, on_device(): parts = lax.all_to_all(send, ('x', 'y'), 0, 0, tiled=True)  21.9 us
    all_gather x1, blocking collectives, on_device(): shares = lax.all_gather(share, 'ens', axis=0)  11.6 us
    pallas_call x8, Pallas kernels, run(): pl.pallas_call(kernel, grid=(1,), in_specs=[places.get(i, whole(value.sha...  10.5 us
    all_gather x1, blocking collectives, on_device(): parts = lax.all_gather(total, 'ens', axis=0)  9.64 us
    all_to_all x1, starting transfers between devices, on_device(): parts = lax.all_to_all(total, 'z', 0, 0, tiled=True)  8.18 us
    ppermute x6, starting transfers between devices, ens_swap(): return lax.ppermute(value, 'ens', [(e, e ^ k) for e in range(ENS)])  7.79 us
    all_to_all x1, waiting for transfers between devices, on_device(): parts = lax.all_to_all(total, 'z', 0, 0, tiled=True)  5.3 us
    ppermute x6, waiting for transfers between devices, ens_swap(): return lax.ppermute(value, 'ens', [(e, e ^ k) for e in range(ENS)])  4.67 us
  transfers between devices with their start and end apart: 9, of which 3 were waited for; matrix products, arithmetic and copies ran while one was open for 2% of the time, Pallas kernels for 9%

profile of v6, /device:TPU:1, one launch (start us, length us, event | category | flops | bytes accessed | tf_op | source)
XLA Modules:
  0.0 87.5 jit_solution(5150747346020699203)
XLA Ops:
  0.7 1.4 %collective-permute-start = (bf16[2,32,1024]{2,1,0:T(8,128)(2,1)}, bf16[2,32,1024]{2,1,0:T(8,128)(2,1)S(1)}, u32[]{:S(2)}, u32[]{:S(2)}) collective-permute-start(bf16[2,32,1024]{2,1,0:T(8,128)(2,1)} %nodes.1), channel_id=1, source_target_pairs={{1,0},{2,1},{3,2},{4,3},{5,4},{6,5},{7,6},{8,7},{9,8},{10,9},{11,1... | collective-permute-start | bytes 393224 | tf_op jit(solution)/shard_map/ppermute | solution.py:289
  2.1 3.8 %collective-permute-start.5 = (bf16[2,32,1024]{2,1,0:T(8,128)(2,1)}, bf16[2,32,1024]{2,1,0:T(8,128)(2,1)S(1)}, u32[]{:S(2)}, u32[]{:S(2)}) collective-permute-start(bf16[2,32,1024]{2,1,0:T(8,128)(2,1)} %nodes.1), channel_id=1, source_target_pairs={{0,128},{64,192},{128,0},{192,64},{1,129},{65,193},{129,1},{193,65... | collective-permute-start | bytes 393224 | tf_op jit(solution)/shard_map/ppermute | solution.py:293
  5.9 1.7 %fusion = (bf16[1024,512]{1,0:T(8,128)(2,1)S(1)}, bf16[1024,512]{1,0:T(8,128)(2,1)S(1)}) fusion(bf16[1024,1024]{1,0:T(8,128)(2,1)} %key_weight.1), kind=kLoop, calls=%fused_computation | loop fusion | bytes 4194304 | tf_op jit(solution)/shard_map/slice | solution.py:301
  7.7 0.6 own_kernel.1
  8.3 0.4 copy-done.2
  8.6 0.7 copy-done.1
  9.4 3.1 %forward_kernel.1 = (f32[2,128,128]{2,1,0:T(8,128)S(1)}, bf16[384,256]{1,0:T(8,128)(2,1)S(1)}, bf16[2,128,1024]{2,1,0:T(8,128)(2,1)S(1)}, f32[2,128,128]{2,1,0:T...) custom-call(bf16[2,128,1024]{2,1,0:T(8,128)(2,1)S(1)} %copy-done.2, ...), custom_call_target="tpu_custom_call" | custom-call | flops 100000000 | bytes 4000000 | tf_op jit(solution)/shard_map/forward_kernel/pallas_call | solution.py:271
  12.5 11.6 %all-gather = bf16[1536,256]{1,0:T(8,128)(2,1)S(1)} all-gather(bf16[384,256]{1,0:T(8,128)(2,1)S(1)} %get-tuple-element.23), channel_id=2, replica_groups=mesh['ens'=4,'z'=8,'x'=4,'y'=2] {'ens'}, dimensions={0}, use_global_device_ids=true | all-gather | bytes 983040 | tf_op jit(solution)/shard_map/all_gather | solution.py:321
  24.1 2.9 %backward_kernel.1 = (bf16[4,128,512]{2,1,0:T(8,128)(2,1)S(1)}, bf16[256,512]{1,0:T(8,128)(2,1)S(1)}, bf16[128,512]{1,0:T(8,128)(2,1)S(1)}, bf16[128,512]{1,0:T(8,128)(2,1)S(1)}, bf16[1024,128]{1,0:T(8,128)(2,1)S(1)}) custom-call(s32[1]{0:T(128)} %bitcast.me, bf16[2,128,1024]{2,1,0:T(8,128)(2,1)S(1)} %copy-done.2, bf16[128,1024]{1,0:T(8,128)(2,1)S(1)} %pad.4.out_weight, ...), custom_call_target="tpu_custom_call" | custom-call | flops 100000000 | bytes 4000000 | tf_op jit(solution)/shard_map/backward_kernel/pallas_call | solution.py:271
  27.0 0.2 collective-permute-start.1
  27.2 0.3 collective-permute-start.4
  27.6 1.4 %collective-permute-start.2 = (bf16[128,512]{1,0:T(8,128)(2,1)S(1)}, bf16[128,512]{1,0:T(8,128)(2,1)S(1)}, u32[]{:S(2)}, u32[]{:S(2)}) collective-permute-start(bf16[128,512]{1,0:T(8,128)(2,1)S(1)} %get-tuple-element.31), channel_id=1, source_target_pairs={{0,128},{64,192},{128,0},{192,64},{1,129},{65,193},{129,1},{193,65... | collective-permute-start | bytes 393224 | tf_op jit(solution)/shard_map/ppermute | solution.py:293
  28.9 1.9 %collective-permute-start.3 = (bf16[128,512]{1,0:T(8,128)(2,1)S(1)}, bf16[128,512]{1,0:T(8,128)(2,1)S(1)}, u32[]{:S(2)}, u32[]{:S(2)}) collective-permute-start(bf16[128,512]{1,0:T(8,128)(2,1)S(1)} %get-tuple-element.32), channel_id=1, source_target_pairs={{0,192},{64,128},{128,64},{192,0},{1,193},{65,129},{129,65},{193,1... | collective-permute-start | bytes 393224 | tf_op jit(solution)/shard_map/ppermute | solution.py:293
  30.9 1.5 %latent_kernel.1 = (f32[64,1024]{1,0:T(8,128)S(1)}, bf16[64,1024]{1,0:T(8,128)(2,1)S(1)}) custom-call(bf16[4,128,512]{2,1,0:T(8,128)(2,1)S(1)} %get-tuple-element.29.halves, bf16[1024,1024]{1,0:T(8,128)(2,1)S(1)} %copy-done, bf16[1024,1024]{1,0:T(8,128)(2,1)S(1)} %copy-done.1), custom_call_target="tpu_custom_call" | custom-call | flops 100000000 | bytes 4000000 | tf_op jit(solution)/shard_map/latent_kernel/pallas_call | solution.py:271
  32.4 1.6 %collective-permute-done.2.last2 = bf16[128,512]{1,0:T(8,128)(2,1)S(1)} collective-permute-done((bf16[128,512]{1,0:T(8,128)(2,1)S(1)}, bf16[128,512]{1,0:T(8,128)(2,1)S(1)}, u32[]{:S(2)}, u32[]{:S(2)}) %collective-permute-start.2) | collective-permute-done | bytes 131104 | tf_op jit(solution)/shard_map/ppermute | solution.py:293
  34.0 3.1 %collective-permute-done.3.last3 = bf16[128,512]{1,0:T(8,128)(2,1)S(1)} collective-permute-done((bf16[128,512]{1,0:T(8,128)(2,1)S(1)}, bf16[128,512]{1,0:T(8,128)(2,1)S(1)}, u32[]{:S(2)}, u32[]{:S(2)}) %collective-permute-start.3) | collective-permute-done | bytes 131104 | tf_op jit(solution)/shard_map/ppermute | solution.py:293
  37.1 0.8 weight_kernel.1
  37.9 21.9 %all_to_all.10.parts = bf16[8,144,512]{2,1,0:T(8,128)(2,1)S(1)} all-to-all(bf16[8,144,512]{2,1,0:T(8,128)(2,1)S(1)} %weight_kernel.1), channel_id=1, replica_groups=mesh['ens'=4,'z'=8,'x'=4,'y'=2] {'x','y'}, dimensions={0} | all-to-all | bytes 2359296 | tf_op jit(solution)/shard_map/all_to_all | solution.py:348
  59.8 0.8 near_sum_kernel.1
  60.6 8.2 %all-to-all-start.1 = ((bf16[8,16,640]{2,1,0:T(8,128)(2,1)}), bf16[8,16,640]{2,1,0:T(8,128)(2,1)S(1)}, u32[]{:S(2)}, u32[]{:S(2)}) async-start(bf16[8,16,640]{2,1,0:T(8,128)(2,1)} %near_sum_kernel.1), calls=%async_computation.1 | async-start | bytes 327680 | tf_op jit(solution)/shard_map/all_to_all | solution.py:350
  68.8 3.0 %collective-permute-start.7 = (bf16[64,1024]{1,0:T(8,128)(2,1)S(1)}, bf16[64,1024]{1,0:T(8,128)(2,1)S(1)}, u32[]{:S(2)}, u32[]{:S(2)}) collective-permute-start(bf16[64,1024]{1,0:T(8,128)(2,1)S(1)} %get-tuple-element.34.upper), channel_id=1, source_target_pairs={{0,1},{1,2},{2,3},{3,4},{4,5},{5,6},{6,7},{7,8},{8,9},{9,10},{10,1... | collective-permute-start | bytes 393224 | tf_op jit(solution)/shard_map/ppermute | solution.py:289
  71.8 5.3 %all-to-all-done.1.parts = bf16[8,16,640]{2,1,0:T(8,128)(2,1)S(1)} async-done(((bf16[8,16,640]{2,1,0:T(8,128)(2,1)}), bf16[8,16,640]{2,1,0:T(8,128)(2,1)S(1)}, u32[]{:S(2)}, u32[]{:S(2)}) %all-to-all-start.1) | async-done | bytes 163872 | tf_op jit(solution)/shard_map/all_to_all | solution.py:350
  77.1 9.6 %all-gather.1 = bf16[64,640]{1,0:T(8,128)(2,1)S(1)} all-gather(bf16[16,640]{1,0:T(8,128)(2,1)S(1)} %sum_kernel.1), channel_id=3, replica_groups=mesh['ens'=4,'z'=8,'x'=4,'y'=2] {'ens'}, dimensions={0}, use_global_device_ids=true | all-gather | bytes 102400 | tf_op jit(solution)/shard_map/all_gather | solution.py:352
  86.8 0.8 finish_kernel.1
  (21 shorter events, 0.2 us)
Async XLA Ops:
  0.6 7.0 %copy-start.3 = (bf16[2,32,1024]{2,1,0:T(8,128)(2,1)S(1)}, bf16[2,32,1024]{2,1,0:T(8,128)(2,1)}, u32[]{:S(2)}) copy-start(bf16[2,32,1024]{2,1,0:T(8,128)(2,1)} %nodes.1) | copy-start | bytes 393220
  0.6 7.0 %copy-start.6 = (bf16[100,1024]{1,0:T(8,128)(2,1)S(1)}, bf16[100,1024]{1,0:T(8,128)(2,1)}, u32[]{:S(2)}) copy-start(bf16[100,1024]{1,0:T(8,128)(2,1)} %param.11) | copy-start | bytes 614404
  0.7 7.0 %copy-start.5 = (s32[2,512]{1,0:T(2,128)S(1)}, s32[2,512]{1,0:T(2,128)}, u32[]{:S(2)}) copy-start(s32[2,512]{1,0:T(2,128)} %edges.1) | copy-start | bytes 12292
  0.7 7.6 %collective-permute-start = (bf16[2,32,1024]{2,1,0:T(8,128)(2,1)}, bf16[2,32,1024]{2,1,0:T(8,128)(2,1)S(1)}, u32[]{:S(2)}, u32[]{:S(2)}) collective-permute-start(bf16[2,32,1024]{2,1,0:T(8,128)(2,1)} %nodes.1), channel_id=1, source_target_pairs={{1,0},{2,1},{3,2},{4,3},{5,4},{6,5},{7,6},{8,7},{9,8},{10,9},{11,1... | collective-permute-start | bytes 393224 | tf_op jit(solution)/shard_map/ppermute | solution.py:289
  2.1 28.8 %collective-permute-start.5 = (bf16[2,32,1024]{2,1,0:T(8,128)(2,1)}, bf16[2,32,1024]{2,1,0:T(8,128)(2,1)S(1)}, u32[]{:S(2)}, u32[]{:S(2)}) collective-permute-start(bf16[2,32,1024]{2,1,0:T(8,128)(2,1)} %nodes.1), channel_id=1, source_target_pairs={{0,128},{64,192},{128,0},{192,64},{1,129},{65,193},{129,1},{193,65... | collective-permute-start | bytes 393224 | tf_op jit(solution)/shard_map/ppermute | solution.py:293
  7.6 1.0 %copy-start.2 = (bf16[2,128,1024]{2,1,0:T(8,128)(2,1)S(1)}, bf16[2,128,1024]{2,1,0:T(8,128)(2,1)}, u32[]{:S(2)}) copy-start(bf16[2,128,1024]{2,1,0:T(8,128)(2,1)} %embed.3) | copy-start | bytes 1572868
  7.6 1.8 %copy-start.1 = (bf16[1024,1024]{1,0:T(8,128)(2,1)S(1)}, bf16[1024,1024]{1,0:T(8,128)(2,1)}, u32[]{:S(2)}) copy-start(bf16[1024,1024]{1,0:T(8,128)(2,1)} %value_weight.3) | copy-start | bytes 6291460
  9.4 14.7 %copy-start.4 = (f32[100,128]{1,0:T(8,128)S(1)}, f32[100,128]{1,0:T(8,128)}, u32[]{:S(2)}) copy-start(f32[100,128]{1,0:T(8,128)} %target.1) | copy-start | bytes 153604
  24.0 6.9 %copy-start = (bf16[1024,1024]{1,0:T(8,128)(2,1)S(1)}, bf16[1024,1024]{1,0:T(8,128)(2,1)}, u32[]{:S(2)}) copy-start(bf16[1024,1024]{1,0:T(8,128)(2,1)} %key_weight.1) | copy-start | bytes 6291460
  27.0 10.1 %collective-permute-start.1 = (bf16[256,512]{1,0:T(8,128)(2,1)S(1)}, bf16[256,512]{1,0:T(8,128)(2,1)S(1)}, u32[]{:S(2)}, u32[]{:S(2)}) collective-permute-start(bf16[256,512]{1,0:T(8,128)(2,1)S(1)} %get-tuple-element.30), channel_id=1, source_target_pairs={{0,64},{64,0},{128,192},{192,128},{1,65},{65,1},{129,193},{193,129... | collective-permute-start | bytes 786440 | tf_op jit(solution)/shard_map/ppermute | solution.py:293
  27.2 5.2 %collective-permute-start.4 = (bf16[2,32,1024]{2,1,0:T(8,128)(2,1)S(1)}, bf16[2,32,1024]{2,1,0:T(8,128)(2,1)S(1)}, u32[]{:S(2)}, u32[]{:S(2)}) collective-permute-start(bf16[2,32,1024]{2,1,0:T(8,128)(2,1)S(1)} %copy-done.3), channel_id=1, source_target_pairs={{0,64},{64,0},{128,192},{192,128},{1,65},{65,1},{129,193},{193,129... | collective-permute-start | bytes 393224 | tf_op jit(solution)/shard_map/ppermute | solution.py:293
  27.6 6.5 %collective-permute-start.2 = (bf16[128,512]{1,0:T(8,128)(2,1)S(1)}, bf16[128,512]{1,0:T(8,128)(2,1)S(1)}, u32[]{:S(2)}, u32[]{:S(2)}) collective-permute-start(bf16[128,512]{1,0:T(8,128)(2,1)S(1)} %get-tuple-element.31), channel_id=1, source_target_pairs={{0,128},{64,192},{128,0},{192,64},{1,129},{65,193},{129,1},{193,65... | collective-permute-start | bytes 393224 | tf_op jit(solution)/shard_map/ppermute | solution.py:293
  28.9 8.2 %collective-permute-start.3 = (bf16[128,512]{1,0:T(8,128)(2,1)S(1)}, bf16[128,512]{1,0:T(8,128)(2,1)S(1)}, u32[]{:S(2)}, u32[]{:S(2)}) collective-permute-start(bf16[128,512]{1,0:T(8,128)(2,1)S(1)} %get-tuple-element.32), channel_id=1, source_target_pairs={{0,192},{64,128},{128,64},{192,0},{1,193},{65,129},{129,65},{193,1... | collective-permute-start | bytes 393224 | tf_op jit(solution)/shard_map/ppermute | solution.py:293
  30.9 6.2 %collective-permute-start.6 = (bf16[2,32,1024]{2,1,0:T(8,128)(2,1)S(1)}, bf16[2,32,1024]{2,1,0:T(8,128)(2,1)S(1)}, u32[]{:S(2)}, u32[]{:S(2)}) collective-permute-start(bf16[2,32,1024]{2,1,0:T(8,128)(2,1)S(1)} %collective-permute-done.5.nodes2), channel_id=1, source_target_pairs={{0,64},{64,0},{128,192},{192,128},{1,65},{65,1},{129,193},{193,129... | collective-permute-start | bytes 393224 | tf_op jit(solution)/shard_map/ppermute | solution.py:293
  60.6 16.5 %all-to-all-start.1 = ((bf16[8,16,640]{2,1,0:T(8,128)(2,1)}), bf16[8,16,640]{2,1,0:T(8,128)(2,1)S(1)}, u32[]{:S(2)}, u32[]{:S(2)}) async-start(bf16[8,16,640]{2,1,0:T(8,128)(2,1)} %near_sum_kernel.1), calls=%async_computation.1 | async-start | bytes 327680 | tf_op jit(solution)/shard_map/all_to_all | solution.py:350
  68.8 18.0 %collective-permute-start.7 = (bf16[64,1024]{1,0:T(8,128)(2,1)S(1)}, bf16[64,1024]{1,0:T(8,128)(2,1)S(1)}, u32[]{:S(2)}, u32[]{:S(2)}) collective-permute-start(bf16[64,1024]{1,0:T(8,128)(2,1)S(1)} %get-tuple-element.34.upper), channel_id=1, source_target_pairs={{0,1},{1,2},{2,3},{3,4},{4,5},{5,6},{6,7},{7,8},{8,9},{9,10},{10,1... | collective-permute-start | bytes 393224 | tf_op jit(solution)/shard_map/ppermute | solution.py:289

commit v7 on v6

--- a/solution.py
+++ b/solution.py
@@ -24,6 +24,8 @@
 BAND = ("z", "x", "y")
 ENS = 4
 NEAR = 8
+STEPS = ((2, 0), (2, 1), (0, 1), (1, 1), (3, 0), (1, 0), (3, 1))
+PATHS = ((1, 0), (3, 0), (0, 1), (1, 1), (3, 0), (1, 0), (3, 1))
 FAR = 8
 SHARE = 16
 COLS = 2 * D // ENS
@@ -183,7 +185,7 @@
                 start = start + HELD_ROWS
                 halves[p, start : start + LAT_DEV, at] = part[LAT_DEV:].astype(LOW)
     for k, block in ((1, next1), (2, next2), (3, next3)):
-        block[: 2 * HELD_ROWS] = halves[me[0] ^ k]
+        block[: 2 * HELD_ROWS] = halves[(me[0] & (ENS - 1)) ^ k]
     for f in range(FAR // 2):
         start = pl.multiple_of(((me[0] & 1) ^ 1) * (D // 2) + f * NEAR * SHARE, NEAR * SHARE)
         next1[2 * HELD_ROWS :, f * VARS_PAD : (f + 1) * VARS_PAD] = out_grad[
@@ -200,37 +202,44 @@
 
 
 def weight_kernel(
-    me, halves, last1, last2, last3, nodes, nodes1, nodes2, nodes3, shares, out_grad, upper, send
+    me, halves, last1, last2, last3, nodes, nodes1, nodes2, nodes3, shares, out_grad,
+    upper, keep, *refs,
 ):
+    sends, product, pair = refs[: NEAR - 1], refs[-2], refs[-1]
     rows = jnp.concatenate(
-        [halves[me[0]], last1[: 2 * HELD_ROWS], last2[...], last3[...]], axis=0
+        [halves[me[0] & (ENS - 1)], last1[: 2 * HELD_ROWS], last2[...], last3[...]], axis=0
     )
     for j in range(GROUPS):
         cols = slice(j * GROUP, (j + 1) * GROUP)
         at = slice(j * HELD_ROWS, (j + 1) * HELD_ROWS)
         left = []
         for k, block in enumerate((nodes, nodes1, nodes2, nodes3)):
-            left += [block[0, :, cols], block[1, :, cols], shares[me[0] ^ k, at]]
+            left += [block[0, :, cols], block[1, :, cols], shares[(me[0] & (ENS - 1)) ^ k, at]]
         left = jnp.concatenate(left, axis=0)
-        product = dot(left, rows, 0, 0).astype(LOW)
-        for b in range(GROUP // SHARE):
-            r = j * (GROUP // SHARE) + b
-            far, near = r // NEAR, r % NEAR
-            at = slice(far * SHARE, (far + 1) * SHARE)
-            send[near, at] = product[b * SHARE : (b + 1) * SHARE]
+        product[cols, :] = dot(left, rows, 0, 0).astype(LOW)
     for f in range(FAR // 2):
         start = pl.multiple_of((me[0] & 1) * (D // 2) + f * NEAR * SHARE, NEAR * SHARE)
-        cols = slice(f * VARS_PAD, (f + 1) * VARS_PAD)
-        pair = out_grad[pl.ds(start, NEAR * SHARE), :].astype(F32)
-        pair = (pair + last1[2 * HELD_ROWS :, cols].astype(F32)).astype(LOW)
-        for near in range(NEAR):
-            send[near, FAR * SHARE :, cols] = pair[near * SHARE : (near + 1) * SHARE]
-
-
-def near_sum_kernel(me, parts, total):
-    value = parts[0].astype(F32)
-    for p in range(1, NEAR):
-        value = value + parts[p].astype(F32)
+        lanes = slice(f * VARS_PAD, (f + 1) * VARS_PAD)
+        own = out_grad[pl.ds(start, NEAR * SHARE), :].astype(F32)
+        pair[:, lanes] = (own + last1[2 * HELD_ROWS :, lanes].astype(F32)).astype(LOW)
+    for (dx, dy), send in zip(((0, 0), *STEPS), (keep, *sends)):
+        near = (((me[0] >> 3) + dx) & 3) * 2 + (((me[0] >> 2) + dy) & 1)
+        for far in range(FAR):
+            start = pl.multiple_of((far * NEAR + near) * SHARE, SHARE)
+            send[far * SHARE : (far + 1) * SHARE] = product[pl.ds(start, SHARE), :]
+        start = pl.multiple_of(near * SHARE, SHARE)
+        send[FAR * SHARE :] = pair[pl.ds(start, SHARE), :]
+
+
+def relay_kernel(up, down, held6, held7, send6, send7):
+    send6[...] = (held6[...].astype(F32) + up[...].astype(F32)).astype(LOW)
+    send7[...] = (held7[...].astype(F32) + down[...].astype(F32)).astype(LOW)
+
+
+def near_sum_kernel(me, first, *refs):
+    value, total = first[...].astype(F32), refs[-1]
+    for part in refs[:-1]:
+        value = value + part[...].astype(F32)
     for far in range(FAR):
         total[far, :, :COLS] = value[far * SHARE : (far + 1) * SHARE].astype(LOW)
         f = far % (FAR // 2)
@@ -293,6 +302,11 @@
     return lax.ppermute(value, "ens", [(e, e ^ k) for e in range(ENS)])
 
 
+def near_shift(value, dx, dy):
+    pairs = [(x * 2 + y, (x + dx) % 4 * 2 + (y + dy) % 2) for x in range(4) for y in range(2)]
+    return lax.ppermute(value, ("x", "y"), pairs)
+
+
 def on_device(grid_embed, latent, key_weight, value_weight, out_weight, target, edges):
     out_rows = jnp.pad(out_weight, ((0, VARS_PAD - VARS), (0, 0)))
     upper_latent = band_shift(latent, -1)
@@ -317,7 +331,8 @@
     )(
         grid_embed, latent, upper_latent, *halves_of_key, value_weight, out_rows, own_keys, count
     )
-    me = lax.axis_index("ens").reshape(1)
+    spot = (lax.axis_index("x") * 2 + lax.axis_index("y")) * ENS + lax.axis_index("ens")
+    me = spot.reshape(1)
     shares = lax.all_gather(share, "ens", axis=0)
     block = (2 * HELD_ROWS, COLS)
     scalar = {0: pl.BlockSpec(memory_space=pltpu.SMEM)}
@@ -334,19 +349,28 @@
         halves, key_weight, value_weight
     )
     lower = band_shift(upper, 1)
-    (send,) = call(
+    share_block = ((FAR + 1) * SHARE, COLS)
+    keep, *sends = call(
         weight_kernel,
-        [((NEAR, (FAR + 1) * SHARE, COLS), LOW)],
+        [(share_block, LOW)] * NEAR,
+        [((D, COLS), LOW), ((NEAR * SHARE, COLS), LOW)],
         specs={
-            **scalar,
+            **{i: pl.BlockSpec(memory_space=pltpu.SMEM) for i in range(1)},
             9: pl.BlockSpec((ENS, PRED_ROW, GROUP), lambda i: (0, 0, 0)),
             11: pl.BlockSpec((16, 128), lambda i: (0, 0)),
         },
     )(
-        me, halves, last1, last2, last3, latent, nodes1, nodes2, nodes3, shares, out_grad, upper
-    )
-    parts = lax.all_to_all(send, ("x", "y"), 0, 0, tiled=True)
-    (total,) = call(near_sum_kernel, [((FAR, SHARE, COLS + VARS_PAD), LOW)], specs=scalar)(me, parts)
+        me, halves, last1, last2, last3, latent, nodes1, nodes2, nodes3, shares,
+        out_grad, upper,
+    )
+    parts = [near_shift(value, *step) for step, value in zip(PATHS[:5], sends[:5])]
+    relayed = call(relay_kernel, [(share_block, LOW), (share_block, LOW)])(
+        parts[0], parts[1], sends[5], sends[6]
+    )
+    parts = parts[2:] + [near_shift(value, *step) for step, value in zip(PATHS[5:], relayed)]
+    (total,) = call(near_sum_kernel, [((FAR, SHARE, COLS + VARS_PAD), LOW)], specs=scalar)(
+        me, keep, *parts
+    )
     parts = lax.all_to_all(total, "z", 0, 0, tiled=True)
     (total,) = call(sum_kernel, [((SHARE, COLS + VARS_PAD), LOW)])(parts)
     parts = lax.all_gather(total, "ens", axis=0)

time: 87.9 us -> 82.2 us (0.935)
  blocking collectives: 43.1 us -> 22.5 us
  starting transfers between devices: 20.4 us -> 32.4 us
  waiting for transfers between devices: 9.97 us -> 12.8 us
    all_to_all x1 -> x0, blocking collectives: 21.9 us -> none  [on_device(): parts = lax.all_to_all(send, ('x', 'y'), 0, 0, tiled=True)]
    ppermute x0 -> x7, starting transfers between devices: none -> 11.6 us  [near_shift(): return lax.ppermute(value, ('x', 'y'), pairs)]
    ppermute x0 -> x7, waiting for transfers between devices: none -> 2.78 us  [near_shift(): return lax.ppermute(value, ('x', 'y'), pairs)]
    all_gather x1, blocking collectives: 9.64 us -> 11 us  [on_device(): parts = lax.all_gather(total, 'ens', axis=0)]
    pallas_call x8 -> x9, Pallas kernels: 10.5 us -> 10.5 us  [run(): pl.pallas_call(kernel, grid=(1,), in_specs=[places.get(i, whole(value.sha...]
  transfers between devices with their start and end apart: 9 -> 16, of which waited for: 3 -> 6; matrix products, arithmetic and copies ran while one was open for 2% -> 2% of each run, Pallas kernels for 9% -> 10%
where the time goes in v7:
time: 82.2 us; the launch traced here: 81.9 us
  starting transfers between devices  32.4 us (39%)
  blocking collectives  22.5 us (27%)
  waiting for transfers between devices  12.8 us (16%)
  Pallas kernels  10.5 us (13%)
  local copies, waits for them, and re-layouts  2.81 us (3%)
    ppermute x7, starting transfers between devices, near_shift(): return lax.ppermute(value, ('x', 'y'), pairs)  11.6 us
    all_gather x1, blocking collectives, on_device(): shares = lax.all_gather(share, 'ens', axis=0)  11.5 us
    all_gather x1, blocking collectives, on_device(): parts = lax.all_gather(total, 'ens', axis=0)  11 us
    pallas_call x9, Pallas kernels, run(): pl.pallas_call(kernel, grid=(1,), in_specs=[places.get(i, whole(value.sha...  10.5 us
    all_to_all x1, starting transfers between devices, on_device(): parts = lax.all_to_all(total, 'z', 0, 0, tiled=True)  8.54 us
    ppermute x6, starting transfers between devices, ens_swap(): return lax.ppermute(value, 'ens', [(e, e ^ k) for e in range(ENS)])  7.79 us
    all_to_all x1, waiting for transfers between devices, on_device(): parts = lax.all_to_all(total, 'z', 0, 0, tiled=True)  5.3 us
    ppermute x6, waiting for transfers between devices, ens_swap(): return lax.ppermute(value, 'ens', [(e, e ^ k) for e in range(ENS)])  4.67 us
  transfers between devices with their start and end apart: 16, of which 6 were waited for; matrix products, arithmetic and copies ran while one was open for 2% of the time, Pallas kernels for 10%

profile of v7, /device:TPU:1, one launch (start us, length us, event | category | flops | bytes accessed | tf_op | source)
XLA Modules:
  0.0 81.9 jit_solution(6909947364011585618)
XLA Ops:
  0.7 1.4 %collective-permute-start = (bf16[2,32,1024]{2,1,0:T(8,128)(2,1)}, bf16[2,32,1024]{2,1,0:T(8,128)(2,1)S(1)}, u32[]{:S(2)}, u32[]{:S(2)}) collective-permute-start(bf16[2,32,1024]{2,1,0:T(8,128)(2,1)} %nodes.1), channel_id=1, source_target_pairs={{1,0},{2,1},{3,2},{4,3},{5,4},{6,5},{7,6},{8,7},{9,8},{10,9},{11,1... | collective-permute-start | bytes 393224 | tf_op jit(solution)/shard_map/ppermute | solution.py:298
  2.1 3.8 %collective-permute-start.5 = (bf16[2,32,1024]{2,1,0:T(8,128)(2,1)}, bf16[2,32,1024]{2,1,0:T(8,128)(2,1)S(1)}, u32[]{:S(2)}, u32[]{:S(2)}) collective-permute-start(bf16[2,32,1024]{2,1,0:T(8,128)(2,1)} %nodes.1), channel_id=1, source_target_pairs={{0,128},{64,192},{128,0},{192,64},{1,129},{65,193},{129,1},{193,65... | collective-permute-start | bytes 393224 | tf_op jit(solution)/shard_map/ppermute | solution.py:302
  5.9 1.7 %fusion = (bf16[1024,512]{1,0:T(8,128)(2,1)S(1)}, bf16[1024,512]{1,0:T(8,128)(2,1)S(1)}) fusion(bf16[1024,1024]{1,0:T(8,128)(2,1)} %key_weight.1), kind=kLoop, calls=%fused_computation | loop fusion | bytes 4194304 | tf_op jit(solution)/shard_map/slice | solution.py:315
  9.4 3.1 %forward_kernel.1 = (f32[2,128,128]{2,1,0:T(8,128)S(1)}, bf16[384,256]{1,0:T(8,128)(2,1)S(1)}, bf16[2,128,1024]{2,1,0:T(8,128)(2,1)S(1)}, f32[2,128,128]{2,1,0:T...) custom-call(bf16[2,128,1024]{2,1,0:T(8,128)(2,1)S(1)} %copy-done.2, ...), custom_call_target="tpu_custom_call" | custom-call | flops 100000000 | bytes 4000000 | tf_op jit(solution)/shard_map/forward_kernel/pallas_call | solution.py:280
  12.5 11.5 %all-gather = bf16[1536,256]{1,0:T(8,128)(2,1)S(1)} all-gather(bf16[384,256]{1,0:T(8,128)(2,1)S(1)} %get-tuple-element.33), channel_id=2, replica_groups=mesh['ens'=4,'z'=8,'x'=4,'y'=2] {'ens'}, dimensions={0}, use_global_device_ids=true | all-gather | bytes 983040 | tf_op jit(solution)/shard_map/all_gather | solution.py:336
  24.1 2.9 %backward_kernel.1 = (bf16[4,128,512]{2,1,0:T(8,128)(2,1)S(1)}, bf16[256,512]{1,0:T(8,128)(2,1)S(1)}, bf16[128,512]{1,0:T(8,128)(2,1)S(1)}, bf16[128,512]{1,0:T(8,128)(2,1)S(1)}, bf16[1024,128]{1,0:T(8,128)(2,1)S(1)}) custom-call(s32[1]{0:T(128)} %bitcast.me, bf16[2,128,1024]{2,1,0:T(8,128)(2,1)S(1)} %copy-done.2, bf16[128,1024]{1,0:T(8,128)(2,1)S(1)} %pad.4.out_weight, ...), custom_call_target="tpu_custom_call" | custom-call | flops 100000000 | bytes 4000000 | tf_op jit(solution)/shard_map/backward_kernel/pallas_call | solution.py:280
  27.6 1.4 %collective-permute-start.2 = (bf16[128,512]{1,0:T(8,128)(2,1)S(1)}, bf16[128,512]{1,0:T(8,128)(2,1)S(1)}, u32[]{:S(2)}, u32[]{:S(2)}) collective-permute-start(bf16[128,512]{1,0:T(8,128)(2,1)S(1)} %get-tuple-element.41), channel_id=1, source_target_pairs={{0,128},{64,192},{128,0},{192,64},{1,129},{65,193},{129,1},{193,65... | collective-permute-start | bytes 393224 | tf_op jit(solution)/shard_map/ppermute | solution.py:302
  28.9 1.9 %collective-permute-start.3 = (bf16[128,512]{1,0:T(8,128)(2,1)S(1)}, bf16[128,512]{1,0:T(8,128)(2,1)S(1)}, u32[]{:S(2)}, u32[]{:S(2)}) collective-permute-start(bf16[128,512]{1,0:T(8,128)(2,1)S(1)} %get-tuple-element.42), channel_id=1, source_target_pairs={{0,192},{64,128},{128,64},{192,0},{1,193},{65,129},{129,65},{193,1... | collective-permute-start | bytes 393224 | tf_op jit(solution)/shard_map/ppermute | solution.py:302
  30.9 1.5 %latent_kernel.1 = (f32[64,1024]{1,0:T(8,128)S(1)}, bf16[64,1024]{1,0:T(8,128)(2,1)S(1)}) custom-call(bf16[4,128,512]{2,1,0:T(8,128)(2,1)S(1)} %get-tuple-element.39.halves, bf16[1024,1024]{1,0:T(8,128)(2,1)S(1)} %copy-done, bf16[1024,1024]{1,0:T(8,128)(2,1)S(1)} %copy-done.1), custom_call_target="tpu_custom_call" | custom-call | flops 100000000 | bytes 4000000 | tf_op jit(solution)/shard_map/latent_kernel/pallas_call | solution.py:280
  32.4 1.6 %collective-permute-done.2.last2 = bf16[128,512]{1,0:T(8,128)(2,1)S(1)} collective-permute-done((bf16[128,512]{1,0:T(8,128)(2,1)S(1)}, bf16[128,512]{1,0:T(8,128)(2,1)S(1)}, u32[]{:S(2)}, u32[]{:S(2)}) %collective-permute-start.2) | collective-permute-done | bytes 131104 | tf_op jit(solution)/shard_map/ppermute | solution.py:302
  34.0 3.1 %collective-permute-done.3.last3 = bf16[128,512]{1,0:T(8,128)(2,1)S(1)} collective-permute-done((bf16[128,512]{1,0:T(8,128)(2,1)S(1)}, bf16[128,512]{1,0:T(8,128)(2,1)S(1)}, u32[]{:S(2)}, u32[]{:S(2)}) %collective-permute-start.3) | collective-permute-done | bytes 131104 | tf_op jit(solution)/shard_map/ppermute | solution.py:302
  37.1 0.8 %weight_kernel.1 = (bf16[144,512]{1,0:T(8,128)(2,1)S(1)}, bf16[144,512]{1,0:T(8,128)(2,1)S(1)}, bf16[144,512]{1,0:T(8,128)(2,1)S(1)}, bf16[144,512]{1,0:T(8,128)...) custom-call(s32[1]{0:T(128)} %bitcast.me, ...), custom_call_target="tpu_custom_call" | custom-call | flops 100000000 | bytes 4000000 | tf_op jit(solution)/shard_map/weight_kernel/pallas_call | solution.py:280
  37.9 1.5 %collective-permute-start.10 = (bf16[144,512]{1,0:T(8,128)(2,1)S(1)}, bf16[144,512]{1,0:T(8,128)(2,1)S(1)}, u32[]{:S(2)}, u32[]{:S(2)}) collective-permute-start(bf16[144,512]{1,0:T(8,128)(2,1)S(1)} %get-tuple-element.49), channel_id=1, source_target_pairs={{0,2},{1,3},{2,4},{3,5},{4,6},{5,7},{6,0},{7,1},{8,10},{9,11},{10,... | collective-permute-start | bytes 442376 | tf_op jit(solution)/shard_map/ppermute | solution.py:307
  39.5 1.9 %collective-permute-start.11 = (bf16[144,512]{1,0:T(8,128)(2,1)S(1)}, bf16[144,512]{1,0:T(8,128)(2,1)S(1)}, u32[]{:S(2)}, u32[]{:S(2)}) collective-permute-start(bf16[144,512]{1,0:T(8,128)(2,1)S(1)} %get-tuple-element.50), channel_id=1, source_target_pairs={{0,6},{1,7},{2,0},{3,1},{4,2},{5,3},{6,4},{7,5},{8,14},{9,15},{10,... | collective-permute-start | bytes 442376 | tf_op jit(solution)/shard_map/ppermute | solution.py:307
  41.3 1.8 %collective-permute-start.7 = (bf16[144,512]{1,0:T(8,128)(2,1)S(1)}, bf16[144,512]{1,0:T(8,128)(2,1)S(1)}, u32[]{:S(2)}, u32[]{:S(2)}) collective-permute-start(bf16[144,512]{1,0:T(8,128)(2,1)S(1)} %get-tuple-element.46), channel_id=1, source_target_pairs={{0,1},{1,0},{2,3},{3,2},{4,5},{5,4},{6,7},{7,6},{8,9},{9,8},{10,11... | collective-permute-start | bytes 442376 | tf_op jit(solution)/shard_map/ppermute | solution.py:307
  43.1 2.4 %collective-permute-start.9 = (bf16[144,512]{1,0:T(8,128)(2,1)S(1)}, bf16[144,512]{1,0:T(8,128)(2,1)S(1)}, u32[]{:S(2)}, u32[]{:S(2)}) collective-permute-start(bf16[144,512]{1,0:T(8,128)(2,1)S(1)} %get-tuple-element.48), channel_id=1, source_target_pairs={{0,6},{1,7},{2,0},{3,1},{4,2},{5,3},{6,4},{7,5},{8,14},{9,15},{10,... | collective-permute-start | bytes 442376 | tf_op jit(solution)/shard_map/ppermute | solution.py:307
  45.8 3.7 %collective-permute-start.13 = (bf16[144,512]{1,0:T(8,128)(2,1)S(1)}, bf16[144,512]{1,0:T(8,128)(2,1)S(1)}, u32[]{:S(2)}, u32[]{:S(2)}) collective-permute-start(bf16[144,512]{1,0:T(8,128)(2,1)S(1)} %get-tuple-element.54), channel_id=1, source_target_pairs={{0,7},{1,6},{2,1},{3,0},{4,3},{5,2},{6,5},{7,4},{8,15},{9,14},{10,... | collective-permute-start | bytes 442376 | tf_op jit(solution)/shard_map/ppermute | solution.py:307
  49.9 2.1 %collective-permute-done.12.refs_3_ = bf16[144,512]{1,0:T(8,128)(2,1)S(1)} collective-permute-done((bf16[144,512]{1,0:T(8,128)(2,1)S(1)}, bf16[144,512]{1,0:T(8,128)(2,1)S(1)}, u32[]{:S(2)}, u32[]{:S(2)}) %collective-permute-start.12) | collective-permute-done | bytes 147488 | tf_op jit(solution)/shard_map/ppermute | solution.py:307
  52.4 0.8 near_sum_kernel.1
  53.1 8.5 %all-to-all-start = ((bf16[8,16,640]{2,1,0:T(8,128)(2,1)}), bf16[8,16,640]{2,1,0:T(8,128)(2,1)S(1)}, u32[]{:S(2)}, u32[]{:S(2)}) async-start(bf16[8,16,640]{2,1,0:T(8,128)(2,1)} %near_sum_kernel.1), calls=%async_computation | async-start | bytes 327680 | tf_op jit(solution)/shard_map/all_to_all | solution.py:374
  61.7 3.1 %collective-permute-start.14 = (bf16[64,1024]{1,0:T(8,128)(2,1)S(1)}, bf16[64,1024]{1,0:T(8,128)(2,1)S(1)}, u32[]{:S(2)}, u32[]{:S(2)}) collective-permute-start(bf16[64,1024]{1,0:T(8,128)(2,1)S(1)} %get-tuple-element.44.upper), channel_id=1, source_target_pairs={{0,1},{1,2},{2,3},{3,4},{4,5},{5,6},{6,7},{7,8},{8,9},{9,10},{10,1... | collective-permute-start | bytes 393224 | tf_op jit(solution)/shard_map/ppermute | solution.py:298
  64.8 5.3 %all-to-all-done.parts = bf16[8,16,640]{2,1,0:T(8,128)(2,1)S(1)} async-done(((bf16[8,16,640]{2,1,0:T(8,128)(2,1)}), bf16[8,16,640]{2,1,0:T(8,128)(2,1)S(1)}, u32[]{:S(2)}, u32[]{:S(2)}) %all-to-all-start) | async-done | bytes 163872 | tf_op jit(solution)/shard_map/all_to_all | solution.py:374
  70.1 11.0 %all-gather.1 = bf16[64,640]{1,0:T(8,128)(2,1)S(1)} all-gather(bf16[16,640]{1,0:T(8,128)(2,1)S(1)} %sum_kernel.1), channel_id=3, replica_groups=mesh['ens'=4,'z'=8,'x'=4,'y'=2] {'ens'}, dimensions={0}, use_global_device_ids=true | all-gather | bytes 102400 | tf_op jit(solution)/shard_map/all_gather | solution.py:376
  81.1 0.8 finish_kernel.1
  (35 shorter events, 3.5 us)
Async XLA Ops:
  0.6 7.1 %copy-start.3 = (bf16[2,32,1024]{2,1,0:T(8,128)(2,1)S(1)}, bf16[2,32,1024]{2,1,0:T(8,128)(2,1)}, u32[]{:S(2)}) copy-start(bf16[2,32,1024]{2,1,0:T(8,128)(2,1)} %nodes.1) | copy-start | bytes 393220
  0.6 7.0 %copy-start.6 = (bf16[100,1024]{1,0:T(8,128)(2,1)S(1)}, bf16[100,1024]{1,0:T(8,128)(2,1)}, u32[]{:S(2)}) copy-start(bf16[100,1024]{1,0:T(8,128)(2,1)} %param.11) | copy-start | bytes 614404
  0.7 7.0 %copy-start.5 = (s32[2,512]{1,0:T(2,128)S(1)}, s32[2,512]{1,0:T(2,128)}, u32[]{:S(2)}) copy-start(s32[2,512]{1,0:T(2,128)} %edges.1) | copy-start | bytes 12292
  0.7 7.6 %collective-permute-start = (bf16[2,32,1024]{2,1,0:T(8,128)(2,1)}, bf16[2,32,1024]{2,1,0:T(8,128)(2,1)S(1)}, u32[]{:S(2)}, u32[]{:S(2)}) collective-permute-start(bf16[2,32,1024]{2,1,0:T(8,128)(2,1)} %nodes.1), channel_id=1, source_target_pairs={{1,0},{2,1},{3,2},{4,3},{5,4},{6,5},{7,6},{8,7},{9,8},{10,9},{11,1... | collective-permute-start | bytes 393224 | tf_op jit(solution)/shard_map/ppermute | solution.py:298
  2.1 28.8 %collective-permute-start.5 = (bf16[2,32,1024]{2,1,0:T(8,128)(2,1)}, bf16[2,32,1024]{2,1,0:T(8,128)(2,1)S(1)}, u32[]{:S(2)}, u32[]{:S(2)}) collective-permute-start(bf16[2,32,1024]{2,1,0:T(8,128)(2,1)} %nodes.1), channel_id=1, source_target_pairs={{0,128},{64,192},{128,0},{192,64},{1,129},{65,193},{129,1},{193,65... | collective-permute-start | bytes 393224 | tf_op jit(solution)/shard_map/ppermute | solution.py:302
  7.6 1.0 %copy-start.2 = (bf16[2,128,1024]{2,1,0:T(8,128)(2,1)S(1)}, bf16[2,128,1024]{2,1,0:T(8,128)(2,1)}, u32[]{:S(2)}) copy-start(bf16[2,128,1024]{2,1,0:T(8,128)(2,1)} %embed.3) | copy-start | bytes 1572868
  7.7 1.7 %copy-start.1 = (bf16[1024,1024]{1,0:T(8,128)(2,1)S(1)}, bf16[1024,1024]{1,0:T(8,128)(2,1)}, u32[]{:S(2)}) copy-start(bf16[1024,1024]{1,0:T(8,128)(2,1)} %value_weight.3) | copy-start | bytes 6291460
  9.4 14.7 %copy-start.4 = (f32[100,128]{1,0:T(8,128)S(1)}, f32[100,128]{1,0:T(8,128)}, u32[]{:S(2)}) copy-start(f32[100,128]{1,0:T(8,128)} %target.1) | copy-start | bytes 153604
  24.0 6.9 %copy-start = (bf16[1024,1024]{1,0:T(8,128)(2,1)S(1)}, bf16[1024,1024]{1,0:T(8,128)(2,1)}, u32[]{:S(2)}) copy-start(bf16[1024,1024]{1,0:T(8,128)(2,1)} %key_weight.1) | copy-start | bytes 6291460
  27.0 10.1 %collective-permute-start.1 = (bf16[256,512]{1,0:T(8,128)(2,1)S(1)}, bf16[256,512]{1,0:T(8,128)(2,1)S(1)}, u32[]{:S(2)}, u32[]{:S(2)}) collective-permute-start(bf16[256,512]{1,0:T(8,128)(2,1)S(1)} %get-tuple-element.40), channel_id=1, source_target_pairs={{0,64},{64,0},{128,192},{192,128},{1,65},{65,1},{129,193},{193,129... | collective-permute-start | bytes 786440 | tf_op jit(solution)/shard_map/ppermute | solution.py:302
  27.2 5.2 %collective-permute-start.4 = (bf16[2,32,1024]{2,1,0:T(8,128)(2,1)S(1)}, bf16[2,32,1024]{2,1,0:T(8,128)(2,1)S(1)}, u32[]{:S(2)}, u32[]{:S(2)}) collective-permute-start(bf16[2,32,1024]{2,1,0:T(8,128)(2,1)S(1)} %copy-done.3), channel_id=1, source_target_pairs={{0,64},{64,0},{128,192},{192,128},{1,65},{65,1},{129,193},{193,129... | collective-permute-start | bytes 393224 | tf_op jit(solution)/shard_map/ppermute | solution.py:302
  27.6 6.5 %collective-permute-start.2 = (bf16[128,512]{1,0:T(8,128)(2,1)S(1)}, bf16[128,512]{1,0:T(8,128)(2,1)S(1)}, u32[]{:S(2)}, u32[]{:S(2)}) collective-permute-start(bf16[128,512]{1,0:T(8,128)(2,1)S(1)} %get-tuple-element.41), channel_id=1, source_target_pairs={{0,128},{64,192},{128,0},{192,64},{1,129},{65,193},{129,1},{193,65... | collective-permute-start | bytes 393224 | tf_op jit(solution)/shard_map/ppermute | solution.py:302
  28.9 8.2 %collective-permute-start.3 = (bf16[128,512]{1,0:T(8,128)(2,1)S(1)}, bf16[128,512]{1,0:T(8,128)(2,1)S(1)}, u32[]{:S(2)}, u32[]{:S(2)}) collective-permute-start(bf16[128,512]{1,0:T(8,128)(2,1)S(1)} %get-tuple-element.42), channel_id=1, source_target_pairs={{0,192},{64,128},{128,64},{192,0},{1,193},{65,129},{129,65},{193,1... | collective-permute-start | bytes 393224 | tf_op jit(solution)/shard_map/ppermute | solution.py:302
  30.8 6.2 %collective-permute-start.6 = (bf16[2,32,1024]{2,1,0:T(8,128)(2,1)S(1)}, bf16[2,32,1024]{2,1,0:T(8,128)(2,1)S(1)}, u32[]{:S(2)}, u32[]{:S(2)}) collective-permute-start(bf16[2,32,1024]{2,1,0:T(8,128)(2,1)S(1)} %collective-permute-done.5.nodes2), channel_id=1, source_target_pairs={{0,64},{64,0},{128,192},{192,128},{1,65},{65,1},{129,193},{193,129... | collective-permute-start | bytes 393224 | tf_op jit(solution)/shard_map/ppermute | solution.py:302
  37.9 7.6 %collective-permute-start.10 = (bf16[144,512]{1,0:T(8,128)(2,1)S(1)}, bf16[144,512]{1,0:T(8,128)(2,1)S(1)}, u32[]{:S(2)}, u32[]{:S(2)}) collective-permute-start(bf16[144,512]{1,0:T(8,128)(2,1)S(1)} %get-tuple-element.49), channel_id=1, source_target_pairs={{0,2},{1,3},{2,4},{3,5},{4,6},{5,7},{6,0},{7,1},{8,10},{9,11},{10,... | collective-permute-start | bytes 442376 | tf_op jit(solution)/shard_map/ppermute | solution.py:307
  39.5 6.0 %collective-permute-start.11 = (bf16[144,512]{1,0:T(8,128)(2,1)S(1)}, bf16[144,512]{1,0:T(8,128)(2,1)S(1)}, u32[]{:S(2)}, u32[]{:S(2)}) collective-permute-start(bf16[144,512]{1,0:T(8,128)(2,1)S(1)} %get-tuple-element.50), channel_id=1, source_target_pairs={{0,6},{1,7},{2,0},{3,1},{4,2},{5,3},{6,4},{7,5},{8,14},{9,15},{10,... | collective-permute-start | bytes 442376 | tf_op jit(solution)/shard_map/ppermute | solution.py:307
  41.3 8.2 %collective-permute-start.7 = (bf16[144,512]{1,0:T(8,128)(2,1)S(1)}, bf16[144,512]{1,0:T(8,128)(2,1)S(1)}, u32[]{:S(2)}, u32[]{:S(2)}) collective-permute-start(bf16[144,512]{1,0:T(8,128)(2,1)S(1)} %get-tuple-element.46), channel_id=1, source_target_pairs={{0,1},{1,0},{2,3},{3,2},{4,5},{5,4},{6,7},{7,6},{8,9},{9,8},{10,11... | collective-permute-start | bytes 442376 | tf_op jit(solution)/shard_map/ppermute | solution.py:307
  43.1 6.8 %collective-permute-start.8 = (bf16[144,512]{1,0:T(8,128)(2,1)S(1)}, bf16[144,512]{1,0:T(8,128)(2,1)S(1)}, u32[]{:S(2)}, u32[]{:S(2)}) collective-permute-start(bf16[144,512]{1,0:T(8,128)(2,1)S(1)} %get-tuple-element.47), channel_id=1, source_target_pairs={{0,3},{1,2},{2,5},{3,4},{4,7},{5,6},{6,1},{7,0},{8,11},{9,10},{10,... | collective-permute-start | bytes 442376 | tf_op jit(solution)/shard_map/ppermute | solution.py:307
  43.1 6.8 %collective-permute-start.9 = (bf16[144,512]{1,0:T(8,128)(2,1)S(1)}, bf16[144,512]{1,0:T(8,128)(2,1)S(1)}, u32[]{:S(2)}, u32[]{:S(2)}) collective-permute-start(bf16[144,512]{1,0:T(8,128)(2,1)S(1)} %get-tuple-element.48), channel_id=1, source_target_pairs={{0,6},{1,7},{2,0},{3,1},{4,2},{5,3},{6,4},{7,5},{8,14},{9,15},{10,... | collective-permute-start | bytes 442376 | tf_op jit(solution)/shard_map/ppermute | solution.py:307
  45.6 6.4 %collective-permute-start.12 = (bf16[144,512]{1,0:T(8,128)(2,1)S(1)}, bf16[144,512]{1,0:T(8,128)(2,1)S(1)}, u32[]{:S(2)}, u32[]{:S(2)}) collective-permute-start(bf16[144,512]{1,0:T(8,128)(2,1)S(1)} %get-tuple-element.53), channel_id=1, source_target_pairs={{0,2},{1,3},{2,4},{3,5},{4,6},{5,7},{6,0},{7,1},{8,10},{9,11},{10,... | collective-permute-start | bytes 442376 | tf_op jit(solution)/shard_map/ppermute | solution.py:307
  45.8 6.5 %collective-permute-start.13 = (bf16[144,512]{1,0:T(8,128)(2,1)S(1)}, bf16[144,512]{1,0:T(8,128)(2,1)S(1)}, u32[]{:S(2)}, u32[]{:S(2)}) collective-permute-start(bf16[144,512]{1,0:T(8,128)(2,1)S(1)} %get-tuple-element.54), channel_id=1, source_target_pairs={{0,7},{1,6},{2,1},{3,0},{4,3},{5,2},{6,5},{7,4},{8,15},{9,14},{10,... | collective-permute-start | bytes 442376 | tf_op jit(solution)/shard_map/ppermute | solution.py:307
  53.1 16.9 %all-to-all-start = ((bf16[8,16,640]{2,1,0:T(8,128)(2,1)}), bf16[8,16,640]{2,1,0:T(8,128)(2,1)S(1)}, u32[]{:S(2)}, u32[]{:S(2)}) async-start(bf16[8,16,640]{2,1,0:T(8,128)(2,1)} %near_sum_kernel.1), calls=%async_computation | async-start | bytes 327680 | tf_op jit(solution)/shard_map/all_to_all | solution.py:374
  61.7 19.4 %collective-permute-start.14 = (bf16[64,1024]{1,0:T(8,128)(2,1)S(1)}, bf16[64,1024]{1,0:T(8,128)(2,1)S(1)}, u32[]{:S(2)}, u32[]{:S(2)}) collective-permute-start(bf16[64,1024]{1,0:T(8,128)(2,1)S(1)} %get-tuple-element.44.upper), channel_id=1, source_target_pairs={{0,1},{1,2},{2,3},{3,4},{4,5},{5,6},{6,7},{7,8},{8,9},{9,10},{10,1... | collective-permute-start | bytes 393224 | tf_op jit(solution)/shard_map/ppermute | solution.py:298

commit v8 on v7

--- a/solution.py
+++ b/solution.py
@@ -256,11 +256,15 @@
 
 
 def finish_kernel(
-    parts, own, lower, key_weight_grad, value_weight_grad, out_weight_grad, grad_latent
+    me, mine, part1, part2, part3, own, lower,
+    key_weight_grad, value_weight_grad, out_weight_grad, grad_latent,
+    parts,
 ):
     for m in range(HELD):
         rows = slice(m * LAT_DEV, (m + 1) * LAT_DEV)
         grad_latent[m] = own[rows] + lower[rows].astype(F32)
+    for k, part in enumerate((mine, part1, part2, part3)):
+        parts[(me[0] & (ENS - 1)) ^ k] = part[...]
     total = parts[0, :, COLS:].astype(F32)
     for e in range(1, ENS):
         total = total + parts[e, :, COLS:].astype(F32)
@@ -373,12 +377,14 @@
     )
     parts = lax.all_to_all(total, "z", 0, 0, tiled=True)
     (total,) = call(sum_kernel, [((SHARE, COLS + VARS_PAD), LOW)])(parts)
-    parts = lax.all_gather(total, "ens", axis=0)
+    parts = [ens_swap(total, k) for k in (1, 2, 3)]
     return tuple(
         call(
             finish_kernel,
             [((16, D), F32), ((16, D), F32), ((16, VARS), F32), ((HELD, LAT_DEV, D), F32)],
-        )(parts, own, lower)
+            [((ENS, SHARE, COLS + VARS_PAD), LOW)],
+            scalar,
+        )(me, total, *parts, own, lower)
     )
 
 

time: 82.2 us -> 81.6 us (level)
  blocking collectives: 22.5 us -> 11.5 us
  starting transfers between devices: 32.4 us -> 40.1 us
  waiting for transfers between devices: 12.8 us -> 15.5 us
    all_gather x1 -> x0, blocking collectives: 11 us -> none  [on_device(): parts = lax.all_gather(total, 'ens', axis=0)]
    ppermute x6 -> x9, starting transfers between devices: 7.79 us -> 15.5 us  [ens_swap(): return lax.ppermute(value, 'ens', [(e, e ^ k) for e in range(ENS)])]
    ppermute x6 -> x9, waiting for transfers between devices: 4.67 us -> 7.37 us  [ens_swap(): return lax.ppermute(value, 'ens', [(e, e ^ k) for e in range(ENS)])]
  transfers between devices with their start and end apart: 16 -> 19, of which waited for: 6 -> 8; matrix products, arithmetic and copies ran while one was open for 2% -> 2% of each run, Pallas kernels for 10% -> 10%
where the time goes in v8:
time: 81.6 us; the launch traced here: 81.3 us
  starting transfers between devices  40.1 us (49%)
  waiting for transfers between devices  15.5 us (19%)
  blocking collectives  11.5 us (14%)
  Pallas kernels  10.5 us (13%)
  local copies, waits for them, and re-layouts  2.81 us (3%)
  between operations  0.82 us (1%)
    ppermute x9, starting transfers between devices, ens_swap(): return lax.ppermute(value, 'ens', [(e, e ^ k) for e in range(ENS)])  15.5 us
    ppermute x7, starting transfers between devices, near_shift(): return lax.ppermute(value, ('x', 'y'), pairs)  11.6 us
    all_gather x1, blocking collectives, on_device(): shares = lax.all_gather(share, 'ens', axis=0)  11.5 us
    pallas_call x9, Pallas kernels, run(): pl.pallas_call(kernel, grid=(1,), in_specs=[places.get(i, whole(value.sha...  10.5 us
    all_to_all x1, starting transfers between devices, on_device(): parts = lax.all_to_all(total, 'z', 0, 0, tiled=True)  8.54 us
    ppermute x9, waiting for transfers between devices, ens_swap(): return lax.ppermute(value, 'ens', [(e, e ^ k) for e in range(ENS)])  7.37 us
    all_to_all x1, waiting for transfers between devices, on_device(): parts = lax.all_to_all(total, 'z', 0, 0, tiled=True)  5.3 us
    ppermute x2, starting transfers between devices, band_shift(): lax.ppermute(value, BAND, [(i, i + by) for i in range(64) if 0 <= i + by...  4.5 us
  transfers between devices with their start and end apart: 19, of which 8 were waited for; matrix products, arithmetic and copies ran while one was open for 2% of the time, Pallas kernels for 10%

profile of v8, /device:TPU:1, one launch (start us, length us, event | category | flops | bytes accessed | tf_op | source)
XLA Modules:
  0.0 81.3 jit_solution(6516873677457660426)
XLA Ops:
  0.7 1.4 %collective-permute-start = (bf16[2,32,1024]{2,1,0:T(8,128)(2,1)}, bf16[2,32,1024]{2,1,0:T(8,128)(2,1)S(1)}, u32[]{:S(2)}, u32[]{:S(2)}) collective-permute-start(bf16[2,32,1024]{2,1,0:T(8,128)(2,1)} %nodes.1), channel_id=1, source_target_pairs={{1,0},{2,1},{3,2},{4,3},{5,4},{6,5},{7,6},{8,7},{9,8},{10,9},{11,1... | collective-permute-start | bytes 393224 | tf_op jit(solution)/shard_map/ppermute | solution.py:302
  2.1 3.8 %collective-permute-start.5 = (bf16[2,32,1024]{2,1,0:T(8,128)(2,1)}, bf16[2,32,1024]{2,1,0:T(8,128)(2,1)S(1)}, u32[]{:S(2)}, u32[]{:S(2)}) collective-permute-start(bf16[2,32,1024]{2,1,0:T(8,128)(2,1)} %nodes.1), channel_id=1, source_target_pairs={{0,128},{64,192},{128,0},{192,64},{1,129},{65,193},{129,1},{193,65... | collective-permute-start | bytes 393224 | tf_op jit(solution)/shard_map/ppermute | solution.py:306
  5.9 1.7 %fusion = (bf16[1024,512]{1,0:T(8,128)(2,1)S(1)}, bf16[1024,512]{1,0:T(8,128)(2,1)S(1)}) fusion(bf16[1024,1024]{1,0:T(8,128)(2,1)} %key_weight.1), kind=kLoop, calls=%fused_computation | loop fusion | bytes 4194304 | tf_op jit(solution)/shard_map/slice | solution.py:319
  9.4 3.1 %forward_kernel.1 = (f32[2,128,128]{2,1,0:T(8,128)S(1)}, bf16[384,256]{1,0:T(8,128)(2,1)S(1)}, bf16[2,128,1024]{2,1,0:T(8,128)(2,1)S(1)}, f32[2,128,128]{2,1,0:T...) custom-call(bf16[2,128,1024]{2,1,0:T(8,128)(2,1)S(1)} %copy-done.2, ...), custom_call_target="tpu_custom_call" | custom-call | flops 100000000 | bytes 4000000 | tf_op jit(solution)/shard_map/forward_kernel/pallas_call | solution.py:284
  12.5 11.5 %all-gather = bf16[1536,256]{1,0:T(8,128)(2,1)S(1)} all-gather(bf16[384,256]{1,0:T(8,128)(2,1)S(1)} %get-tuple-element.33), channel_id=2, replica_groups=mesh['ens'=4,'z'=8,'x'=4,'y'=2] {'ens'}, dimensions={0}, use_global_device_ids=true | all-gather | bytes 983040 | tf_op jit(solution)/shard_map/all_gather | solution.py:340
  24.1 2.9 %backward_kernel.1 = (bf16[4,128,512]{2,1,0:T(8,128)(2,1)S(1)}, bf16[256,512]{1,0:T(8,128)(2,1)S(1)}, bf16[128,512]{1,0:T(8,128)(2,1)S(1)}, bf16[128,512]{1,0:T(8,128)(2,1)S(1)}, bf16[1024,128]{1,0:T(8,128)(2,1)S(1)}) custom-call(s32[1]{0:T(128)} %bitcast.me, bf16[2,128,1024]{2,1,0:T(8,128)(2,1)S(1)} %copy-done.2, bf16[128,1024]{1,0:T(8,128)(2,1)S(1)} %pad.4.out_weight, ...), custom_call_target="tpu_custom_call" | custom-call | flops 100000000 | bytes 4000000 | tf_op jit(solution)/shard_map/backward_kernel/pallas_call | solution.py:284
  27.6 1.4 %collective-permute-start.2 = (bf16[128,512]{1,0:T(8,128)(2,1)S(1)}, bf16[128,512]{1,0:T(8,128)(2,1)S(1)}, u32[]{:S(2)}, u32[]{:S(2)}) collective-permute-start(bf16[128,512]{1,0:T(8,128)(2,1)S(1)} %get-tuple-element.41), channel_id=1, source_target_pairs={{0,128},{64,192},{128,0},{192,64},{1,129},{65,193},{129,1},{193,65... | collective-permute-start | bytes 393224 | tf_op jit(solution)/shard_map/ppermute | solution.py:306
  28.9 1.9 %collective-permute-start.3 = (bf16[128,512]{1,0:T(8,128)(2,1)S(1)}, bf16[128,512]{1,0:T(8,128)(2,1)S(1)}, u32[]{:S(2)}, u32[]{:S(2)}) collective-permute-start(bf16[128,512]{1,0:T(8,128)(2,1)S(1)} %get-tuple-element.42), channel_id=1, source_target_pairs={{0,192},{64,128},{128,64},{192,0},{1,193},{65,129},{129,65},{193,1... | collective-permute-start | bytes 393224 | tf_op jit(solution)/shard_map/ppermute | solution.py:306
  30.9 1.5 %latent_kernel.1 = (f32[64,1024]{1,0:T(8,128)S(1)}, bf16[64,1024]{1,0:T(8,128)(2,1)S(1)}) custom-call(bf16[4,128,512]{2,1,0:T(8,128)(2,1)S(1)} %get-tuple-element.39.halves, bf16[1024,1024]{1,0:T(8,128)(2,1)S(1)} %copy-done, bf16[1024,1024]{1,0:T(8,128)(2,1)S(1)} %copy-done.1), custom_call_target="tpu_custom_call" | custom-call | flops 100000000 | bytes 4000000 | tf_op jit(solution)/shard_map/latent_kernel/pallas_call | solution.py:284
  32.4 1.6 %collective-permute-done.2.last2 = bf16[128,512]{1,0:T(8,128)(2,1)S(1)} collective-permute-done((bf16[128,512]{1,0:T(8,128)(2,1)S(1)}, bf16[128,512]{1,0:T(8,128)(2,1)S(1)}, u32[]{:S(2)}, u32[]{:S(2)}) %collective-permute-start.2) | collective-permute-done | bytes 131104 | tf_op jit(solution)/shard_map/ppermute | solution.py:306
  34.0 3.1 %collective-permute-done.3.last3 = bf16[128,512]{1,0:T(8,128)(2,1)S(1)} collective-permute-done((bf16[128,512]{1,0:T(8,128)(2,1)S(1)}, bf16[128,512]{1,0:T(8,128)(2,1)S(1)}, u32[]{:S(2)}, u32[]{:S(2)}) %collective-permute-start.3) | collective-permute-done | bytes 131104 | tf_op jit(solution)/shard_map/ppermute | solution.py:306
  37.9 1.5 %collective-permute-start.10 = (bf16[144,512]{1,0:T(8,128)(2,1)S(1)}, bf16[144,512]{1,0:T(8,128)(2,1)S(1)}, u32[]{:S(2)}, u32[]{:S(2)}) collective-permute-start(bf16[144,512]{1,0:T(8,128)(2,1)S(1)} %get-tuple-element.49), channel_id=1, source_target_pairs={{0,2},{1,3},{2,4},{3,5},{4,6},{5,7},{6,0},{7,1},{8,10},{9,11},{10,... | collective-permute-start | bytes 442376 | tf_op jit(solution)/shard_map/ppermute | solution.py:311
  39.5 1.9 %collective-permute-start.11 = (bf16[144,512]{1,0:T(8,128)(2,1)S(1)}, bf16[144,512]{1,0:T(8,128)(2,1)S(1)}, u32[]{:S(2)}, u32[]{:S(2)}) collective-permute-start(bf16[144,512]{1,0:T(8,128)(2,1)S(1)} %get-tuple-element.50), channel_id=1, source_target_pairs={{0,6},{1,7},{2,0},{3,1},{4,2},{5,3},{6,4},{7,5},{8,14},{9,15},{10,... | collective-permute-start | bytes 442376 | tf_op jit(solution)/shard_map/ppermute | solution.py:311
  41.3 1.8 %collective-permute-start.7 = (bf16[144,512]{1,0:T(8,128)(2,1)S(1)}, bf16[144,512]{1,0:T(8,128)(2,1)S(1)}, u32[]{:S(2)}, u32[]{:S(2)}) collective-permute-start(bf16[144,512]{1,0:T(8,128)(2,1)S(1)} %get-tuple-element.46), channel_id=1, source_target_pairs={{0,1},{1,0},{2,3},{3,2},{4,5},{5,4},{6,7},{7,6},{8,9},{9,8},{10,11... | collective-permute-start | bytes 442376 | tf_op jit(solution)/shard_map/ppermute | solution.py:311
  43.1 2.4 %collective-permute-start.9 = (bf16[144,512]{1,0:T(8,128)(2,1)S(1)}, bf16[144,512]{1,0:T(8,128)(2,1)S(1)}, u32[]{:S(2)}, u32[]{:S(2)}) collective-permute-start(bf16[144,512]{1,0:T(8,128)(2,1)S(1)} %get-tuple-element.48), channel_id=1, source_target_pairs={{0,6},{1,7},{2,0},{3,1},{4,2},{5,3},{6,4},{7,5},{8,14},{9,15},{10,... | collective-permute-start | bytes 442376 | tf_op jit(solution)/shard_map/ppermute | solution.py:311
  45.8 3.7 %collective-permute-start.13 = (bf16[144,512]{1,0:T(8,128)(2,1)S(1)}, bf16[144,512]{1,0:T(8,128)(2,1)S(1)}, u32[]{:S(2)}, u32[]{:S(2)}) collective-permute-start(bf16[144,512]{1,0:T(8,128)(2,1)S(1)} %get-tuple-element.54), channel_id=1, source_target_pairs={{0,7},{1,6},{2,1},{3,0},{4,3},{5,2},{6,5},{7,4},{8,15},{9,14},{10,... | collective-permute-start | bytes 442376 | tf_op jit(solution)/shard_map/ppermute | solution.py:311
  49.9 2.1 %collective-permute-done.12.refs_3_ = bf16[144,512]{1,0:T(8,128)(2,1)S(1)} collective-permute-done((bf16[144,512]{1,0:T(8,128)(2,1)S(1)}, bf16[144,512]{1,0:T(8,128)(2,1)S(1)}, u32[]{:S(2)}, u32[]{:S(2)}) %collective-permute-start.12) | collective-permute-done | bytes 147488 | tf_op jit(solution)/shard_map/ppermute | solution.py:311
  53.1 8.5 %all-to-all-start = ((bf16[8,16,640]{2,1,0:T(8,128)(2,1)}), bf16[8,16,640]{2,1,0:T(8,128)(2,1)S(1)}, u32[]{:S(2)}, u32[]{:S(2)}) async-start(bf16[8,16,640]{2,1,0:T(8,128)(2,1)} %near_sum_kernel.1), calls=%async_computation | async-start | bytes 327680 | tf_op jit(solution)/shard_map/all_to_all | solution.py:378
  61.7 3.1 %collective-permute-start.17 = (bf16[64,1024]{1,0:T(8,128)(2,1)S(1)}, bf16[64,1024]{1,0:T(8,128)(2,1)S(1)}, u32[]{:S(2)}, u32[]{:S(2)}) collective-permute-start(bf16[64,1024]{1,0:T(8,128)(2,1)S(1)} %get-tuple-element.44.upper), channel_id=1, source_target_pairs={{0,1},{1,2},{2,3},{3,4},{4,5},{5,6},{6,7},{7,8},{8,9},{9,10},{10,1... | collective-permute-start | bytes 393224 | tf_op jit(solution)/shard_map/ppermute | solution.py:302
  64.8 5.3 %all-to-all-done.parts = bf16[8,16,640]{2,1,0:T(8,128)(2,1)S(1)} async-done(((bf16[8,16,640]{2,1,0:T(8,128)(2,1)}), bf16[8,16,640]{2,1,0:T(8,128)(2,1)S(1)}, u32[]{:S(2)}, u32[]{:S(2)}) %all-to-all-start) | async-done | bytes 163872 | tf_op jit(solution)/shard_map/all_to_all | solution.py:378
  70.1 4.5 %collective-permute-start.14 = (bf16[16,640]{1,0:T(8,128)(2,1)S(1)}, bf16[16,640]{1,0:T(8,128)(2,1)S(1)}, u32[]{:S(2)}, u32[]{:S(2)}) collective-permute-start(bf16[16,640]{1,0:T(8,128)(2,1)S(1)} %sum_kernel.1.mine), channel_id=1, source_target_pairs={{0,64},{64,0},{128,192},{192,128},{1,65},{65,1},{129,193},{193,129... | collective-permute-start | bytes 61448 | tf_op jit(solution)/shard_map/ppermute | solution.py:306
  74.6 1.2 %collective-permute-start.15 = (bf16[16,640]{1,0:T(8,128)(2,1)S(1)}, bf16[16,640]{1,0:T(8,128)(2,1)S(1)}, u32[]{:S(2)}, u32[]{:S(2)}) collective-permute-start(bf16[16,640]{1,0:T(8,128)(2,1)S(1)} %sum_kernel.1.mine), channel_id=1, source_target_pairs={{0,128},{64,192},{128,0},{192,64},{1,129},{65,193},{129,1},{193,65... | collective-permute-start | bytes 61448 | tf_op jit(solution)/shard_map/ppermute | solution.py:306
  75.8 2.0 %collective-permute-start.16 = (bf16[16,640]{1,0:T(8,128)(2,1)S(1)}, bf16[16,640]{1,0:T(8,128)(2,1)S(1)}, u32[]{:S(2)}, u32[]{:S(2)}) collective-permute-start(bf16[16,640]{1,0:T(8,128)(2,1)S(1)} %sum_kernel.1.mine), channel_id=1, source_target_pairs={{0,192},{64,128},{128,64},{192,0},{1,193},{65,129},{129,65},{193,1... | collective-permute-start | bytes 61448 | tf_op jit(solution)/shard_map/ppermute | solution.py:306
  78.7 1.8 %collective-permute-done.16.part3 = bf16[16,640]{1,0:T(8,128)(2,1)S(1)} collective-permute-done((bf16[16,640]{1,0:T(8,128)(2,1)S(1)}, bf16[16,640]{1,0:T(8,128)(2,1)S(1)}, u32[]{:S(2)}, u32[]{:S(2)}) %collective-permute-start.16) | collective-permute-done | bytes 20512 | tf_op jit(solution)/shard_map/ppermute | solution.py:306
  (40 shorter events, 6.8 us)
Async XLA Ops:
  0.6 7.1 %copy-start.3 = (bf16[2,32,1024]{2,1,0:T(8,128)(2,1)S(1)}, bf16[2,32,1024]{2,1,0:T(8,128)(2,1)}, u32[]{:S(2)}) copy-start(bf16[2,32,1024]{2,1,0:T(8,128)(2,1)} %nodes.1) | copy-start | bytes 393220
  0.6 7.0 %copy-start.6 = (bf16[100,1024]{1,0:T(8,128)(2,1)S(1)}, bf16[100,1024]{1,0:T(8,128)(2,1)}, u32[]{:S(2)}) copy-start(bf16[100,1024]{1,0:T(8,128)(2,1)} %param.11) | copy-start | bytes 614404
  0.7 7.0 %copy-start.5 = (s32[2,512]{1,0:T(2,128)S(1)}, s32[2,512]{1,0:T(2,128)}, u32[]{:S(2)}) copy-start(s32[2,512]{1,0:T(2,128)} %edges.1) | copy-start | bytes 12292
  0.7 7.6 %collective-permute-start = (bf16[2,32,1024]{2,1,0:T(8,128)(2,1)}, bf16[2,32,1024]{2,1,0:T(8,128)(2,1)S(1)}, u32[]{:S(2)}, u32[]{:S(2)}) collective-permute-start(bf16[2,32,1024]{2,1,0:T(8,128)(2,1)} %nodes.1), channel_id=1, source_target_pairs={{1,0},{2,1},{3,2},{4,3},{5,4},{6,5},{7,6},{8,7},{9,8},{10,9},{11,1... | collective-permute-start | bytes 393224 | tf_op jit(solution)/shard_map/ppermute | solution.py:302
  2.1 28.8 %collective-permute-start.5 = (bf16[2,32,1024]{2,1,0:T(8,128)(2,1)}, bf16[2,32,1024]{2,1,0:T(8,128)(2,1)S(1)}, u32[]{:S(2)}, u32[]{:S(2)}) collective-permute-start(bf16[2,32,1024]{2,1,0:T(8,128)(2,1)} %nodes.1), channel_id=1, source_target_pairs={{0,128},{64,192},{128,0},{192,64},{1,129},{65,193},{129,1},{193,65... | collective-permute-start | bytes 393224 | tf_op jit(solution)/shard_map/ppermute | solution.py:306
  9.4 14.7 %copy-start.4 = (f32[100,128]{1,0:T(8,128)S(1)}, f32[100,128]{1,0:T(8,128)}, u32[]{:S(2)}) copy-start(f32[100,128]{1,0:T(8,128)} %target.1) | copy-start | bytes 153604
  24.0 6.9 %copy-start = (bf16[1024,1024]{1,0:T(8,128)(2,1)S(1)}, bf16[1024,1024]{1,0:T(8,128)(2,1)}, u32[]{:S(2)}) copy-start(bf16[1024,1024]{1,0:T(8,128)(2,1)} %key_weight.1) | copy-start | bytes 6291460
  27.0 10.1 %collective-permute-start.1 = (bf16[256,512]{1,0:T(8,128)(2,1)S(1)}, bf16[256,512]{1,0:T(8,128)(2,1)S(1)}, u32[]{:S(2)}, u32[]{:S(2)}) collective-permute-start(bf16[256,512]{1,0:T(8,128)(2,1)S(1)} %get-tuple-element.40), channel_id=1, source_target_pairs={{0,64},{64,0},{128,192},{192,128},{1,65},{65,1},{129,193},{193,129... | collective-permute-start | bytes 786440 | tf_op jit(solution)/shard_map/ppermute | solution.py:306
  27.2 5.2 %collective-permute-start.4 = (bf16[2,32,1024]{2,1,0:T(8,128)(2,1)S(1)}, bf16[2,32,1024]{2,1,0:T(8,128)(2,1)S(1)}, u32[]{:S(2)}, u32[]{:S(2)}) collective-permute-start(bf16[2,32,1024]{2,1,0:T(8,128)(2,1)S(1)} %copy-done.3), channel_id=1, source_target_pairs={{0,64},{64,0},{128,192},{192,128},{1,65},{65,1},{129,193},{193,129... | collective-permute-start | bytes 393224 | tf_op jit(solution)/shard_map/ppermute | solution.py:306
  27.6 6.5 %collective-permute-start.2 = (bf16[128,512]{1,0:T(8,128)(2,1)S(1)}, bf16[128,512]{1,0:T(8,128)(2,1)S(1)}, u32[]{:S(2)}, u32[]{:S(2)}) collective-permute-start(bf16[128,512]{1,0:T(8,128)(2,1)S(1)} %get-tuple-element.41), channel_id=1, source_target_pairs={{0,128},{64,192},{128,0},{192,64},{1,129},{65,193},{129,1},{193,65... | collective-permute-start | bytes 393224 | tf_op jit(solution)/shard_map/ppermute | solution.py:306
  28.9 8.2 %collective-permute-start.3 = (bf16[128,512]{1,0:T(8,128)(2,1)S(1)}, bf16[128,512]{1,0:T(8,128)(2,1)S(1)}, u32[]{:S(2)}, u32[]{:S(2)}) collective-permute-start(bf16[128,512]{1,0:T(8,128)(2,1)S(1)} %get-tuple-element.42), channel_id=1, source_target_pairs={{0,192},{64,128},{128,64},{192,0},{1,193},{65,129},{129,65},{193,1... | collective-permute-start | bytes 393224 | tf_op jit(solution)/shard_map/ppermute | solution.py:306
  30.8 6.2 %collective-permute-start.6 = (bf16[2,32,1024]{2,1,0:T(8,128)(2,1)S(1)}, bf16[2,32,1024]{2,1,0:T(8,128)(2,1)S(1)}, u32[]{:S(2)}, u32[]{:S(2)}) collective-permute-start(bf16[2,32,1024]{2,1,0:T(8,128)(2,1)S(1)} %collective-permute-done.5.nodes2), channel_id=1, source_target_pairs={{0,64},{64,0},{128,192},{192,128},{1,65},{65,1},{129,193},{193,129... | collective-permute-start | bytes 393224 | tf_op jit(solution)/shard_map/ppermute | solution.py:306
  37.9 7.6 %collective-permute-start.10 = (bf16[144,512]{1,0:T(8,128)(2,1)S(1)}, bf16[144,512]{1,0:T(8,128)(2,1)S(1)}, u32[]{:S(2)}, u32[]{:S(2)}) collective-permute-start(bf16[144,512]{1,0:T(8,128)(2,1)S(1)} %get-tuple-element.49), channel_id=1, source_target_pairs={{0,2},{1,3},{2,4},{3,5},{4,6},{5,7},{6,0},{7,1},{8,10},{9,11},{10,... | collective-permute-start | bytes 442376 | tf_op jit(solution)/shard_map/ppermute | solution.py:311
  39.5 6.0 %collective-permute-start.11 = (bf16[144,512]{1,0:T(8,128)(2,1)S(1)}, bf16[144,512]{1,0:T(8,128)(2,1)S(1)}, u32[]{:S(2)}, u32[]{:S(2)}) collective-permute-start(bf16[144,512]{1,0:T(8,128)(2,1)S(1)} %get-tuple-element.50), channel_id=1, source_target_pairs={{0,6},{1,7},{2,0},{3,1},{4,2},{5,3},{6,4},{7,5},{8,14},{9,15},{10,... | collective-permute-start | bytes 442376 | tf_op jit(solution)/shard_map/ppermute | solution.py:311
  41.3 8.2 %collective-permute-start.7 = (bf16[144,512]{1,0:T(8,128)(2,1)S(1)}, bf16[144,512]{1,0:T(8,128)(2,1)S(1)}, u32[]{:S(2)}, u32[]{:S(2)}) collective-permute-start(bf16[144,512]{1,0:T(8,128)(2,1)S(1)} %get-tuple-element.46), channel_id=1, source_target_pairs={{0,1},{1,0},{2,3},{3,2},{4,5},{5,4},{6,7},{7,6},{8,9},{9,8},{10,11... | collective-permute-start | bytes 442376 | tf_op jit(solution)/shard_map/ppermute | solution.py:311
  43.1 6.8 %collective-permute-start.8 = (bf16[144,512]{1,0:T(8,128)(2,1)S(1)}, bf16[144,512]{1,0:T(8,128)(2,1)S(1)}, u32[]{:S(2)}, u32[]{:S(2)}) collective-permute-start(bf16[144,512]{1,0:T(8,128)(2,1)S(1)} %get-tuple-element.47), channel_id=1, source_target_pairs={{0,3},{1,2},{2,5},{3,4},{4,7},{5,6},{6,1},{7,0},{8,11},{9,10},{10,... | collective-permute-start | bytes 442376 | tf_op jit(solution)/shard_map/ppermute | solution.py:311
  43.1 6.8 %collective-permute-start.9 = (bf16[144,512]{1,0:T(8,128)(2,1)S(1)}, bf16[144,512]{1,0:T(8,128)(2,1)S(1)}, u32[]{:S(2)}, u32[]{:S(2)}) collective-permute-start(bf16[144,512]{1,0:T(8,128)(2,1)S(1)} %get-tuple-element.48), channel_id=1, source_target_pairs={{0,6},{1,7},{2,0},{3,1},{4,2},{5,3},{6,4},{7,5},{8,14},{9,15},{10,... | collective-permute-start | bytes 442376 | tf_op jit(solution)/shard_map/ppermute | solution.py:311
  45.6 6.4 %collective-permute-start.12 = (bf16[144,512]{1,0:T(8,128)(2,1)S(1)}, bf16[144,512]{1,0:T(8,128)(2,1)S(1)}, u32[]{:S(2)}, u32[]{:S(2)}) collective-permute-start(bf16[144,512]{1,0:T(8,128)(2,1)S(1)} %get-tuple-element.53), channel_id=1, source_target_pairs={{0,2},{1,3},{2,4},{3,5},{4,6},{5,7},{6,0},{7,1},{8,10},{9,11},{10,... | collective-permute-start | bytes 442376 | tf_op jit(solution)/shard_map/ppermute | solution.py:311
  45.8 6.5 %collective-permute-start.13 = (bf16[144,512]{1,0:T(8,128)(2,1)S(1)}, bf16[144,512]{1,0:T(8,128)(2,1)S(1)}, u32[]{:S(2)}, u32[]{:S(2)}) collective-permute-start(bf16[144,512]{1,0:T(8,128)(2,1)S(1)} %get-tuple-element.54), channel_id=1, source_target_pairs={{0,7},{1,6},{2,1},{3,0},{4,3},{5,2},{6,5},{7,4},{8,15},{9,14},{10,... | collective-permute-start | bytes 442376 | tf_op jit(solution)/shard_map/ppermute | solution.py:311
  53.1 16.9 %all-to-all-start = ((bf16[8,16,640]{2,1,0:T(8,128)(2,1)}), bf16[8,16,640]{2,1,0:T(8,128)(2,1)S(1)}, u32[]{:S(2)}, u32[]{:S(2)}) async-start(bf16[8,16,640]{2,1,0:T(8,128)(2,1)} %near_sum_kernel.1), calls=%async_computation | async-start | bytes 327680 | tf_op jit(solution)/shard_map/all_to_all | solution.py:378
  61.7 16.1 %collective-permute-start.17 = (bf16[64,1024]{1,0:T(8,128)(2,1)S(1)}, bf16[64,1024]{1,0:T(8,128)(2,1)S(1)}, u32[]{:S(2)}, u32[]{:S(2)}) collective-permute-start(bf16[64,1024]{1,0:T(8,128)(2,1)S(1)} %get-tuple-element.44.upper), channel_id=1, source_target_pairs={{0,1},{1,2},{2,3},{3,4},{4,5},{5,6},{6,7},{7,8},{8,9},{9,10},{10,1... | collective-permute-start | bytes 393224 | tf_op jit(solution)/shard_map/ppermute | solution.py:302
  70.1 7.7 %collective-permute-start.14 = (bf16[16,640]{1,0:T(8,128)(2,1)S(1)}, bf16[16,640]{1,0:T(8,128)(2,1)S(1)}, u32[]{:S(2)}, u32[]{:S(2)}) collective-permute-start(bf16[16,640]{1,0:T(8,128)(2,1)S(1)} %sum_kernel.1.mine), channel_id=1, source_target_pairs={{0,64},{64,0},{128,192},{192,128},{1,65},{65,1},{129,193},{193,129... | collective-permute-start | bytes 61448 | tf_op jit(solution)/shard_map/ppermute | solution.py:306
  74.6 4.2 %collective-permute-start.15 = (bf16[16,640]{1,0:T(8,128)(2,1)S(1)}, bf16[16,640]{1,0:T(8,128)(2,1)S(1)}, u32[]{:S(2)}, u32[]{:S(2)}) collective-permute-start(bf16[16,640]{1,0:T(8,128)(2,1)S(1)} %sum_kernel.1.mine), channel_id=1, source_target_pairs={{0,128},{64,192},{128,0},{192,64},{1,129},{65,193},{129,1},{193,65... | collective-permute-start | bytes 61448 | tf_op jit(solution)/shard_map/ppermute | solution.py:306
  75.8 4.7 %collective-permute-start.16 = (bf16[16,640]{1,0:T(8,128)(2,1)S(1)}, bf16[16,640]{1,0:T(8,128)(2,1)S(1)}, u32[]{:S(2)}, u32[]{:S(2)}) collective-permute-start(bf16[16,640]{1,0:T(8,128)(2,1)S(1)} %sum_kernel.1.mine), channel_id=1, source_target_pairs={{0,192},{64,128},{128,64},{192,0},{1,193},{65,129},{129,65},{193,1... | collective-permute-start | bytes 61448 | tf_op jit(solution)/shard_map/ppermute | solution.py:306
  (2 other events, 2.8 us)

commit v9 on v8

--- a/solution.py
+++ b/solution.py
@@ -24,8 +24,8 @@
 BAND = ("z", "x", "y")
 ENS = 4
 NEAR = 8
-STEPS = ((2, 0), (2, 1), (0, 1), (1, 1), (3, 0), (1, 0), (3, 1))
-PATHS = ((1, 0), (3, 0), (0, 1), (1, 1), (3, 0), (1, 0), (3, 1))
+STEPS = ((2, 0), (2, 1), (1, 1), (3, 0), (1, 0), (3, 1), (0, 1))
+PATHS = ((1, 0), (3, 0), (1, 0), (3, 0), (1, 0), (3, 1), (0, 1))
 FAR = 8
 SHARE = 16
 COLS = 2 * D // ENS
@@ -231,9 +231,9 @@
         send[FAR * SHARE :] = pair[pl.ds(start, SHARE), :]
 
 
-def relay_kernel(up, down, held6, held7, send6, send7):
-    send6[...] = (held6[...].astype(F32) + up[...].astype(F32)).astype(LOW)
-    send7[...] = (held7[...].astype(F32) + down[...].astype(F32)).astype(LOW)
+def relay_kernel(up, down, side, held5, held6, held7, send5, send6, send7):
+    for part, held, send in ((up, held5, send5), (down, held6, send6), (side, held7, send7)):
+        send[...] = (held[...].astype(F32) + part[...].astype(F32)).astype(LOW)
 
 
 def near_sum_kernel(me, first, *refs):
@@ -367,11 +367,9 @@
         me, halves, last1, last2, last3, latent, nodes1, nodes2, nodes3, shares,
         out_grad, upper,
     )
-    parts = [near_shift(value, *step) for step, value in zip(PATHS[:5], sends[:5])]
-    relayed = call(relay_kernel, [(share_block, LOW), (share_block, LOW)])(
-        parts[0], parts[1], sends[5], sends[6]
-    )
-    parts = parts[2:] + [near_shift(value, *step) for step, value in zip(PATHS[5:], relayed)]
+    parts = [near_shift(value, *step) for step, value in zip(PATHS[:4], sends[:4])]
+    relayed = call(relay_kernel, [(share_block, LOW)] * 3)(*parts[:3], *sends[4:])
+    parts = parts[3:] + [near_shift(value, *step) for step, value in zip(PATHS[4:], relayed)]
     (total,) = call(near_sum_kernel, [((FAR, SHARE, COLS + VARS_PAD), LOW)], specs=scalar)(
         me, keep, *parts
     )

time: 81.6 us -> 87.2 us (1.069)
  waiting for transfers between devices: 15.5 us -> 25.4 us
  starting transfers between devices: 40.1 us -> 35.8 us
    ppermute x7, waiting for transfers between devices: 2.78 us -> 10.8 us  [near_shift(): return lax.ppermute(value, ('x', 'y'), pairs)]
    ppermute x7, starting transfers between devices: 11.6 us -> 9.13 us  [near_shift(): return lax.ppermute(value, ('x', 'y'), pairs)]
    ppermute x9, starting transfers between devices: 15.5 us -> 13.4 us  [ens_swap(): return lax.ppermute(value, 'ens', [(e, e ^ k) for e in range(ENS)])]
    all_to_all x1, starting transfers between devices: 8.54 us -> 10.5 us  [on_device(): parts = lax.all_to_all(total, 'z', 0, 0, tiled=True)]
    all_to_all x1, waiting for transfers between devices: 5.3 us -> 7.11 us  [on_device(): parts = lax.all_to_all(total, 'z', 0, 0, tiled=True)]
    ppermute x2, starting transfers between devices: 4.5 us -> 2.71 us  [band_shift(): lax.ppermute(value, BAND, [(i, i + by) for i in range(64) if 0 <= i + by...]
  transfers between devices with their start and end apart: 19 -> 19, of which waited for: 8 -> 10; matrix products, arithmetic and copies ran while one was open for 2% -> 2% of each run, Pallas kernels for 10% -> 9%
where the time goes in v9:
time: 87.2 us; the launch traced here: 86.9 us
  starting transfers between devices  35.8 us (41%)
  waiting for transfers between devices  25.4 us (29%)
  blocking collectives  11.5 us (13%)
  Pallas kernels  10.5 us (12%)
  local copies, waits for them, and re-layouts  2.81 us (3%)
    ppermute x9, starting transfers between devices, ens_swap(): return lax.ppermute(value, 'ens', [(e, e ^ k) for e in range(ENS)])  13.4 us
    all_gather x1, blocking collectives, on_device(): shares = lax.all_gather(share, 'ens', axis=0)  11.5 us
    ppermute x7, waiting for transfers between devices, near_shift(): return lax.ppermute(value, ('x', 'y'), pairs)  10.8 us
    pallas_call x9, Pallas kernels, run(): pl.pallas_call(kernel, grid=(1,), in_specs=[places.get(i, whole(value.sha...  10.5 us
    all_to_all x1, starting transfers between devices, on_device(): parts = lax.all_to_all(total, 'z', 0, 0, tiled=True)  10.5 us
    ppermute x7, starting transfers between devices, near_shift(): return lax.ppermute(value, ('x', 'y'), pairs)  9.13 us
    ppermute x9, waiting for transfers between devices, ens_swap(): return lax.ppermute(value, 'ens', [(e, e ^ k) for e in range(ENS)])  7.47 us
    all_to_all x1, waiting for transfers between devices, on_device(): parts = lax.all_to_all(total, 'z', 0, 0, tiled=True)  7.11 us
  transfers between devices with their start and end apart: 19, of which 10 were waited for; matrix products, arithmetic and copies ran while one was open for 2% of the time, Pallas kernels for 9%

profile of v9, /device:TPU:1, one launch (start us, length us, event | category | flops | bytes accessed | tf_op | source)
XLA Modules:
  0.0 86.9 jit_solution(8839953667884043138)
XLA Ops:
  0.7 1.4 %collective-permute-start = (bf16[2,32,1024]{2,1,0:T(8,128)(2,1)}, bf16[2,32,1024]{2,1,0:T(8,128)(2,1)S(1)}, u32[]{:S(2)}, u32[]{:S(2)}) collective-permute-start(bf16[2,32,1024]{2,1,0:T(8,128)(2,1)} %nodes.1), channel_id=1, source_target_pairs={{1,0},{2,1},{3,2},{4,3},{5,4},{6,5},{7,6},{8,7},{9,8},{10,9},{11,1... | collective-permute-start | bytes 393224 | tf_op jit(solution)/shard_map/ppermute | solution.py:302
  2.1 3.8 %collective-permute-start.5 = (bf16[2,32,1024]{2,1,0:T(8,128)(2,1)}, bf16[2,32,1024]{2,1,0:T(8,128)(2,1)S(1)}, u32[]{:S(2)}, u32[]{:S(2)}) collective-permute-start(bf16[2,32,1024]{2,1,0:T(8,128)(2,1)} %nodes.1), channel_id=1, source_target_pairs={{0,128},{64,192},{128,0},{192,64},{1,129},{65,193},{129,1},{193,65... | collective-permute-start | bytes 393224 | tf_op jit(solution)/shard_map/ppermute | solution.py:306
  5.9 1.7 %fusion = (bf16[1024,512]{1,0:T(8,128)(2,1)S(1)}, bf16[1024,512]{1,0:T(8,128)(2,1)S(1)}) fusion(bf16[1024,1024]{1,0:T(8,128)(2,1)} %key_weight.1), kind=kLoop, calls=%fused_computation | loop fusion | bytes 4194304 | tf_op jit(solution)/shard_map/slice | solution.py:319
  9.4 3.1 %forward_kernel.1 = (f32[2,128,128]{2,1,0:T(8,128)S(1)}, bf16[384,256]{1,0:T(8,128)(2,1)S(1)}, bf16[2,128,1024]{2,1,0:T(8,128)(2,1)S(1)}, f32[2,128,128]{2,1,0:T...) custom-call(bf16[2,128,1024]{2,1,0:T(8,128)(2,1)S(1)} %copy-done.2, ...), custom_call_target="tpu_custom_call" | custom-call | flops 100000000 | bytes 4000000 | tf_op jit(solution)/shard_map/forward_kernel/pallas_call | solution.py:284
  12.5 11.5 %all-gather = bf16[1536,256]{1,0:T(8,128)(2,1)S(1)} all-gather(bf16[384,256]{1,0:T(8,128)(2,1)S(1)} %get-tuple-element.34), channel_id=2, replica_groups=mesh['ens'=4,'z'=8,'x'=4,'y'=2] {'ens'}, dimensions={0}, use_global_device_ids=true | all-gather | bytes 983040 | tf_op jit(solution)/shard_map/all_gather | solution.py:340
  24.1 2.9 %backward_kernel.1 = (bf16[4,128,512]{2,1,0:T(8,128)(2,1)S(1)}, bf16[256,512]{1,0:T(8,128)(2,1)S(1)}, bf16[128,512]{1,0:T(8,128)(2,1)S(1)}, bf16[128,512]{1,0:T(8,128)(2,1)S(1)}, bf16[1024,128]{1,0:T(8,128)(2,1)S(1)}) custom-call(s32[1]{0:T(128)} %bitcast.me, bf16[2,128,1024]{2,1,0:T(8,128)(2,1)S(1)} %copy-done.2, bf16[128,1024]{1,0:T(8,128)(2,1)S(1)} %pad.4.out_weight, ...), custom_call_target="tpu_custom_call" | custom-call | flops 100000000 | bytes 4000000 | tf_op jit(solution)/shard_map/backward_kernel/pallas_call | solution.py:284
  27.6 1.4 %collective-permute-start.2 = (bf16[128,512]{1,0:T(8,128)(2,1)S(1)}, bf16[128,512]{1,0:T(8,128)(2,1)S(1)}, u32[]{:S(2)}, u32[]{:S(2)}) collective-permute-start(bf16[128,512]{1,0:T(8,128)(2,1)S(1)} %get-tuple-element.42), channel_id=1, source_target_pairs={{0,128},{64,192},{128,0},{192,64},{1,129},{65,193},{129,1},{193,65... | collective-permute-start | bytes 393224 | tf_op jit(solution)/shard_map/ppermute | solution.py:306
  28.9 1.9 %collective-permute-start.3 = (bf16[128,512]{1,0:T(8,128)(2,1)S(1)}, bf16[128,512]{1,0:T(8,128)(2,1)S(1)}, u32[]{:S(2)}, u32[]{:S(2)}) collective-permute-start(bf16[128,512]{1,0:T(8,128)(2,1)S(1)} %get-tuple-element.43), channel_id=1, source_target_pairs={{0,192},{64,128},{128,64},{192,0},{1,193},{65,129},{129,65},{193,1... | collective-permute-start | bytes 393224 | tf_op jit(solution)/shard_map/ppermute | solution.py:306
  30.9 1.5 %latent_kernel.1 = (f32[64,1024]{1,0:T(8,128)S(1)}, bf16[64,1024]{1,0:T(8,128)(2,1)S(1)}) custom-call(bf16[4,128,512]{2,1,0:T(8,128)(2,1)S(1)} %get-tuple-element.40.halves, bf16[1024,1024]{1,0:T(8,128)(2,1)S(1)} %copy-done, bf16[1024,1024]{1,0:T(8,128)(2,1)S(1)} %copy-done.1), custom_call_target="tpu_custom_call" | custom-call | flops 100000000 | bytes 4000000 | tf_op jit(solution)/shard_map/latent_kernel/pallas_call | solution.py:284
  32.4 1.6 %collective-permute-done.2.last2 = bf16[128,512]{1,0:T(8,128)(2,1)S(1)} collective-permute-done((bf16[128,512]{1,0:T(8,128)(2,1)S(1)}, bf16[128,512]{1,0:T(8,128)(2,1)S(1)}, u32[]{:S(2)}, u32[]{:S(2)}) %collective-permute-start.2) | collective-permute-done | bytes 131104 | tf_op jit(solution)/shard_map/ppermute | solution.py:306
  34.0 3.1 %collective-permute-done.3.last3 = bf16[128,512]{1,0:T(8,128)(2,1)S(1)} collective-permute-done((bf16[128,512]{1,0:T(8,128)(2,1)S(1)}, bf16[128,512]{1,0:T(8,128)(2,1)S(1)}, u32[]{:S(2)}, u32[]{:S(2)}) %collective-permute-start.3) | collective-permute-done | bytes 131104 | tf_op jit(solution)/shard_map/ppermute | solution.py:306
  37.9 1.6 %collective-permute-start.10 = (bf16[144,512]{1,0:T(8,128)(2,1)S(1)}, bf16[144,512]{1,0:T(8,128)(2,1)S(1)}, u32[]{:S(2)}, u32[]{:S(2)}) collective-permute-start(bf16[144,512]{1,0:T(8,128)(2,1)S(1)} %get-tuple-element.50), channel_id=1, source_target_pairs={{0,2},{1,3},{2,4},{3,5},{4,6},{5,7},{6,0},{7,1},{8,10},{9,11},{10,... | collective-permute-start | bytes 442376 | tf_op jit(solution)/shard_map/ppermute | solution.py:311
  40.7 1.5 %collective-permute-start.9 = (bf16[144,512]{1,0:T(8,128)(2,1)S(1)}, bf16[144,512]{1,0:T(8,128)(2,1)S(1)}, u32[]{:S(2)}, u32[]{:S(2)}) collective-permute-start(bf16[144,512]{1,0:T(8,128)(2,1)S(1)} %get-tuple-element.49), channel_id=1, source_target_pairs={{0,6},{1,7},{2,0},{3,1},{4,2},{5,3},{6,4},{7,5},{8,14},{9,15},{10,... | collective-permute-start | bytes 442376 | tf_op jit(solution)/shard_map/ppermute | solution.py:311
  42.8 2.4 %collective-permute-done.10.side = bf16[144,512]{1,0:T(8,128)(2,1)S(1)} collective-permute-done((bf16[144,512]{1,0:T(8,128)(2,1)S(1)}, bf16[144,512]{1,0:T(8,128)(2,1)S(1)}, u32[]{:S(2)}, u32[]{:S(2)}) %collective-permute-start.10) | collective-permute-done | bytes 147488 | tf_op jit(solution)/shard_map/ppermute | solution.py:311
  45.1 3.2 %collective-permute-done.8.up = bf16[144,512]{1,0:T(8,128)(2,1)S(1)} collective-permute-done((bf16[144,512]{1,0:T(8,128)(2,1)S(1)}, bf16[144,512]{1,0:T(8,128)(2,1)S(1)}, u32[]{:S(2)}, u32[]{:S(2)}) %collective-permute-start.8) | collective-permute-done | bytes 147488 | tf_op jit(solution)/shard_map/ppermute | solution.py:311
  48.5 4.2 %collective-permute-start.12 = (bf16[144,512]{1,0:T(8,128)(2,1)S(1)}, bf16[144,512]{1,0:T(8,128)(2,1)S(1)}, u32[]{:S(2)}, u32[]{:S(2)}) collective-permute-start(bf16[144,512]{1,0:T(8,128)(2,1)S(1)} %get-tuple-element.55), channel_id=1, source_target_pairs={{0,7},{1,6},{2,1},{3,0},{4,3},{5,2},{6,5},{7,4},{8,15},{9,14},{10,... | collective-permute-start | bytes 442376 | tf_op jit(solution)/shard_map/ppermute | solution.py:311
  52.7 1.7 %collective-permute-done.11.refs_1_ = bf16[144,512]{1,0:T(8,128)(2,1)S(1)} collective-permute-done((bf16[144,512]{1,0:T(8,128)(2,1)S(1)}, bf16[144,512]{1,0:T(8,128)(2,1)S(1)}, u32[]{:S(2)}, u32[]{:S(2)}) %collective-permute-start.11) | collective-permute-done | bytes 147488 | tf_op jit(solution)/shard_map/ppermute | solution.py:311
  54.8 3.2 %collective-permute-done.13.refs_3_ = bf16[144,512]{1,0:T(8,128)(2,1)S(1)} collective-permute-done((bf16[144,512]{1,0:T(8,128)(2,1)S(1)}, bf16[144,512]{1,0:T(8,128)(2,1)S(1)}, u32[]{:S(2)}, u32[]{:S(2)}) %collective-permute-start.13) | collective-permute-done | bytes 147488 | tf_op jit(solution)/shard_map/ppermute | solution.py:311
  58.7 10.5 %all-to-all-start = ((bf16[8,16,640]{2,1,0:T(8,128)(2,1)}), bf16[8,16,640]{2,1,0:T(8,128)(2,1)S(1)}, u32[]{:S(2)}, u32[]{:S(2)}) async-start(bf16[8,16,640]{2,1,0:T(8,128)(2,1)} %near_sum_kernel.1), calls=%async_computation | async-start | bytes 327680 | tf_op jit(solution)/shard_map/all_to_all | solution.py:376
  70.5 7.1 %all-to-all-done.parts = bf16[8,16,640]{2,1,0:T(8,128)(2,1)S(1)} async-done(((bf16[8,16,640]{2,1,0:T(8,128)(2,1)}), bf16[8,16,640]{2,1,0:T(8,128)(2,1)S(1)}, u32[]{:S(2)}, u32[]{:S(2)}) %all-to-all-start) | async-done | bytes 163872 | tf_op jit(solution)/shard_map/all_to_all | solution.py:376
  77.7 2.4 %collective-permute-start.14 = (bf16[16,640]{1,0:T(8,128)(2,1)S(1)}, bf16[16,640]{1,0:T(8,128)(2,1)S(1)}, u32[]{:S(2)}, u32[]{:S(2)}) collective-permute-start(bf16[16,640]{1,0:T(8,128)(2,1)S(1)} %sum_kernel.1.mine), channel_id=1, source_target_pairs={{0,64},{64,0},{128,192},{192,128},{1,65},{65,1},{129,193},{193,129... | collective-permute-start | bytes 61448 | tf_op jit(solution)/shard_map/ppermute | solution.py:306
  80.1 1.3 %collective-permute-start.15 = (bf16[16,640]{1,0:T(8,128)(2,1)S(1)}, bf16[16,640]{1,0:T(8,128)(2,1)S(1)}, u32[]{:S(2)}, u32[]{:S(2)}) collective-permute-start(bf16[16,640]{1,0:T(8,128)(2,1)S(1)} %sum_kernel.1.mine), channel_id=1, source_target_pairs={{0,128},{64,192},{128,0},{192,64},{1,129},{65,193},{129,1},{193,65... | collective-permute-start | bytes 61448 | tf_op jit(solution)/shard_map/ppermute | solution.py:306
  81.4 1.9 %collective-permute-start.16 = (bf16[16,640]{1,0:T(8,128)(2,1)S(1)}, bf16[16,640]{1,0:T(8,128)(2,1)S(1)}, u32[]{:S(2)}, u32[]{:S(2)}) collective-permute-start(bf16[16,640]{1,0:T(8,128)(2,1)S(1)} %sum_kernel.1.mine), channel_id=1, source_target_pairs={{0,192},{64,128},{128,64},{192,0},{1,193},{65,129},{129,65},{193,1... | collective-permute-start | bytes 61448 | tf_op jit(solution)/shard_map/ppermute | solution.py:306
  84.2 1.9 %collective-permute-done.16.part3 = bf16[16,640]{1,0:T(8,128)(2,1)S(1)} collective-permute-done((bf16[16,640]{1,0:T(8,128)(2,1)S(1)}, bf16[16,640]{1,0:T(8,128)(2,1)S(1)}, u32[]{:S(2)}, u32[]{:S(2)}) %collective-permute-start.16) | collective-permute-done | bytes 20512 | tf_op jit(solution)/shard_map/ppermute | solution.py:306
  (40 shorter events, 9.4 us)
Async XLA Ops:
  0.6 7.1 %copy-start.3 = (bf16[2,32,1024]{2,1,0:T(8,128)(2,1)S(1)}, bf16[2,32,1024]{2,1,0:T(8,128)(2,1)}, u32[]{:S(2)}) copy-start(bf16[2,32,1024]{2,1,0:T(8,128)(2,1)} %nodes.1) | copy-start | bytes 393220
  0.6 7.0 %copy-start.6 = (bf16[100,1024]{1,0:T(8,128)(2,1)S(1)}, bf16[100,1024]{1,0:T(8,128)(2,1)}, u32[]{:S(2)}) copy-start(bf16[100,1024]{1,0:T(8,128)(2,1)} %param.11) | copy-start | bytes 614404
  0.7 7.0 %copy-start.5 = (s32[2,512]{1,0:T(2,128)S(1)}, s32[2,512]{1,0:T(2,128)}, u32[]{:S(2)}) copy-start(s32[2,512]{1,0:T(2,128)} %edges.1) | copy-start | bytes 12292
  0.7 7.6 %collective-permute-start = (bf16[2,32,1024]{2,1,0:T(8,128)(2,1)}, bf16[2,32,1024]{2,1,0:T(8,128)(2,1)S(1)}, u32[]{:S(2)}, u32[]{:S(2)}) collective-permute-start(bf16[2,32,1024]{2,1,0:T(8,128)(2,1)} %nodes.1), channel_id=1, source_target_pairs={{1,0},{2,1},{3,2},{4,3},{5,4},{6,5},{7,6},{8,7},{9,8},{10,9},{11,1... | collective-permute-start | bytes 393224 | tf_op jit(solution)/shard_map/ppermute | solution.py:302
  2.1 28.8 %collective-permute-start.5 = (bf16[2,32,1024]{2,1,0:T(8,128)(2,1)}, bf16[2,32,1024]{2,1,0:T(8,128)(2,1)S(1)}, u32[]{:S(2)}, u32[]{:S(2)}) collective-permute-start(bf16[2,32,1024]{2,1,0:T(8,128)(2,1)} %nodes.1), channel_id=1, source_target_pairs={{0,128},{64,192},{128,0},{192,64},{1,129},{65,193},{129,1},{193,65... | collective-permute-start | bytes 393224 | tf_op jit(solution)/shard_map/ppermute | solution.py:306
  9.4 14.7 %copy-start.4 = (f32[100,128]{1,0:T(8,128)S(1)}, f32[100,128]{1,0:T(8,128)}, u32[]{:S(2)}) copy-start(f32[100,128]{1,0:T(8,128)} %target.1) | copy-start | bytes 153604
  24.0 6.9 %copy-start = (bf16[1024,1024]{1,0:T(8,128)(2,1)S(1)}, bf16[1024,1024]{1,0:T(8,128)(2,1)}, u32[]{:S(2)}) copy-start(bf16[1024,1024]{1,0:T(8,128)(2,1)} %key_weight.1) | copy-start | bytes 6291460
  27.0 10.1 %collective-permute-start.1 = (bf16[256,512]{1,0:T(8,128)(2,1)S(1)}, bf16[256,512]{1,0:T(8,128)(2,1)S(1)}, u32[]{:S(2)}, u32[]{:S(2)}) collective-permute-start(bf16[256,512]{1,0:T(8,128)(2,1)S(1)} %get-tuple-element.41), channel_id=1, source_target_pairs={{0,64},{64,0},{128,192},{192,128},{1,65},{65,1},{129,193},{193,129... | collective-permute-start | bytes 786440 | tf_op jit(solution)/shard_map/ppermute | solution.py:306
  27.2 5.2 %collective-permute-start.4 = (bf16[2,32,1024]{2,1,0:T(8,128)(2,1)S(1)}, bf16[2,32,1024]{2,1,0:T(8,128)(2,1)S(1)}, u32[]{:S(2)}, u32[]{:S(2)}) collective-permute-start(bf16[2,32,1024]{2,1,0:T(8,128)(2,1)S(1)} %copy-done.3), channel_id=1, source_target_pairs={{0,64},{64,0},{128,192},{192,128},{1,65},{65,1},{129,193},{193,129... | collective-permute-start | bytes 393224 | tf_op jit(solution)/shard_map/ppermute | solution.py:306
  27.6 6.5 %collective-permute-start.2 = (bf16[128,512]{1,0:T(8,128)(2,1)S(1)}, bf16[128,512]{1,0:T(8,128)(2,1)S(1)}, u32[]{:S(2)}, u32[]{:S(2)}) collective-permute-start(bf16[128,512]{1,0:T(8,128)(2,1)S(1)} %get-tuple-element.42), channel_id=1, source_target_pairs={{0,128},{64,192},{128,0},{192,64},{1,129},{65,193},{129,1},{193,65... | collective-permute-start | bytes 393224 | tf_op jit(solution)/shard_map/ppermute | solution.py:306
  28.9 8.2 %collective-permute-start.3 = (bf16[128,512]{1,0:T(8,128)(2,1)S(1)}, bf16[128,512]{1,0:T(8,128)(2,1)S(1)}, u32[]{:S(2)}, u32[]{:S(2)}) collective-permute-start(bf16[128,512]{1,0:T(8,128)(2,1)S(1)} %get-tuple-element.43), channel_id=1, source_target_pairs={{0,192},{64,128},{128,64},{192,0},{1,193},{65,129},{129,65},{193,1... | collective-permute-start | bytes 393224 | tf_op jit(solution)/shard_map/ppermute | solution.py:306
  30.8 6.2 %collective-permute-start.6 = (bf16[2,32,1024]{2,1,0:T(8,128)(2,1)S(1)}, bf16[2,32,1024]{2,1,0:T(8,128)(2,1)S(1)}, u32[]{:S(2)}, u32[]{:S(2)}) collective-permute-start(bf16[2,32,1024]{2,1,0:T(8,128)(2,1)S(1)} %collective-permute-done.5.nodes2), channel_id=1, source_target_pairs={{0,64},{64,0},{128,192},{192,128},{1,65},{65,1},{129,193},{193,129... | collective-permute-start | bytes 393224 | tf_op jit(solution)/shard_map/ppermute | solution.py:306
  37.9 7.2 %collective-permute-start.10 = (bf16[144,512]{1,0:T(8,128)(2,1)S(1)}, bf16[144,512]{1,0:T(8,128)(2,1)S(1)}, u32[]{:S(2)}, u32[]{:S(2)}) collective-permute-start(bf16[144,512]{1,0:T(8,128)(2,1)S(1)} %get-tuple-element.50), channel_id=1, source_target_pairs={{0,2},{1,3},{2,4},{3,5},{4,6},{5,7},{6,0},{7,1},{8,10},{9,11},{10,... | collective-permute-start | bytes 442376 | tf_op jit(solution)/shard_map/ppermute | solution.py:311
  39.5 8.8 %collective-permute-start.8 = (bf16[144,512]{1,0:T(8,128)(2,1)S(1)}, bf16[144,512]{1,0:T(8,128)(2,1)S(1)}, u32[]{:S(2)}, u32[]{:S(2)}) collective-permute-start(bf16[144,512]{1,0:T(8,128)(2,1)S(1)} %get-tuple-element.48), channel_id=1, source_target_pairs={{0,2},{1,3},{2,4},{3,5},{4,6},{5,7},{6,0},{7,1},{8,10},{9,11},{10,... | collective-permute-start | bytes 442376 | tf_op jit(solution)/shard_map/ppermute | solution.py:311
  40.7 7.6 %collective-permute-start.9 = (bf16[144,512]{1,0:T(8,128)(2,1)S(1)}, bf16[144,512]{1,0:T(8,128)(2,1)S(1)}, u32[]{:S(2)}, u32[]{:S(2)}) collective-permute-start(bf16[144,512]{1,0:T(8,128)(2,1)S(1)} %get-tuple-element.49), channel_id=1, source_target_pairs={{0,6},{1,7},{2,0},{3,1},{4,2},{5,3},{6,4},{7,5},{8,14},{9,15},{10,... | collective-permute-start | bytes 442376 | tf_op jit(solution)/shard_map/ppermute | solution.py:311
  42.1 10.5 %collective-permute-start.7 = (bf16[144,512]{1,0:T(8,128)(2,1)S(1)}, bf16[144,512]{1,0:T(8,128)(2,1)S(1)}, u32[]{:S(2)}, u32[]{:S(2)}) collective-permute-start(bf16[144,512]{1,0:T(8,128)(2,1)S(1)} %get-tuple-element.47), channel_id=1, source_target_pairs={{0,6},{1,7},{2,0},{3,1},{4,2},{5,3},{6,4},{7,5},{8,14},{9,15},{10,... | collective-permute-start | bytes 442376 | tf_op jit(solution)/shard_map/ppermute | solution.py:311
  48.4 6.0 %collective-permute-start.11 = (bf16[144,512]{1,0:T(8,128)(2,1)S(1)}, bf16[144,512]{1,0:T(8,128)(2,1)S(1)}, u32[]{:S(2)}, u32[]{:S(2)}) collective-permute-start(bf16[144,512]{1,0:T(8,128)(2,1)S(1)} %get-tuple-element.54), channel_id=1, source_target_pairs={{0,2},{1,3},{2,4},{3,5},{4,6},{5,7},{6,0},{7,1},{8,10},{9,11},{10,... | collective-permute-start | bytes 442376 | tf_op jit(solution)/shard_map/ppermute | solution.py:311
  48.5 6.3 %collective-permute-start.12 = (bf16[144,512]{1,0:T(8,128)(2,1)S(1)}, bf16[144,512]{1,0:T(8,128)(2,1)S(1)}, u32[]{:S(2)}, u32[]{:S(2)}) collective-permute-start(bf16[144,512]{1,0:T(8,128)(2,1)S(1)} %get-tuple-element.55), channel_id=1, source_target_pairs={{0,7},{1,6},{2,1},{3,0},{4,3},{5,2},{6,5},{7,4},{8,15},{9,14},{10,... | collective-permute-start | bytes 442376 | tf_op jit(solution)/shard_map/ppermute | solution.py:311
  52.7 5.3 %collective-permute-start.13 = (bf16[144,512]{1,0:T(8,128)(2,1)S(1)}, bf16[144,512]{1,0:T(8,128)(2,1)S(1)}, u32[]{:S(2)}, u32[]{:S(2)}) collective-permute-start(bf16[144,512]{1,0:T(8,128)(2,1)S(1)} %get-tuple-element.56), channel_id=1, source_target_pairs={{0,1},{1,0},{2,3},{3,2},{4,5},{5,4},{6,7},{7,6},{8,9},{9,8},{10,11... | collective-permute-start | bytes 442376 | tf_op jit(solution)/shard_map/ppermute | solution.py:311
  58.7 18.9 %all-to-all-start = ((bf16[8,16,640]{2,1,0:T(8,128)(2,1)}), bf16[8,16,640]{2,1,0:T(8,128)(2,1)S(1)}, u32[]{:S(2)}, u32[]{:S(2)}) async-start(bf16[8,16,640]{2,1,0:T(8,128)(2,1)} %near_sum_kernel.1), calls=%async_computation | async-start | bytes 327680 | tf_op jit(solution)/shard_map/all_to_all | solution.py:376
  69.2 14.1 %collective-permute-start.17 = (bf16[64,1024]{1,0:T(8,128)(2,1)S(1)}, bf16[64,1024]{1,0:T(8,128)(2,1)S(1)}, u32[]{:S(2)}, u32[]{:S(2)}) collective-permute-start(bf16[64,1024]{1,0:T(8,128)(2,1)S(1)} %get-tuple-element.45.upper), channel_id=1, source_target_pairs={{0,1},{1,2},{2,3},{3,4},{4,5},{5,6},{6,7},{7,8},{8,9},{9,10},{10,1... | collective-permute-start | bytes 393224 | tf_op jit(solution)/shard_map/ppermute | solution.py:302
  77.7 5.6 %collective-permute-start.14 = (bf16[16,640]{1,0:T(8,128)(2,1)S(1)}, bf16[16,640]{1,0:T(8,128)(2,1)S(1)}, u32[]{:S(2)}, u32[]{:S(2)}) collective-permute-start(bf16[16,640]{1,0:T(8,128)(2,1)S(1)} %sum_kernel.1.mine), channel_id=1, source_target_pairs={{0,64},{64,0},{128,192},{192,128},{1,65},{65,1},{129,193},{193,129... | collective-permute-start | bytes 61448 | tf_op jit(solution)/shard_map/ppermute | solution.py:306
  80.1 4.2 %collective-permute-start.15 = (bf16[16,640]{1,0:T(8,128)(2,1)S(1)}, bf16[16,640]{1,0:T(8,128)(2,1)S(1)}, u32[]{:S(2)}, u32[]{:S(2)}) collective-permute-start(bf16[16,640]{1,0:T(8,128)(2,1)S(1)} %sum_kernel.1.mine), channel_id=1, source_target_pairs={{0,128},{64,192},{128,0},{192,64},{1,129},{65,193},{129,1},{193,65... | collective-permute-start | bytes 61448 | tf_op jit(solution)/shard_map/ppermute | solution.py:306
  81.4 4.7 %collective-permute-start.16 = (bf16[16,640]{1,0:T(8,128)(2,1)S(1)}, bf16[16,640]{1,0:T(8,128)(2,1)S(1)}, u32[]{:S(2)}, u32[]{:S(2)}) collective-permute-start(bf16[16,640]{1,0:T(8,128)(2,1)S(1)} %sum_kernel.1.mine), channel_id=1, source_target_pairs={{0,192},{64,128},{128,64},{192,0},{1,193},{65,129},{129,65},{193,1... | collective-permute-start | bytes 61448 | tf_op jit(solution)/shard_map/ppermute | solution.py:306
  (2 other events, 2.8 us)

commit v10 on v8

--- a/solution.py
+++ b/solution.py
@@ -24,8 +24,8 @@
 BAND = ("z", "x", "y")
 ENS = 4
 NEAR = 8
-STEPS = ((2, 0), (2, 1), (0, 1), (1, 1), (3, 0), (1, 0), (3, 1))
-PATHS = ((1, 0), (3, 0), (0, 1), (1, 1), (3, 0), (1, 0), (3, 1))
+STEPS = ((2, 0), (2, 1), (0, 1), (1, 1), (3, 0), (3, 1), (1, 0))
+PATHS = ((1, 0), (3, 0), (0, 1), (1, 1), (3, 0), (3, 1), (1, 0))
 FAR = 8
 SHARE = 16
 COLS = 2 * D // ENS
@@ -369,7 +369,7 @@
     )
     parts = [near_shift(value, *step) for step, value in zip(PATHS[:5], sends[:5])]
     relayed = call(relay_kernel, [(share_block, LOW), (share_block, LOW)])(
-        parts[0], parts[1], sends[5], sends[6]
+        parts[1], parts[0], sends[5], sends[6]
     )
     parts = parts[2:] + [near_shift(value, *step) for step, value in zip(PATHS[5:], relayed)]
     (total,) = call(near_sum_kernel, [((FAR, SHARE, COLS + VARS_PAD), LOW)], specs=scalar)(

time: 81.6 us -> 83.5 us (1.023)
  waiting for transfers between devices: 15.5 us -> 20.8 us
  starting transfers between devices: 40.1 us -> 36.7 us
    ppermute x7, waiting for transfers between devices: 2.78 us -> 6.04 us  [near_shift(): return lax.ppermute(value, ('x', 'y'), pairs)]
    all_to_all x1, waiting for transfers between devices: 5.3 us -> 6.57 us  [on_device(): parts = lax.all_to_all(total, 'z', 0, 0, tiled=True)]
    ppermute x2, starting transfers between devices: 4.5 us -> 3.24 us  [band_shift(): lax.ppermute(value, BAND, [(i, i + by) for i in range(64) if 0 <= i + by...]
    ppermute x7, starting transfers between devices: 11.6 us -> 10.5 us  [near_shift(): return lax.ppermute(value, ('x', 'y'), pairs)]
    ppermute x9, starting transfers between devices: 15.5 us -> 14.6 us  [ens_swap(): return lax.ppermute(value, 'ens', [(e, e ^ k) for e in range(ENS)])]
  transfers between devices with their start and end apart: 19 -> 19, of which waited for: 8 -> 9; matrix products, arithmetic and copies ran while one was open for 2% -> 2% of each run, Pallas kernels for 10% -> 10%
where the time goes in v10:
time: 83.5 us; the launch traced here: 83.2 us
  starting transfers between devices  36.7 us (44%)
  waiting for transfers between devices  20.8 us (25%)
  blocking collectives  11.5 us (14%)
  Pallas kernels  10.5 us (13%)
  local copies, waits for them, and re-layouts  2.81 us (3%)
    ppermute x9, starting transfers between devices, ens_swap(): return lax.ppermute(value, 'ens', [(e, e ^ k) for e in range(ENS)])  14.6 us
    all_gather x1, blocking collectives, on_device(): shares = lax.all_gather(share, 'ens', axis=0)  11.5 us
    pallas_call x9, Pallas kernels, run(): pl.pallas_call(kernel, grid=(1,), in_specs=[places.get(i, whole(value.sha...  10.5 us
    ppermute x7, starting transfers between devices, near_shift(): return lax.ppermute(value, ('x', 'y'), pairs)  10.5 us
    all_to_all x1, starting transfers between devices, on_device(): parts = lax.all_to_all(total, 'z', 0, 0, tiled=True)  8.3 us
    ppermute x9, waiting for transfers between devices, ens_swap(): return lax.ppermute(value, 'ens', [(e, e ^ k) for e in range(ENS)])  8.15 us
    all_to_all x1, waiting for transfers between devices, on_device(): parts = lax.all_to_all(total, 'z', 0, 0, tiled=True)  6.57 us
    ppermute x7, waiting for transfers between devices, near_shift(): return lax.ppermute(value, ('x', 'y'), pairs)  6.04 us
  transfers between devices with their start and end apart: 19, of which 9 were waited for; matrix products, arithmetic and copies ran while one was open for 2% of the time, Pallas kernels for 10%

profile of v10, /device:TPU:1, one launch (start us, length us, event | category | flops | bytes accessed | tf_op | source)
XLA Modules:
  0.0 83.2 jit_solution(13896208834607895811)
XLA Ops:
  0.7 1.4 %collective-permute-start = (bf16[2,32,1024]{2,1,0:T(8,128)(2,1)}, bf16[2,32,1024]{2,1,0:T(8,128)(2,1)S(1)}, u32[]{:S(2)}, u32[]{:S(2)}) collective-permute-start(bf16[2,32,1024]{2,1,0:T(8,128)(2,1)} %nodes.1), channel_id=1, source_target_pairs={{1,0},{2,1},{3,2},{4,3},{5,4},{6,5},{7,6},{8,7},{9,8},{10,9},{11,1... | collective-permute-start | bytes 393224 | tf_op jit(solution)/shard_map/ppermute | solution.py:302
  2.1 3.8 %collective-permute-start.5 = (bf16[2,32,1024]{2,1,0:T(8,128)(2,1)}, bf16[2,32,1024]{2,1,0:T(8,128)(2,1)S(1)}, u32[]{:S(2)}, u32[]{:S(2)}) collective-permute-start(bf16[2,32,1024]{2,1,0:T(8,128)(2,1)} %nodes.1), channel_id=1, source_target_pairs={{0,128},{64,192},{128,0},{192,64},{1,129},{65,193},{129,1},{193,65... | collective-permute-start | bytes 393224 | tf_op jit(solution)/shard_map/ppermute | solution.py:306
  5.9 1.7 %fusion = (bf16[1024,512]{1,0:T(8,128)(2,1)S(1)}, bf16[1024,512]{1,0:T(8,128)(2,1)S(1)}) fusion(bf16[1024,1024]{1,0:T(8,128)(2,1)} %key_weight.1), kind=kLoop, calls=%fused_computation | loop fusion | bytes 4194304 | tf_op jit(solution)/shard_map/slice | solution.py:319
  9.4 3.1 %forward_kernel.1 = (f32[2,128,128]{2,1,0:T(8,128)S(1)}, bf16[384,256]{1,0:T(8,128)(2,1)S(1)}, bf16[2,128,1024]{2,1,0:T(8,128)(2,1)S(1)}, f32[2,128,128]{2,1,0:T...) custom-call(bf16[2,128,1024]{2,1,0:T(8,128)(2,1)S(1)} %copy-done.2, ...), custom_call_target="tpu_custom_call" | custom-call | flops 100000000 | bytes 4000000 | tf_op jit(solution)/shard_map/forward_kernel/pallas_call | solution.py:284
  12.5 11.5 %all-gather = bf16[1536,256]{1,0:T(8,128)(2,1)S(1)} all-gather(bf16[384,256]{1,0:T(8,128)(2,1)S(1)} %get-tuple-element.33), channel_id=2, replica_groups=mesh['ens'=4,'z'=8,'x'=4,'y'=2] {'ens'}, dimensions={0}, use_global_device_ids=true | all-gather | bytes 983040 | tf_op jit(solution)/shard_map/all_gather | solution.py:340
  24.1 2.9 %backward_kernel.1 = (bf16[4,128,512]{2,1,0:T(8,128)(2,1)S(1)}, bf16[256,512]{1,0:T(8,128)(2,1)S(1)}, bf16[128,512]{1,0:T(8,128)(2,1)S(1)}, bf16[128,512]{1,0:T(8,128)(2,1)S(1)}, bf16[1024,128]{1,0:T(8,128)(2,1)S(1)}) custom-call(s32[1]{0:T(128)} %bitcast.me, bf16[2,128,1024]{2,1,0:T(8,128)(2,1)S(1)} %copy-done.2, bf16[128,1024]{1,0:T(8,128)(2,1)S(1)} %pad.4.out_weight, ...), custom_call_target="tpu_custom_call" | custom-call | flops 100000000 | bytes 4000000 | tf_op jit(solution)/shard_map/backward_kernel/pallas_call | solution.py:284
  27.6 1.4 %collective-permute-start.2 = (bf16[128,512]{1,0:T(8,128)(2,1)S(1)}, bf16[128,512]{1,0:T(8,128)(2,1)S(1)}, u32[]{:S(2)}, u32[]{:S(2)}) collective-permute-start(bf16[128,512]{1,0:T(8,128)(2,1)S(1)} %get-tuple-element.41), channel_id=1, source_target_pairs={{0,128},{64,192},{128,0},{192,64},{1,129},{65,193},{129,1},{193,65... | collective-permute-start | bytes 393224 | tf_op jit(solution)/shard_map/ppermute | solution.py:306
  28.9 1.9 %collective-permute-start.3 = (bf16[128,512]{1,0:T(8,128)(2,1)S(1)}, bf16[128,512]{1,0:T(8,128)(2,1)S(1)}, u32[]{:S(2)}, u32[]{:S(2)}) collective-permute-start(bf16[128,512]{1,0:T(8,128)(2,1)S(1)} %get-tuple-element.42), channel_id=1, source_target_pairs={{0,192},{64,128},{128,64},{192,0},{1,193},{65,129},{129,65},{193,1... | collective-permute-start | bytes 393224 | tf_op jit(solution)/shard_map/ppermute | solution.py:306
  30.9 1.5 %latent_kernel.1 = (f32[64,1024]{1,0:T(8,128)S(1)}, bf16[64,1024]{1,0:T(8,128)(2,1)S(1)}) custom-call(bf16[4,128,512]{2,1,0:T(8,128)(2,1)S(1)} %get-tuple-element.39.halves, bf16[1024,1024]{1,0:T(8,128)(2,1)S(1)} %copy-done, bf16[1024,1024]{1,0:T(8,128)(2,1)S(1)} %copy-done.1), custom_call_target="tpu_custom_call" | custom-call | flops 100000000 | bytes 4000000 | tf_op jit(solution)/shard_map/latent_kernel/pallas_call | solution.py:284
  32.4 1.6 %collective-permute-done.2.last2 = bf16[128,512]{1,0:T(8,128)(2,1)S(1)} collective-permute-done((bf16[128,512]{1,0:T(8,128)(2,1)S(1)}, bf16[128,512]{1,0:T(8,128)(2,1)S(1)}, u32[]{:S(2)}, u32[]{:S(2)}) %collective-permute-start.2) | collective-permute-done | bytes 131104 | tf_op jit(solution)/shard_map/ppermute | solution.py:306
  34.0 3.1 %collective-permute-done.3.last3 = bf16[128,512]{1,0:T(8,128)(2,1)S(1)} collective-permute-done((bf16[128,512]{1,0:T(8,128)(2,1)S(1)}, bf16[128,512]{1,0:T(8,128)(2,1)S(1)}, u32[]{:S(2)}, u32[]{:S(2)}) %collective-permute-start.3) | collective-permute-done | bytes 131104 | tf_op jit(solution)/shard_map/ppermute | solution.py:306
  37.9 3.2 %collective-permute-start.10 = (bf16[144,512]{1,0:T(8,128)(2,1)S(1)}, bf16[144,512]{1,0:T(8,128)(2,1)S(1)}, u32[]{:S(2)}, u32[]{:S(2)}) collective-permute-start(bf16[144,512]{1,0:T(8,128)(2,1)S(1)} %get-tuple-element.49), channel_id=1, source_target_pairs={{0,6},{1,7},{2,0},{3,1},{4,2},{5,3},{6,4},{7,5},{8,14},{9,15},{10,... | collective-permute-start | bytes 442376 | tf_op jit(solution)/shard_map/ppermute | solution.py:311
  41.1 1.8 %collective-permute-start.7 = (bf16[144,512]{1,0:T(8,128)(2,1)S(1)}, bf16[144,512]{1,0:T(8,128)(2,1)S(1)}, u32[]{:S(2)}, u32[]{:S(2)}) collective-permute-start(bf16[144,512]{1,0:T(8,128)(2,1)S(1)} %get-tuple-element.46), channel_id=1, source_target_pairs={{0,1},{1,0},{2,3},{3,2},{4,5},{5,4},{6,7},{7,6},{8,9},{9,8},{10,11... | collective-permute-start | bytes 442376 | tf_op jit(solution)/shard_map/ppermute | solution.py:311
  42.8 2.7 %collective-permute-start.9 = (bf16[144,512]{1,0:T(8,128)(2,1)S(1)}, bf16[144,512]{1,0:T(8,128)(2,1)S(1)}, u32[]{:S(2)}, u32[]{:S(2)}) collective-permute-start(bf16[144,512]{1,0:T(8,128)(2,1)S(1)} %get-tuple-element.48), channel_id=1, source_target_pairs={{0,6},{1,7},{2,0},{3,1},{4,2},{5,3},{6,4},{7,5},{8,14},{9,15},{10,... | collective-permute-start | bytes 442376 | tf_op jit(solution)/shard_map/ppermute | solution.py:311
  45.5 1.8 %collective-permute-done.11.down = bf16[144,512]{1,0:T(8,128)(2,1)S(1)} collective-permute-done((bf16[144,512]{1,0:T(8,128)(2,1)S(1)}, bf16[144,512]{1,0:T(8,128)(2,1)S(1)}, u32[]{:S(2)}, u32[]{:S(2)}) %collective-permute-start.11) | collective-permute-done | bytes 147488 | tf_op jit(solution)/shard_map/ppermute | solution.py:311
  47.4 1.8 %collective-permute-start.12 = (bf16[144,512]{1,0:T(8,128)(2,1)S(1)}, bf16[144,512]{1,0:T(8,128)(2,1)S(1)}, u32[]{:S(2)}, u32[]{:S(2)}) collective-permute-start(bf16[144,512]{1,0:T(8,128)(2,1)S(1)} %get-tuple-element.53), channel_id=1, source_target_pairs={{0,7},{1,6},{2,1},{3,0},{4,3},{5,2},{6,5},{7,4},{8,15},{9,14},{10,... | collective-permute-start | bytes 442376 | tf_op jit(solution)/shard_map/ppermute | solution.py:311
  50.4 2.0 %collective-permute-done.8.refs_1_ = bf16[144,512]{1,0:T(8,128)(2,1)S(1)} collective-permute-done((bf16[144,512]{1,0:T(8,128)(2,1)S(1)}, bf16[144,512]{1,0:T(8,128)(2,1)S(1)}, u32[]{:S(2)}, u32[]{:S(2)}) %collective-permute-start.8) | collective-permute-done | bytes 147488 | tf_op jit(solution)/shard_map/ppermute | solution.py:311
  52.4 1.7 %collective-permute-done.12.refs_3_ = bf16[144,512]{1,0:T(8,128)(2,1)S(1)} collective-permute-done((bf16[144,512]{1,0:T(8,128)(2,1)S(1)}, bf16[144,512]{1,0:T(8,128)(2,1)S(1)}, u32[]{:S(2)}, u32[]{:S(2)}) %collective-permute-start.12) | collective-permute-done | bytes 147488 | tf_op jit(solution)/shard_map/ppermute | solution.py:311
  55.4 8.3 %all-to-all-start = ((bf16[8,16,640]{2,1,0:T(8,128)(2,1)}), bf16[8,16,640]{2,1,0:T(8,128)(2,1)S(1)}, u32[]{:S(2)}, u32[]{:S(2)}) async-start(bf16[8,16,640]{2,1,0:T(8,128)(2,1)} %near_sum_kernel.1), calls=%async_computation | async-start | bytes 327680 | tf_op jit(solution)/shard_map/all_to_all | solution.py:378
  63.7 1.8 %collective-permute-start.17 = (bf16[64,1024]{1,0:T(8,128)(2,1)S(1)}, bf16[64,1024]{1,0:T(8,128)(2,1)S(1)}, u32[]{:S(2)}, u32[]{:S(2)}) collective-permute-start(bf16[64,1024]{1,0:T(8,128)(2,1)S(1)} %get-tuple-element.44.upper), channel_id=1, source_target_pairs={{0,1},{1,2},{2,3},{3,4},{4,5},{5,6},{6,7},{7,8},{8,9},{9,10},{10,1... | collective-permute-start | bytes 393224 | tf_op jit(solution)/shard_map/ppermute | solution.py:302
  65.5 6.6 %all-to-all-done.parts = bf16[8,16,640]{2,1,0:T(8,128)(2,1)S(1)} async-done(((bf16[8,16,640]{2,1,0:T(8,128)(2,1)}), bf16[8,16,640]{2,1,0:T(8,128)(2,1)S(1)}, u32[]{:S(2)}, u32[]{:S(2)}) %all-to-all-start) | async-done | bytes 163872 | tf_op jit(solution)/shard_map/all_to_all | solution.py:378
  72.1 3.6 %collective-permute-start.14 = (bf16[16,640]{1,0:T(8,128)(2,1)S(1)}, bf16[16,640]{1,0:T(8,128)(2,1)S(1)}, u32[]{:S(2)}, u32[]{:S(2)}) collective-permute-start(bf16[16,640]{1,0:T(8,128)(2,1)S(1)} %sum_kernel.1.mine), channel_id=1, source_target_pairs={{0,64},{64,0},{128,192},{192,128},{1,65},{65,1},{129,193},{193,129... | collective-permute-start | bytes 61448 | tf_op jit(solution)/shard_map/ppermute | solution.py:306
  75.7 2.0 %collective-permute-start.15 = (bf16[16,640]{1,0:T(8,128)(2,1)S(1)}, bf16[16,640]{1,0:T(8,128)(2,1)S(1)}, u32[]{:S(2)}, u32[]{:S(2)}) collective-permute-start(bf16[16,640]{1,0:T(8,128)(2,1)S(1)} %sum_kernel.1.mine), channel_id=1, source_target_pairs={{0,128},{64,192},{128,0},{192,64},{1,129},{65,193},{129,1},{193,65... | collective-permute-start | bytes 61448 | tf_op jit(solution)/shard_map/ppermute | solution.py:306
  79.8 2.6 %collective-permute-done.16.part3 = bf16[16,640]{1,0:T(8,128)(2,1)S(1)} collective-permute-done((bf16[16,640]{1,0:T(8,128)(2,1)S(1)}, bf16[16,640]{1,0:T(8,128)(2,1)S(1)}, u32[]{:S(2)}, u32[]{:S(2)}) %collective-permute-start.16) | collective-permute-done | bytes 20512 | tf_op jit(solution)/shard_map/ppermute | solution.py:306
  (40 shorter events, 8.7 us)
Async XLA Ops:
  0.6 7.1 %copy-start.3 = (bf16[2,32,1024]{2,1,0:T(8,128)(2,1)S(1)}, bf16[2,32,1024]{2,1,0:T(8,128)(2,1)}, u32[]{:S(2)}) copy-start(bf16[2,32,1024]{2,1,0:T(8,128)(2,1)} %nodes.1) | copy-start | bytes 393220
  0.6 7.0 %copy-start.6 = (bf16[100,1024]{1,0:T(8,128)(2,1)S(1)}, bf16[100,1024]{1,0:T(8,128)(2,1)}, u32[]{:S(2)}) copy-start(bf16[100,1024]{1,0:T(8,128)(2,1)} %param.11) | copy-start | bytes 614404
  0.7 7.0 %copy-start.5 = (s32[2,512]{1,0:T(2,128)S(1)}, s32[2,512]{1,0:T(2,128)}, u32[]{:S(2)}) copy-start(s32[2,512]{1,0:T(2,128)} %edges.1) | copy-start | bytes 12292
  0.7 7.6 %collective-permute-start = (bf16[2,32,1024]{2,1,0:T(8,128)(2,1)}, bf16[2,32,1024]{2,1,0:T(8,128)(2,1)S(1)}, u32[]{:S(2)}, u32[]{:S(2)}) collective-permute-start(bf16[2,32,1024]{2,1,0:T(8,128)(2,1)} %nodes.1), channel_id=1, source_target_pairs={{1,0},{2,1},{3,2},{4,3},{5,4},{6,5},{7,6},{8,7},{9,8},{10,9},{11,1... | collective-permute-start | bytes 393224 | tf_op jit(solution)/shard_map/ppermute | solution.py:302
  2.1 28.8 %collective-permute-start.5 = (bf16[2,32,1024]{2,1,0:T(8,128)(2,1)}, bf16[2,32,1024]{2,1,0:T(8,128)(2,1)S(1)}, u32[]{:S(2)}, u32[]{:S(2)}) collective-permute-start(bf16[2,32,1024]{2,1,0:T(8,128)(2,1)} %nodes.1), channel_id=1, source_target_pairs={{0,128},{64,192},{128,0},{192,64},{1,129},{65,193},{129,1},{193,65... | collective-permute-start | bytes 393224 | tf_op jit(solution)/shard_map/ppermute | solution.py:306
  9.4 14.7 %copy-start.4 = (f32[100,128]{1,0:T(8,128)S(1)}, f32[100,128]{1,0:T(8,128)}, u32[]{:S(2)}) copy-start(f32[100,128]{1,0:T(8,128)} %target.1) | copy-start | bytes 153604
  24.0 6.9 %copy-start = (bf16[1024,1024]{1,0:T(8,128)(2,1)S(1)}, bf16[1024,1024]{1,0:T(8,128)(2,1)}, u32[]{:S(2)}) copy-start(bf16[1024,1024]{1,0:T(8,128)(2,1)} %key_weight.1) | copy-start | bytes 6291460
  27.0 10.1 %collective-permute-start.1 = (bf16[256,512]{1,0:T(8,128)(2,1)S(1)}, bf16[256,512]{1,0:T(8,128)(2,1)S(1)}, u32[]{:S(2)}, u32[]{:S(2)}) collective-permute-start(bf16[256,512]{1,0:T(8,128)(2,1)S(1)} %get-tuple-element.40), channel_id=1, source_target_pairs={{0,64},{64,0},{128,192},{192,128},{1,65},{65,1},{129,193},{193,129... | collective-permute-start | bytes 786440 | tf_op jit(solution)/shard_map/ppermute | solution.py:306
  27.2 5.2 %collective-permute-start.4 = (bf16[2,32,1024]{2,1,0:T(8,128)(2,1)S(1)}, bf16[2,32,1024]{2,1,0:T(8,128)(2,1)S(1)}, u32[]{:S(2)}, u32[]{:S(2)}) collective-permute-start(bf16[2,32,1024]{2,1,0:T(8,128)(2,1)S(1)} %copy-done.3), channel_id=1, source_target_pairs={{0,64},{64,0},{128,192},{192,128},{1,65},{65,1},{129,193},{193,129... | collective-permute-start | bytes 393224 | tf_op jit(solution)/shard_map/ppermute | solution.py:306
  27.6 6.5 %collective-permute-start.2 = (bf16[128,512]{1,0:T(8,128)(2,1)S(1)}, bf16[128,512]{1,0:T(8,128)(2,1)S(1)}, u32[]{:S(2)}, u32[]{:S(2)}) collective-permute-start(bf16[128,512]{1,0:T(8,128)(2,1)S(1)} %get-tuple-element.41), channel_id=1, source_target_pairs={{0,128},{64,192},{128,0},{192,64},{1,129},{65,193},{129,1},{193,65... | collective-permute-start | bytes 393224 | tf_op jit(solution)/shard_map/ppermute | solution.py:306
  28.9 8.2 %collective-permute-start.3 = (bf16[128,512]{1,0:T(8,128)(2,1)S(1)}, bf16[128,512]{1,0:T(8,128)(2,1)S(1)}, u32[]{:S(2)}, u32[]{:S(2)}) collective-permute-start(bf16[128,512]{1,0:T(8,128)(2,1)S(1)} %get-tuple-element.42), channel_id=1, source_target_pairs={{0,192},{64,128},{128,64},{192,0},{1,193},{65,129},{129,65},{193,1... | collective-permute-start | bytes 393224 | tf_op jit(solution)/shard_map/ppermute | solution.py:306
  30.8 6.2 %collective-permute-start.6 = (bf16[2,32,1024]{2,1,0:T(8,128)(2,1)S(1)}, bf16[2,32,1024]{2,1,0:T(8,128)(2,1)S(1)}, u32[]{:S(2)}, u32[]{:S(2)}) collective-permute-start(bf16[2,32,1024]{2,1,0:T(8,128)(2,1)S(1)} %collective-permute-done.5.nodes2), channel_id=1, source_target_pairs={{0,64},{64,0},{128,192},{192,128},{1,65},{65,1},{129,193},{193,129... | collective-permute-start | bytes 393224 | tf_op jit(solution)/shard_map/ppermute | solution.py:306
  37.9 7.6 %collective-permute-start.10 = (bf16[144,512]{1,0:T(8,128)(2,1)S(1)}, bf16[144,512]{1,0:T(8,128)(2,1)S(1)}, u32[]{:S(2)}, u32[]{:S(2)}) collective-permute-start(bf16[144,512]{1,0:T(8,128)(2,1)S(1)} %get-tuple-element.49), channel_id=1, source_target_pairs={{0,6},{1,7},{2,0},{3,1},{4,2},{5,3},{6,4},{7,5},{8,14},{9,15},{10,... | collective-permute-start | bytes 442376 | tf_op jit(solution)/shard_map/ppermute | solution.py:311
  41.1 6.3 %collective-permute-start.11 = (bf16[144,512]{1,0:T(8,128)(2,1)S(1)}, bf16[144,512]{1,0:T(8,128)(2,1)S(1)}, u32[]{:S(2)}, u32[]{:S(2)}) collective-permute-start(bf16[144,512]{1,0:T(8,128)(2,1)S(1)} %get-tuple-element.50), channel_id=1, source_target_pairs={{0,2},{1,3},{2,4},{3,5},{4,6},{5,7},{6,0},{7,1},{8,10},{9,11},{10,... | collective-permute-start | bytes 442376 | tf_op jit(solution)/shard_map/ppermute | solution.py:311
  41.1 9.3 %collective-permute-start.7 = (bf16[144,512]{1,0:T(8,128)(2,1)S(1)}, bf16[144,512]{1,0:T(8,128)(2,1)S(1)}, u32[]{:S(2)}, u32[]{:S(2)}) collective-permute-start(bf16[144,512]{1,0:T(8,128)(2,1)S(1)} %get-tuple-element.46), channel_id=1, source_target_pairs={{0,1},{1,0},{2,3},{3,2},{4,5},{5,4},{6,7},{7,6},{8,9},{9,8},{10,11... | collective-permute-start | bytes 442376 | tf_op jit(solution)/shard_map/ppermute | solution.py:311
  42.8 9.6 %collective-permute-start.8 = (bf16[144,512]{1,0:T(8,128)(2,1)S(1)}, bf16[144,512]{1,0:T(8,128)(2,1)S(1)}, u32[]{:S(2)}, u32[]{:S(2)}) collective-permute-start(bf16[144,512]{1,0:T(8,128)(2,1)S(1)} %get-tuple-element.47), channel_id=1, source_target_pairs={{0,3},{1,2},{2,5},{3,4},{4,7},{5,6},{6,1},{7,0},{8,11},{9,10},{10,... | collective-permute-start | bytes 442376 | tf_op jit(solution)/shard_map/ppermute | solution.py:311
  42.8 9.6 %collective-permute-start.9 = (bf16[144,512]{1,0:T(8,128)(2,1)S(1)}, bf16[144,512]{1,0:T(8,128)(2,1)S(1)}, u32[]{:S(2)}, u32[]{:S(2)}) collective-permute-start(bf16[144,512]{1,0:T(8,128)(2,1)S(1)} %get-tuple-element.48), channel_id=1, source_target_pairs={{0,6},{1,7},{2,0},{3,1},{4,2},{5,3},{6,4},{7,5},{8,14},{9,15},{10,... | collective-permute-start | bytes 442376 | tf_op jit(solution)/shard_map/ppermute | solution.py:311
  47.4 6.6 %collective-permute-start.12 = (bf16[144,512]{1,0:T(8,128)(2,1)S(1)}, bf16[144,512]{1,0:T(8,128)(2,1)S(1)}, u32[]{:S(2)}, u32[]{:S(2)}) collective-permute-start(bf16[144,512]{1,0:T(8,128)(2,1)S(1)} %get-tuple-element.53), channel_id=1, source_target_pairs={{0,7},{1,6},{2,1},{3,0},{4,3},{5,2},{6,5},{7,4},{8,15},{9,14},{10,... | collective-permute-start | bytes 442376 | tf_op jit(solution)/shard_map/ppermute | solution.py:311
  49.2 5.3 %collective-permute-start.13 = (bf16[144,512]{1,0:T(8,128)(2,1)S(1)}, bf16[144,512]{1,0:T(8,128)(2,1)S(1)}, u32[]{:S(2)}, u32[]{:S(2)}) collective-permute-start(bf16[144,512]{1,0:T(8,128)(2,1)S(1)} %get-tuple-element.54), channel_id=1, source_target_pairs={{0,2},{1,3},{2,4},{3,5},{4,6},{5,7},{6,0},{7,1},{8,10},{9,11},{10,... | collective-permute-start | bytes 442376 | tf_op jit(solution)/shard_map/ppermute | solution.py:311
  55.4 16.7 %all-to-all-start = ((bf16[8,16,640]{2,1,0:T(8,128)(2,1)}), bf16[8,16,640]{2,1,0:T(8,128)(2,1)S(1)}, u32[]{:S(2)}, u32[]{:S(2)}) async-start(bf16[8,16,640]{2,1,0:T(8,128)(2,1)} %near_sum_kernel.1), calls=%async_computation | async-start | bytes 327680 | tf_op jit(solution)/shard_map/all_to_all | solution.py:378
  63.7 15.3 %collective-permute-start.17 = (bf16[64,1024]{1,0:T(8,128)(2,1)S(1)}, bf16[64,1024]{1,0:T(8,128)(2,1)S(1)}, u32[]{:S(2)}, u32[]{:S(2)}) collective-permute-start(bf16[64,1024]{1,0:T(8,128)(2,1)S(1)} %get-tuple-element.44.upper), channel_id=1, source_target_pairs={{0,1},{1,2},{2,3},{3,4},{4,5},{5,6},{6,7},{7,8},{8,9},{9,10},{10,1... | collective-permute-start | bytes 393224 | tf_op jit(solution)/shard_map/ppermute | solution.py:302
  72.1 6.9 %collective-permute-start.14 = (bf16[16,640]{1,0:T(8,128)(2,1)S(1)}, bf16[16,640]{1,0:T(8,128)(2,1)S(1)}, u32[]{:S(2)}, u32[]{:S(2)}) collective-permute-start(bf16[16,640]{1,0:T(8,128)(2,1)S(1)} %sum_kernel.1.mine), channel_id=1, source_target_pairs={{0,64},{64,0},{128,192},{192,128},{1,65},{65,1},{129,193},{193,129... | collective-permute-start | bytes 61448 | tf_op jit(solution)/shard_map/ppermute | solution.py:306
  75.7 4.2 %collective-permute-start.15 = (bf16[16,640]{1,0:T(8,128)(2,1)S(1)}, bf16[16,640]{1,0:T(8,128)(2,1)S(1)}, u32[]{:S(2)}, u32[]{:S(2)}) collective-permute-start(bf16[16,640]{1,0:T(8,128)(2,1)S(1)} %sum_kernel.1.mine), channel_id=1, source_target_pairs={{0,128},{64,192},{128,0},{192,64},{1,129},{65,193},{129,1},{193,65... | collective-permute-start | bytes 61448 | tf_op jit(solution)/shard_map/ppermute | solution.py:306
  77.7 4.7 %collective-permute-start.16 = (bf16[16,640]{1,0:T(8,128)(2,1)S(1)}, bf16[16,640]{1,0:T(8,128)(2,1)S(1)}, u32[]{:S(2)}, u32[]{:S(2)}) collective-permute-start(bf16[16,640]{1,0:T(8,128)(2,1)S(1)} %sum_kernel.1.mine), channel_id=1, source_target_pairs={{0,192},{64,128},{128,64},{192,0},{1,193},{65,129},{129,65},{193,1... | collective-permute-start | bytes 61448 | tf_op jit(solution)/shard_map/ppermute | solution.py:306
  (2 other events, 2.8 us)
